TPU v7x, 128 devices: a whole 4x4x4 slice. The times are simulated.
128 devices in a mesh: gx: 16 (over x, z_lo, core), gy: 8 (over y, z_hi).
Axes of the slice: x: 4, y: 4, z: 4 (z_hi: 2, z_lo: 2; z = z_hi * 2 + z_lo), core: 2. Of those that a mesh axis runs over, the one named last changes fastest.
Arguments:
- tokens: bfloat16 [512, 8192], P('gy', 'gx'), may hold values from -6 to 6
- out_grad: bfloat16 [512, 8192], P('gy', 'gx'), may hold values from -6 to 6
- gate_weight: bfloat16 [8192, 28672], P('gx', 'gy'), may hold values from -0.0625 to 0.0625
- up_weight: bfloat16 [8192, 28672], P('gx', 'gy'), may hold values from -0.0625 to 0.0625
- down_weight: bfloat16 [28672, 8192], P('gy', 'gx'), may hold values from -0.03125 to 0.03125
Outputs:
- grad_tokens: bfloat16 [512, 8192], P('gy', 'gx')
- grad_gate_weight: bfloat16 [8192, 28672], P('gx', 'gy')
- grad_up_weight: bfloat16 [8192, 28672], P('gx', 'gy')
- grad_down_weight: bfloat16 [28672, 8192], P('gy', 'gx')
All inputs are finite; a program needn't handle non-finite values.
Results may differ from a plain program's by a relative error of at most 0.005.
Values may be sent and summed in bfloat16 or wider, within the bound.
No kernel may reach another device: no remote copies, remote signals or barrier semaphores. Data moves between devices by JAX's collectives and lax.ppermute only.
A program may use at most 192 MiB of HBM per device.

v0:
```python
import jax
import jax.numpy as jnp
from jax import lax
from jax.sharding import PartitionSpec as P


def local_grads(gate_sum, upper_sum, back_sum):
    sigmoid_gate = jax.nn.sigmoid(gate_sum)
    silu_gate = gate_sum * sigmoid_gate
    hidden = (silu_gate * upper_sum).astype(jnp.bfloat16)
    grad_gate = (
        back_sum * upper_sum * sigmoid_gate * (1.0 + gate_sum * (1.0 - sigmoid_gate))
    ).astype(jnp.bfloat16)
    grad_upper = (back_sum * silu_gate).astype(jnp.bfloat16)
    return (hidden, grad_gate, grad_upper)


def shards(tokens, out_grad, gate_weight, up_weight, down_weight):
    contract_last = (((1,), (1,)), ((), ()))
    tokens_by_columns = (((0,), (1,)), ((), ()))
    tok_all, grad_all = (
        lax.all_gather(tokens, "gy", axis=0, tiled=True),
        lax.all_gather(out_grad, "gy", axis=0, tiled=True),
    )
    hidden_width = gate_weight.shape[1]
    gate_term = jnp.dot(tok_all, gate_weight, preferred_element_type=jnp.float32)
    upper_term = jnp.dot(tok_all, up_weight, preferred_element_type=jnp.float32)
    back_term = lax.dot_general(
        grad_all, down_weight, contract_last, preferred_element_type=jnp.float32
    )
    summed = lax.psum_scatter(
        jnp.concatenate([gate_term, upper_term, back_term], axis=1),
        "gx",
        scatter_dimension=0,
        tiled=True,
    )
    hidden, grad_gate, grad_upper = local_grads(
        summed[:, :hidden_width],
        summed[:, hidden_width : 2 * hidden_width],
        summed[:, 2 * hidden_width :],
    )
    packed = jnp.concatenate([hidden, grad_gate, grad_upper], axis=1)
    gathered = lax.all_gather(packed, "gx", axis=0, tiled=True)
    hidden_t = gathered[:, :hidden_width].T
    gate_t = gathered[:, hidden_width : 2 * hidden_width].T
    upper_t = gathered[:, 2 * hidden_width :].T
    grad_down_weight = jnp.dot(hidden_t, grad_all, preferred_element_type=jnp.float32).astype(
        jnp.bfloat16
    )
    grad_gate_weight = lax.dot_general(
        tok_all, gate_t, tokens_by_columns, preferred_element_type=jnp.float32
    ).astype(jnp.bfloat16)
    grad_up_weight = lax.dot_general(
        tok_all, upper_t, tokens_by_columns, preferred_element_type=jnp.float32
    ).astype(jnp.bfloat16)
    result = lax.dot_general(
        gate_t, gate_weight, (((0,), (1,)), ((), ())), preferred_element_type=jnp.float32
    )
    grad_tokens = lax.psum_scatter(
        result
        + lax.dot_general(
            upper_t, up_weight, (((0,), (1,)), ((), ())), preferred_element_type=jnp.float32
        ),
        "gy",
        scatter_dimension=0,
        tiled=True,
    )
    return (grad_tokens.astype(jnp.bfloat16), grad_gate_weight, grad_up_weight, grad_down_weight)


def solution(mesh):
    return jax.shard_map(
        shards,
        mesh=mesh,
        in_specs=(P("gy", "gx"), P("gy", "gx"), P("gx", "gy"), P("gx", "gy"), P("gy", "gx")),
        out_specs=(P("gy", "gx"), P("gx", "gy"), P("gx", "gy"), P("gy", "gx")),
        check_vma=False,
    )
```

profile of v0, /device:TPU:1, one launch (start us, length us, event | category | flops | bytes accessed | tf_op | source)
XLA Modules:
  0.0 488.0 jit_solution(13058267235208708872)
XLA Ops:
  7.2 0.0 reduce-scatter.3.cloned.1.call-start
  7.2 31.2 %all_gather.9 = bf16[512,512]{1,0:T(8,128)(2,1)S(1)} all-gather(bf16[64,512]{1,0:T(8,128)(2,1)} %param.5), channel_id=1, replica_groups=mesh['gx'=16,'gy'=8] {'gy'}, dimensions={0}, use_global_device_ids=true | all-gather | bytes 589824 | tf_op jit(solution)/shard_map/all_gather | solution.py:22
  38.4 29.9 %all_gather.10 = bf16[512,512]{1,0:T(8,128)(2,1)S(1)} all-gather(bf16[64,512]{1,0:T(8,128)(2,1)} %param.6), channel_id=1, replica_groups=mesh['gx'=16,'gy'=8] {'gy'}, dimensions={0}, use_global_device_ids=true | all-gather | bytes 589824 | tf_op jit(solution)/shard_map/all_gather | solution.py:23
  68.3 0.0 copy-start.1
  68.3 4.3 fusion.14
  72.6 0.0 copy-done.1
  72.6 0.0 copy-start
  72.6 2.1 fusion.13
  74.7 0.0 copy-done
  74.7 2.1 fusion.15
  76.8 7.7 %pad_maximum_fusion = f32[512,10752]{1,0:T(8,128)} fusion(f32[512,3584]{1,0:T(8,128)S(1)} %fusion.15, f32[512,3584]{1,0:T(8,128)S(1)} %fusion.14, f32[512,3584]{1,0:T(8,128)S(1)} %fusion.13), kind=kLoop, calls=%fused_computation | loop fusion | flops 11010048 | bytes 44040192 | tf_op jit(solution)/shard_map/concatenate | solution.py:32
  84.5 0.0 reduce-scatter.3.cloned.1.call-update
  84.5 0.0 all-gather.2.cloned.1.call-start
  84.6 246.4 %reduce-scatter.3.cloned.1.call-done = f32[32,10752]{1,0:T(8,128)} async-done(((f32[512,10752]{1,0:T(8,128)}), f32[32,10752]{1,0:T(8,128)}) %reduce-scatter.3.cloned.1.call-update) | async-done | bytes 1376272 | tf_op jit(solution)/shard_map/reduce_scatter | solution.py:31
  331.0 1.5 multiply_convert_fusion.2
  332.6 0.9 pad_maximum_fusion.1
  333.4 0.0 all-gather.2.cloned.1.call-update
  333.5 0.2 reduce-scatter.5.cloned.1.call-start
  333.7 64.9 %all-gather.2.cloned.1.call-done = bf16[512,10752]{1,0:T(8,128)(2,1)} async-done(((bf16[32,10752]{1,0:T(8,128)(2,1)}), bf16[512,10752]{1,0:T(8,128)(2,1)}) %all-gather.2.cloned.1.call-update) | async-done | bytes 11010064 | tf_op jit(solution)/shard_map/all_gather | solution.py:43
  398.6 0.0 copy-start.2
  398.6 5.4 %fusion.4 = f32[512,512]{1,0:T(8,128)S(1)} fusion(bf16[512,3584]{1,0:T(8,128)(2,1)} %param.8, bf16[512,10752]{1,0:T(8,128)(2,1)} %all-gather.2.cloned.1.call-done), kind=kOutput, calls=%fused_computation.8 | convolution fusion | flops 1879048192 | bytes 8388608 | tf_op jit(solution)/shard_map/dot_general | solution.py:61
  404.0 0.0 copy-done.2
  404.0 5.1 %fusion.9 = f32[512,512]{1,0:T(8,128)} fusion(f32[512,512]{1,0:T(8,128)S(1)} %fusion.4, bf16[512,3584]{1,0:T(8,128)(2,1)S(1)} %copy-done.2, bf16[512,10752]{1,0:T(8,128)(2,1)} %all-gather.2.cloned.1.call-done), kind=kOutput, calls=%fused_computation.13 | convolution fusion | flops 1879310336 | bytes 9437184 | tf_op jit(solution)/shard_map/dot_general | solution.py:56
  409.1 0.0 reduce-scatter.5.cloned.1.call-update
  409.1 6.0 %fusion.1 = bf16[512,3584]{0,1:T(8,128)(2,1)} fusion(bf16[512,512]{1,0:T(8,128)(2,1)S(1)} %all_gather.9, bf16[512,10752]{1,0:T(8,128)(2,1)} %all-gather.2.cloned.1.call-done), kind=kOutput, calls=%fused_computation.5 | convolution fusion | flops 1880883200 | bytes 7864320 | tf_op jit(solution)/shard_map/dot_general | solution.py:53
  415.1 5.9 %copy.10 = bf16[512,3584]{1,0:T(8,128)(2,1)} copy(bf16[512,3584]{0,1:T(8,128)(2,1)} %fusion.1) | data formatting | bytes 7340032
  421.0 6.0 %fusion = bf16[512,3584]{0,1:T(8,128)(2,1)} fusion(bf16[512,512]{1,0:T(8,128)(2,1)S(1)} %all_gather.9, bf16[512,10752]{1,0:T(8,128)(2,1)} %all-gather.2.cloned.1.call-done), kind=kOutput, calls=%fused_computation.4 | convolution fusion | flops 1880883200 | bytes 7864320 | tf_op jit(solution)/shard_map/dot_general | solution.py:50
  427.0 6.0 %copy.9 = bf16[512,3584]{1,0:T(8,128)(2,1)} copy(bf16[512,3584]{0,1:T(8,128)(2,1)} %fusion) | data formatting | bytes 7340032
  432.9 6.0 %convolution_convert_fusion = bf16[3584,512]{1,0:T(8,128)(2,1)} fusion(bf16[512,512]{1,0:T(8,128)(2,1)S(1)} %all_gather.10, bf16[512,10752]{1,0:T(8,128)(2,1)} %all-gather.2.cloned.1.call-done), kind=kOutput, calls=%fused_computation.1 | convolution fusion | flops 1880883200 | bytes 7864320 | tf_op jit(solution)/shard_map/dot_general | solution.py:47
  438.9 41.0 %reduce-scatter.5.cloned.1.call-done = f32[64,512]{1,0:T(8,128)} async-done(((f32[512,512]{1,0:T(8,128)}), f32[64,512]{1,0:T(8,128)}) %reduce-scatter.5.cloned.1.call-update) | async-done | bytes 131088 | tf_op jit(solution)/shard_map/reduce_scatter | solution.py:59
  479.9 1.5 convert_element_type.30
Async XLA Ops:
  7.2 323.8 %reduce-scatter.3.cloned.1.call-start = ((), (), s32[]{:S(2)}) async-start(), calls=%async_computation.2 | async-start | bytes 23396352 | tf_op jit(solution)/shard_map/reduce_scatter | solution.py:31
  68.3 4.3 copy-start.1
  72.6 2.1 copy-start
  84.5 314.1 %all-gather.2.cloned.1.call-start = ((), (), s32[]{:S(2)}) async-start(), calls=%async_computation.3 | async-start | bytes 11698176 | tf_op jit(solution)/shard_map/all_gather | solution.py:43
  333.5 146.4 %reduce-scatter.5.cloned.1.call-start = ((), (), s32[]{:S(2)}) async-start(), calls=%async_computation.4 | async-start | bytes 1179648 | tf_op jit(solution)/shard_map/reduce_scatter | solution.py:59
  398.6 5.4 %copy-start.2 = (bf16[512,3584]{1,0:T(8,128)(2,1)S(1)}, bf16[512,3584]{1,0:T(8,128)(2,1)}, u32[]{:S(2)}) copy-start(bf16[512,3584]{1,0:T(8,128)(2,1)} %param.7) | copy-start | bytes 11010052
Sparse Core Ops, SparseCore 0:
  84.6 246.3 reduce-scatter.2
  333.6 64.9 all-gather.1
  409.2 70.6 reduce-scatter.4
where the time goes:
time: 490 us; the launch traced here: 488 us
  waiting for transfers between devices  352 us (72%)
  blocking collectives  61.1 us (12%)
  matrix products  36.9 us (8%)
  between operations  13.8 us (3%)
  local copies, waits for them, and re-layouts  11.9 us (2%)
  other arithmetic  11.7 us (2%)
    reduce_scatter x1, waiting for transfers between devices, shards(): lax.psum_scatter(jnp.concatenate([gate_term, upper_term, back_term], axis...  246 us
    all_gather x1, waiting for transfers between devices, shards(): gathered = lax.all_gather(packed, 'gx', axis=0, tiled=True)  64.9 us
    reduce_scatter x1, waiting for transfers between devices, shards(): lax.psum_scatter(result + lax.dot_general(upper_t, up_weight, (((0,), (1,...  41 us
    all_gather x1, blocking collectives, shards(): lax.all_gather(tokens, 'gy', axis=0, tiled=True)  31.2 us
    all_gather x1, blocking collectives, shards(): lax.all_gather(out_grad, 'gy', axis=0, tiled=True)  29.9 us
    unnamed x8, local copies, waits for them, and re-layouts  11.9 us
  transfers between devices with their start and end apart: 3, of which 3 were waited for; matrix products, arithmetic and copies ran while one was open for 6% of the time, Pallas kernels for 0%

commit v1 on v0

v1 whole, which is shorter than its diff:
```python
import functools

import jax
import jax.numpy as jnp
from jax import lax
from jax.experimental import pallas as pl
from jax.experimental.pallas import tpu as pltpu
from jax.sharding import PartitionSpec as P

BF, F32 = jnp.bfloat16, jnp.float32
BLK = 64
TILE = 256
T_TILES, S_TILES = 3, 4
HALF = (T_TILES + S_TILES) * TILE
VMEM = 40 * 1024 * 1024


def gx_perm(move):
    pairs = []
    for i in range(16):
        x, z, c = move(i // 4, (i // 2) % 2, i % 2)
        pairs.append((i, (x % 4) * 4 + (z % 2) * 2 + c % 2))
    return pairs


CORE = gx_perm(lambda x, z, c: (x, z, c + 1))
XP = gx_perm(lambda x, z, c: (x + 1, z, c))
XM = gx_perm(lambda x, z, c: (x - 1, z, c))
ZS = gx_perm(lambda x, z, c: (x, z + 1, c))


def gy_perm(dy, dh):
    return [(i, ((i // 2 + dy) % 4) * 2 + (i + dh) % 2) for i in range(8)]


def send(a, pairs, axis="gx"):
    return lax.ppermute(a, axis, pairs)


def dot(a, b, ca, cb):
    return lax.dot_general(a, b, (((ca,), (cb,)), ((), ())), preferred_element_type=F32)


def place(pos, r):
    return (((r // 2 - pos[0]) & 3) * 2 + ((r & 1) ^ pos[1])) * BLK


def whole(shape):
    return pl.BlockSpec(shape, lambda i, pos: (0,) * len(shape))


def params():
    return pltpu.CompilerParams(vmem_limit_bytes=VMEM, dimension_semantics=("arbitrary",))


def order_kernel(pos, *refs):
    pieces, (tg, tok_t) = refs[:8], refs[8:]
    for r in range(8):
        tg[pl.ds(pl.multiple_of(place(pos, r), BLK), BLK), :] = pieces[r][...]
    tok_t[...] = tg[:, :512].T


def order(pos, pieces):
    return pl.pallas_call(
        order_kernel,
        grid_spec=pltpu.PrefetchScalarGridSpec(
            num_scalar_prefetch=1,
            grid=(1,),
            in_specs=[whole((BLK, 1024))] * 8,
            out_specs=[whole((512, 1024)), whole((512, 512))],
        ),
        out_shape=[jax.ShapeDtypeStruct((512, 1024), BF), jax.ShapeDtypeStruct((512, 512), BF)],
        compiler_params=params(),
        cost_estimate=pl.CostEstimate(flops=0, bytes_accessed=4 << 20, transcendentals=0),
    )(pos, *pieces)


def sums_kernel(split, pos, tg, tg_sib, gw, uw, dw, gw_sib, uw_sib, dw_sib, *outs):
    for a in range(3):
        if a < 2:
            own, sib = ((gw, gw_sib), (uw, uw_sib))[a]
            total = dot(tg[:, :512], own[...], 1, 0) + dot(tg_sib[:, :512], sib[...], 1, 0)
        else:
            total = dot(tg[:, 512:], dw[...], 1, 1) + dot(tg_sib[:, 512:], dw_sib[...], 1, 1)
        split(a, lambda j: total[j * BLK : (j + 1) * BLK], *outs)


def split_s(a, block, m1p, m1m, m2p, m2m, k1, k3, k0, k01):
    m1p[a] = block(4).astype(BF)
    m1m[a] = block(5).astype(BF)
    m2p[a] = block(3).astype(BF)
    m2m[a] = block(6).astype(BF)
    k1[a] = block(2)
    k3[a] = block(7)
    k0[a] = block(0)
    k01[a] = block(1)


def split_t(a, block, mza, mzb, keep):
    mza[a] = block(5).astype(BF)
    for i, jx in enumerate((1, 3, 0)):
        mzb[i, a] = block(jx * 2 + 1).astype(BF)
    for jx in range(4):
        keep[jx, a] = block(jx * 2)


def sums(pos, tg, tg_sib, weights, weights_sib, split, first, tiles, lead):
    cols, rows = (512, TILE), (TILE, 512)
    own = lambda i, pos: (0, pos[2] * (HALF // TILE) + first + i)
    sib = lambda i, pos: (0, first + i)
    flip = lambda f: (lambda i, pos: f(i, pos)[::-1])
    width = tiles * TILE

    def out_spec(n):
        zeros = (0,) * (n + 2)
        return lambda i, pos: (*zeros, i)

    flops = 2 * 3 * 512 * 1024 * width
    return pl.pallas_call(
        functools.partial(sums_kernel, split),
        grid_spec=pltpu.PrefetchScalarGridSpec(
            num_scalar_prefetch=1,
            grid=(tiles,),
            in_specs=[
                whole((512, 1024)),
                whole((512, 1024)),
                pl.BlockSpec(cols, own),
                pl.BlockSpec(cols, own),
                pl.BlockSpec(rows, flip(own)),
                pl.BlockSpec(cols, sib),
                pl.BlockSpec(cols, sib),
                pl.BlockSpec(rows, flip(sib)),
            ],
            out_specs=[pl.BlockSpec((*n, 3, BLK, TILE), out_spec(len(n))) for n, _ in lead],
        ),
        out_shape=[jax.ShapeDtypeStruct((*n, 3, BLK, width), t) for n, t in lead],
        compiler_params=params(),
        cost_estimate=pl.CostEstimate(flops=flops, bytes_accessed=16 << 20, transcendentals=0),
    )(pos, tg, tg_sib, *weights, *weights_sib)


def input_grads_kernel(first, last, pos, grads, tok_t, gw, uw, *refs):
    if first:
        ggw, guw, *out, acc = refs
    else:
        before, _, _, ggw, guw, *out, acc = refs
    step = pl.program_id(0)
    gate, upper = grads[0], grads[1]
    ggw[...] = dot(tok_t[...], gate, 1, 0).astype(BF)
    guw[...] = dot(tok_t[...], upper, 1, 0).astype(BF)
    term = dot(gate, gw[...], 1, 1) + dot(upper, uw[...], 1, 1)

    @pl.when(step == 0)
    def _():
        acc[...] = term if first else before[...] + term

    @pl.when(step > 0)
    def _():
        acc[...] += term

    @pl.when(step == pl.num_programs(0) - 1)
    def _():
        if not last:
            out[0][...] = acc[...]
        else:
            for r in range(8):
                out[r][...] = acc[pl.ds(pl.multiple_of(place(pos, r), BLK), BLK), :]


def input_grads(pos, grads, tok_t, gw, uw, at, carry, last):
    tiles = grads.shape[-1] // TILE
    first = carry is None
    tile = lambda i, pos: (0, at(pos) + i)
    weight = pl.BlockSpec((512, TILE), tile)
    square = whole((512, 512))
    in_specs = [pl.BlockSpec((2, 512, TILE), lambda i, pos: (0, 0, i)), square, weight, weight]
    if not first:
        in_specs += [square, pl.BlockSpec(memory_space=pl.ANY), pl.BlockSpec(memory_space=pl.ANY)]
    full = jax.ShapeDtypeStruct((512, 2 * HALF), BF)
    if last:
        tail_specs, tail = [whole((BLK, 512))] * 8, [jax.ShapeDtypeStruct((BLK, 512), F32)] * 8
    else:
        tail_specs, tail = [square], [jax.ShapeDtypeStruct((512, 512), F32)]
    outs = pl.pallas_call(
        functools.partial(input_grads_kernel, first, last),
        grid_spec=pltpu.PrefetchScalarGridSpec(
            num_scalar_prefetch=1,
            grid=(tiles,),
            in_specs=in_specs,
            out_specs=[weight, weight, *tail_specs],
            scratch_shapes=[pltpu.VMEM((512, 512), F32)],
        ),
        out_shape=[full, full, *tail],
        input_output_aliases={} if first else {6: 0, 7: 1},
        compiler_params=params(),
        cost_estimate=pl.CostEstimate(
            flops=8 * 512 * 512 * tiles * TILE, bytes_accessed=tiles << 20, transcendentals=0
        ),
    )(pos, grads, tok_t, gw, uw, *([] if first else [carry[2], carry[0], carry[1]]))
    return outs


def down_grad_kernel(pos, hidden, tg, *refs):
    refs[-1][...] = dot(hidden[...], tg[:, 512:], 0, 0).astype(BF)


def down_grad(pos, hidden, tg, at, carry):
    tiles = hidden.shape[-1] // TILE
    rest = [] if carry is None else [carry]
    return pl.pallas_call(
        down_grad_kernel,
        grid_spec=pltpu.PrefetchScalarGridSpec(
            num_scalar_prefetch=1,
            grid=(tiles,),
            in_specs=[pl.BlockSpec((512, TILE), lambda i, pos: (0, i)), whole((512, 1024))]
            + [pl.BlockSpec(memory_space=pl.ANY)] * len(rest),
            out_specs=pl.BlockSpec((TILE, 512), lambda i, pos: (at(pos) + i, 0)),
        ),
        out_shape=jax.ShapeDtypeStruct((2 * HALF, 512), BF),
        input_output_aliases={3: 0} if rest else {},
        compiler_params=params(),
        cost_estimate=pl.CostEstimate(
            flops=2 * 512 * 512 * tiles * TILE, bytes_accessed=3 << 20, transcendentals=0
        ),
    )(pos, hidden, tg, *rest)


def wide(a):
    return a.astype(F32)


def scatter_s(m1p, m1m, m2p, m2m, k1, k3, k0, k01):
    r1p, r1m = send(m1p, XP), send(m1m, XM)
    r2p, r2m = send(m2p, XP), send(m2m, XM)
    r3p = send((k1 + wide(r1p)).astype(BF), XP)
    r3m = send((k3 + wide(r1m)).astype(BF), XM)
    rz = send((k01 + wide(r2p) + wide(r3m)).astype(BF), ZS)
    return k0 + wide(r2m) + wide(r3p) + wide(rz)


def scatter_t(mza, mzb, keep):
    rza, rzb = send(mza, ZS), send(mzb, ZS)
    d2 = (keep[2] + wide(rza)).astype(BF)
    r1p, r1m = send(d2[:, :32], XP), send(d2[:, 32:], XM)
    d1, d3, d0 = keep[1] + wide(rzb[0]), keep[3] + wide(rzb[1]), keep[0] + wide(rzb[2])
    r2p, r2m = send(d1[:, 32:].astype(BF), XP), send(d3[:, :32].astype(BF), XM)
    r3p = send((d1[:, :32] + wide(r1p)).astype(BF), XP)
    r3m = send((d3[:, 32:] + wide(r1m)).astype(BF), XM)
    low = d0[:, :32] + wide(r3p) + wide(r2m)
    high = d0[:, 32:] + wide(r2p) + wide(r3m)
    return jnp.concatenate([low, high], axis=1)


def gather_s(e):
    ez = send(e, ZS)
    g30, g10 = send(e, XP), send(e, XM)
    g31, g11 = send(ez, XP), send(ez, XM)
    g20, g21 = send(g30, XP), send(g11, XM)
    return jnp.concatenate([e, ez, g10, g11, g20, g21, g30, g31], axis=-2)


def gather_t(e):
    h3, h1 = send(e, XP), send(e, XM)
    z0 = send(e, ZS)
    lo, hi = send(h3[..., :32, :], XP), send(h1[..., 32:, :], XM)
    z1, z3 = send(h1, ZS), send(h3, ZS)
    zlo, zhi = send(lo, ZS), send(hi, ZS)
    return jnp.concatenate([e, z0, h1, z1, lo, hi, zlo, zhi, h3, z3], axis=-2)


def local_grads(gate_sum, upper_sum, back_sum):
    sigmoid_gate = jax.nn.sigmoid(gate_sum)
    silu_gate = gate_sum * sigmoid_gate
    hidden = (silu_gate * upper_sum).astype(BF)
    grad_gate = (
        back_sum * upper_sum * sigmoid_gate * (1.0 + gate_sum * (1.0 - sigmoid_gate))
    ).astype(BF)
    grad_upper = (back_sum * silu_gate).astype(BF)
    return hidden, jnp.stack([grad_gate, grad_upper])


def shards(tokens, out_grad, gate_weight, up_weight, down_weight):
    gx = lax.axis_index("gx")
    core = gx % 2
    pos = jnp.stack([gx // 4, (gx // 2) % 2, core]).astype(jnp.int32)
    far = (1 - core) * HALF

    both = jnp.concatenate([tokens, out_grad], axis=1)
    pieces = [both] + [send(both, gy_perm(-(r // 2), r % 2), "gy") for r in range(1, 8)]
    weights = (gate_weight, up_weight, down_weight)
    weights_sib = [
        send(lax.dynamic_slice_in_dim(w, far, HALF, axis), CORE)
        for w, axis in zip(weights, (1, 1, 0))
    ]
    tg, tok_t = order(pos, pieces)
    tg_sib = send(tg, CORE)

    lead_t = [((), BF), ((3,), BF), ((4,), F32)]
    lead_s = [((), BF)] * 4 + [((), F32)] * 4
    parts_t = sums(pos, tg, tg_sib, weights, weights_sib, split_t, 0, T_TILES, lead_t)
    parts_s = sums(pos, tg, tg_sib, weights, weights_sib, split_s, T_TILES, S_TILES, lead_s)
    sum_s = scatter_s(*parts_s)
    sum_t = scatter_t(*parts_t)
    hidden_s, grads_s = local_grads(sum_s[0], sum_s[1], sum_s[2])
    hidden_t, grads_t = local_grads(sum_t[0], sum_t[1], sum_t[2])

    full_s, full_t = gather_s(grads_s), gather_t(grads_t)
    sib_s, sib_t = send(full_s, CORE), send(full_t, CORE)
    hid_s, hid_t = gather_s(hidden_s), gather_t(hidden_t)
    hid_s_sib, hid_t_sib = send(hid_s, CORE), send(hid_t, CORE)

    per_half = HALF // TILE
    own_t = lambda pos: pos[2] * per_half
    own_s = lambda pos: pos[2] * per_half + T_TILES
    far_t = lambda pos: (1 - pos[2]) * per_half
    far_s = lambda pos: (1 - pos[2]) * per_half + T_TILES
    carry = None
    for grads, at in ((full_t, own_t), (full_s, own_s), (sib_t, far_t), (sib_s, far_s)):
        last = grads is sib_s
        carry = input_grads(pos, grads, tok_t, gate_weight, up_weight, at, carry, last)
    ggw, guw, *terms = carry
    total = terms[0]
    for r in range(1, 8):
        total = total + send(terms[r], gy_perm(r // 2, r % 2), "gy")

    gdw = None
    for hidden, at in ((hid_t, own_t), (hid_s, own_s), (hid_t_sib, far_t), (hid_s_sib, far_s)):
        gdw = down_grad(pos, hidden, tg, at, gdw)
    return total.astype(BF), ggw, guw, gdw


def solution(mesh):
    return jax.shard_map(
        shards,
        mesh=mesh,
        in_specs=(P("gy", "gx"), P("gy", "gx"), P("gx", "gy"), P("gx", "gy"), P("gy", "gx")),
        out_specs=(P("gy", "gx"), P("gx", "gy"), P("gx", "gy"), P("gy", "gx")),
        check_vma=False,
    )
```

time: 490 us -> 256 us (0.52)
  waiting for transfers between devices: 352 us -> 95.5 us
  starting transfers between devices: 0.3 us -> 106 us
  blocking collectives: 61.1 us -> 0 us
  Pallas kernels: 0 us -> 43.4 us
  matrix products: 36.9 us -> 0 us
  between operations: 13.8 us -> 1.23 us
  other arithmetic: 11.7 us -> 2.2 us
  local copies, waits for them, and re-layouts: 11.9 us -> 6.18 us
    reduce_scatter x2 -> x0, waiting for transfers between devices: 287 us -> none  [the longest x1 246 us: shards(): lax.psum_scatter(jnp.concatenate([gate_term, upper_term, back_term], axis...]
    ppermute x0 -> x69, starting transfers between devices: none -> 106 us  [send(): return lax.ppermute(a, axis, pairs)]
    ppermute x0 -> x69, waiting for transfers between devices: none -> 95.5 us  [send(): return lax.ppermute(a, axis, pairs)]
    all_gather x1 -> x0, waiting for transfers between devices: 64.9 us -> none  [shards(): gathered = lax.all_gather(packed, 'gx', axis=0, tiled=True)]
    all_gather x2 -> x0, blocking collectives: 61.1 us -> none  [the longest x1 31.2 us: shards(): lax.all_gather(tokens, 'gy', axis=0, tiled=True)]
    pallas_call x0 -> x11, Pallas kernels: none -> 43.4 us  [the longest x4 19.1 us: input_grads(): pl.pallas_call(functools.partial(input_grads_kernel, first, last), grid_s...]
    dot_general x8 -> x0, matrix products: 36.9 us -> none  [the longest x1 6 us: shards(): jnp.dot(hidden_t, grad_all, preferred_element_type=jnp.float32)]
    unnamed x8 -> x41, local copies, waits for them, and re-layouts: 11.9 us -> 0.34 us
  transfers between devices with their start and end apart: 3 -> 69, of which waited for: 3 -> 27; matrix products, arithmetic and copies ran while one was open for 6% -> 2% of each run, Pallas kernels for 0% -> 15%
where the time goes in v1:
time: 256 us; the launch traced here: 255 us
  starting transfers between devices  106 us (41%)
  waiting for transfers between devices  95.5 us (37%)
  Pallas kernels  43.4 us (17%)
  local copies, waits for them, and re-layouts  6.18 us (2%)
    ppermute x69, starting transfers between devices, send(): return lax.ppermute(a, axis, pairs)  106 us
    ppermute x69, waiting for transfers between devices, send(): return lax.ppermute(a, axis, pairs)  95.5 us
    pallas_call x4, Pallas kernels, input_grads(): pl.pallas_call(functools.partial(input_grads_kernel, first, last), grid_s...  19.1 us
    pallas_call x2, Pallas kernels, sums(): pl.pallas_call(functools.partial(sums_kernel, split), grid_spec=pltpu.Pre...  12 us
    pallas_call x4, Pallas kernels, down_grad(): pl.pallas_call(down_grad_kernel, grid_spec=pltpu.PrefetchScalarGridSpec(n...  11.6 us
    dynamic_slice x3, local copies, waits for them, and re-layouts, shards(): lax.dynamic_slice_in_dim(w, far, HALF, axis)  5.7 us
  transfers between devices with their start and end apart: 69, of which 27 were waited for; matrix products, arithmetic and copies ran while one was open for 2% of the time, Pallas kernels for 15%

profile of v1, /device:TPU:1, one launch (start us, length us, event | category | flops | bytes accessed | tf_op | source)
XLA Modules:
  0.0 254.7 jit_solution(7228070112222172)
XLA Ops:
  0.7 3.0 %constant_dynamic-slice_fusion = bf16[1792,512]{1,0:T(8,128)(2,1)} fusion(bf16[3584,512]{1,0:T(8,128)(2,1)} %dw.3, s32[]{:T(128)S(6)} %select_n.27), kind=kLoop, calls=%fused_computation.87 | loop fusion | bytes 3670020 | tf_op jit(solution)/shard_map/dynamic_slice | solution.py:292
  9.2 3.8 %collective-permute-start = (bf16[64,1024]{1,0:T(8,128)(2,1)S(1)}, bf16[64,1024]{1,0:T(8,128)(2,1)S(1)}, u32[]{:S(2)}, u32[]{:S(2)}) collective-permute-start(bf16[64,1024]{1,0:T(8,128)(2,1)S(1)} %constant_dynamic-update-slice_fusion.refs_0_), channel_id=1, source_target_pairs={{0,1},{1,0},{2,3},{3,2},{4,5},{5,4},{6,7},{7,6},{8,9},{9,8},{10,11... | collective-permute-start | bytes 393224 | tf_op jit(solution)/shard_map/ppermute | solution.py:37
  12.9 2.7 %collective-permute-start.1 = (bf16[64,1024]{1,0:T(8,128)(2,1)S(1)}, bf16[64,1024]{1,0:T(8,128)(2,1)S(1)}, u32[]{:S(2)}, u32[]{:S(2)}) collective-permute-start(bf16[64,1024]{1,0:T(8,128)(2,1)S(1)} %constant_dynamic-update-slice_fusion.refs_0_), channel_id=1, source_target_pairs={{0,6},{1,7},{2,0},{3,1},{4,2},{5,3},{6,4},{7,5},{8,14},{9,15},{10,... | collective-permute-start | bytes 393224 | tf_op jit(solution)/shard_map/ppermute | solution.py:37
  16.8 5.2 %collective-permute-start.2 = (bf16[64,1024]{1,0:T(8,128)(2,1)S(1)}, bf16[64,1024]{1,0:T(8,128)(2,1)S(1)}, u32[]{:S(2)}, u32[]{:S(2)}) collective-permute-start(bf16[64,1024]{1,0:T(8,128)(2,1)S(1)} %constant_dynamic-update-slice_fusion.refs_0_), channel_id=1, source_target_pairs={{0,7},{1,6},{2,1},{3,0},{4,3},{5,2},{6,5},{7,4},{8,15},{9,14},{10,... | collective-permute-start | bytes 393224 | tf_op jit(solution)/shard_map/ppermute | solution.py:37
  22.4 4.6 %collective-permute-done.2.refs_3_ = bf16[64,1024]{1,0:T(8,128)(2,1)S(1)} collective-permute-done((bf16[64,1024]{1,0:T(8,128)(2,1)S(1)}, bf16[64,1024]{1,0:T(8,128)(2,1)S(1)}, u32[]{:S(2)}, u32[]{:S(2)}) %collective-permute-start.2) | collective-permute-done | bytes 131104 | tf_op jit(solution)/shard_map/ppermute | solution.py:37
  28.8 4.7 %collective-permute-start.5 = (bf16[64,1024]{1,0:T(8,128)(2,1)S(1)}, bf16[64,1024]{1,0:T(8,128)(2,1)S(1)}, u32[]{:S(2)}, u32[]{:S(2)}) collective-permute-start(bf16[64,1024]{1,0:T(8,128)(2,1)S(1)} %constant_dynamic-update-slice_fusion.refs_0_), channel_id=1, source_target_pairs={{0,2},{1,3},{2,4},{3,5},{4,6},{5,7},{6,0},{7,1},{8,10},{9,11},{10,... | collective-permute-start | bytes 393224 | tf_op jit(solution)/shard_map/ppermute | solution.py:37
  36.0 7.0 %collective-permute-done.6.refs_7_ = bf16[64,1024]{1,0:T(8,128)(2,1)S(1)} collective-permute-done((bf16[64,1024]{1,0:T(8,128)(2,1)S(1)}, bf16[64,1024]{1,0:T(8,128)(2,1)S(1)}, u32[]{:S(2)}, u32[]{:S(2)}) %collective-permute-start.6) | collective-permute-done | bytes 131104 | tf_op jit(solution)/shard_map/ppermute | solution.py:37
  43.8 4.2 %collective-permute-start.7 = (bf16[512,1024]{1,0:T(8,128)(2,1)S(1)}, bf16[512,1024]{1,0:T(8,128)(2,1)S(1)}, u32[]{:S(2)}, u32[]{:S(2)}) collective-permute-start(bf16[512,1024]{1,0:T(8,128)(2,1)S(1)} %get-tuple-element.36.tg), channel_id=1, source_target_pairs={{0,8},{8,0},{16,24},{24,16},{32,40},{40,32},{48,56},{56,48},{64,72... | collective-permute-start | bytes 3145736 | tf_op jit(solution)/shard_map/ppermute | solution.py:37
  50.4 5.4 %shard_map.86 = (bf16[3,64,768]{2,1,0:T(8,128)(2,1)S(1)}, bf16[3,3,64,768]{3,2,1,0:T(8,128)(2,1)S(1)}, f32[4,3,64,768]{3,2,1,0:T(8,128)S(1)}) custom-call(s32[3]{0:T(128)S(1)} %pad_add_fusion.pos, bf16[512,1024]{1,0:T(8,128)(2,1)S(1)} %get-tuple-element.36.tg, bf16[512,1024]{1,0:T(8,128)(2,1)S(1)} %collective-permute-done.7.tg_sib, bf16[512,3584]{1,0:T(8,128)(2,1)} %gw.11, ...), custom_call_target="tpu_custom_call" | custom-call | flops 2415919104 | bytes 16777216 | tf_op jit(solution)/shard_map/pallas_call | solution.py:119
  57.3 6.6 %shard_map.85 = (bf16[3,64,1024]{2,1,0:T(8,128)(2,1)S(1)}, bf16[3,64,1024]{2,1,0:T(8,128)(2,1)S(1)}, bf16[3,64,1024]{2,1,0:T(8,128)(2,1)S(1)}, bf16[3,64,1024]{2...) custom-call(s32[3]{0:T(128)S(1)} %pad_add_fusion.pos, ...), custom_call_target="tpu_custom_call" | custom-call | flops 3221225472 | bytes 16777216 | tf_op jit(solution)/shard_map/pallas_call | solution.py:119
  66.6 16.3 %collective-permute-done.27 = bf16[3,64,768]{2,1,0:T(8,128)(2,1)S(1)} collective-permute-done((bf16[3,64,768]{2,1,0:T(8,128)(2,1)S(1)}, bf16[3,64,768]{2,1,0:T(8,128)(2,1)S(1)}, u32[]{:S(2)}, u32[]{:S(2)}) %collective-permute-start.27) | collective-permute-done | bytes 294944 | tf_op jit(solution)/shard_map/ppermute | solution.py:37
  89.4 6.4 %collective-permute-done.32 = bf16[3,32,768]{2,1,0:T(8,128)(2,1)S(1)} collective-permute-done((bf16[3,32,768]{2,1,0:T(8,128)(2,1)S(1)}, bf16[3,32,768]{2,1,0:T(8,128)(2,1)S(1)}, u32[]{:S(2)}, u32[]{:S(2)}) %collective-permute-start.32) | collective-permute-done | bytes 147488 | tf_op jit(solution)/shard_map/ppermute | solution.py:37
  95.8 3.5 %collective-permute-start.33 = (bf16[3,32,768]{2,1,0:T(8,128)(2,1)S(1)}, bf16[3,32,768]{2,1,0:T(8,128)(2,1)S(1)}, u32[]{:S(2)}, u32[]{:S(2)}) collective-permute-start(bf16[3,32,768]{2,1,0:T(8,128)(2,1)S(1)} %fusion.1), channel_id=1, source_target_pairs={{0,96},{8,104},{16,112},{24,120},{32,0},{40,8},{48,16},{56,24},{64... | collective-permute-start | bytes 442376 | tf_op jit(solution)/shard_map/ppermute | solution.py:37
  112.6 9.2 %collective-permute-done.62 = bf16[64,768]{1,0:T(8,128)(2,1)S(1)} collective-permute-done((bf16[64,768]{1,0:T(8,128)(2,1)S(1)}, bf16[64,768]{1,0:T(8,128)(2,1)S(1)}, u32[]{:S(2)}, u32[]{:S(2)}) %collective-permute-start.62) | collective-permute-done | bytes 98336 | tf_op jit(solution)/shard_map/ppermute | solution.py:37
  139.8 5.1 %collective-permute-done.36 = bf16[2,64,768]{2,1,0:T(8,128)(2,1)S(1)} collective-permute-done((bf16[2,64,768]{2,1,0:T(8,128)(2,1)S(1)}, bf16[2,64,768]{2,1,0:T(8,128)(2,1)S(1)}, u32[]{:S(2)}, u32[]{:S(2)}) %collective-permute-start.36) | collective-permute-done | bytes 196640 | tf_op jit(solution)/shard_map/ppermute | solution.py:37
  145.0 4.7 %collective-permute-done.38 = bf16[2,32,768]{2,1,0:T(8,128)(2,1)S(1)} collective-permute-done((bf16[2,32,768]{2,1,0:T(8,128)(2,1)S(1)}, bf16[2,32,768]{2,1,0:T(8,128)(2,1)S(1)}, u32[]{:S(2)}, u32[]{:S(2)}) %collective-permute-start.38) | collective-permute-done | bytes 98336 | tf_op jit(solution)/shard_map/ppermute | solution.py:37
  149.6 3.6 %collective-permute-done.39 = bf16[2,32,768]{2,1,0:T(8,128)(2,1)S(1)} collective-permute-done((bf16[2,32,768]{2,1,0:T(8,128)(2,1)S(1)}, bf16[2,32,768]{2,1,0:T(8,128)(2,1)S(1)}, u32[]{:S(2)}, u32[]{:S(2)}) %collective-permute-start.39) | collective-permute-done | bytes 98336 | tf_op jit(solution)/shard_map/ppermute | solution.py:37
  159.5 3.2 %collective-permute-start.23 = (bf16[2,64,1024]{2,1,0:T(8,128)(2,1)S(1)}, bf16[2,64,1024]{2,1,0:T(8,128)(2,1)S(1)}, u32[]{:S(2)}, u32[]{:S(2)}) collective-permute-start(bf16[2,64,1024]{2,1,0:T(8,128)(2,1)S(1)} %collective-permute-done.20), channel_id=1, source_target_pairs={{0,96},{8,104},{16,112},{24,120},{32,0},{40,8},{48,16},{56,24},{64... | collective-permute-start | bytes 786440 | tf_op jit(solution)/shard_map/ppermute | solution.py:37
  167.7 3.1 %collective-permute-done.24 = bf16[2,64,1024]{2,1,0:T(8,128)(2,1)S(1)} collective-permute-done((bf16[2,64,1024]{2,1,0:T(8,128)(2,1)S(1)}, bf16[2,64,1024]{2,1,0:T(8,128)(2,1)S(1)}, u32[]{:S(2)}, u32[]{:S(2)}) %collective-permute-start.24) | collective-permute-done | bytes 262176 | tf_op jit(solution)/shard_map/ppermute | solution.py:37
  171.5 3.0 %collective-permute-done.41 = bf16[2,32,768]{2,1,0:T(8,128)(2,1)S(1)} collective-permute-done((bf16[2,32,768]{2,1,0:T(8,128)(2,1)S(1)}, bf16[2,32,768]{2,1,0:T(8,128)(2,1)S(1)}, u32[]{:S(2)}, u32[]{:S(2)}) %collective-permute-start.41) | collective-permute-done | bytes 98336 | tf_op jit(solution)/shard_map/ppermute | solution.py:37
  174.5 13.4 %collective-permute-start.25 = (bf16[2,512,1024]{2,1,0:T(8,128)(2,1)S(1)}, bf16[2,512,1024]{2,1,0:T(8,128)(2,1)S(1)}, u32[]{:S(2)}, u32[]{:S(2)}) collective-permute-start(bf16[2,512,1024]{2,1,0:T(8,128)(2,1)S(1)} %constant_dynamic-update-slice_fusion.2.grads), channel_id=1, source_target_pairs={{0,8},{8,0},{16,24},{24,16},{32,40},{40,32},{48,56},{56,48},{64,72... | collective-permute-start | bytes 6291464 | tf_op jit(solution)/shard_map/ppermute | solution.py:37
  191.4 2.7 %collective-permute-start.53 = (bf16[64,1024]{1,0:T(8,128)(2,1)S(1)}, bf16[64,1024]{1,0:T(8,128)(2,1)S(1)}, u32[]{:S(2)}, u32[]{:S(2)}) collective-permute-start(bf16[64,1024]{1,0:T(8,128)(2,1)S(1)} %collective-permute-done.51), channel_id=1, source_target_pairs={{0,96},{8,104},{16,112},{24,120},{32,0},{40,8},{48,16},{56,24},{64... | collective-permute-start | bytes 393224 | tf_op jit(solution)/shard_map/ppermute | solution.py:37
  196.8 2.7 %collective-permute-start.56 = (bf16[64,1024]{1,0:T(8,128)(2,1)S(1)}, bf16[64,1024]{1,0:T(8,128)(2,1)S(1)}, u32[]{:S(2)}, u32[]{:S(2)}) collective-permute-start(bf16[64,1024]{1,0:T(8,128)(2,1)S(1)} %collective-permute-done.53), channel_id=1, source_target_pairs={{0,96},{8,104},{16,112},{24,120},{32,0},{40,8},{48,16},{56,24},{64... | collective-permute-start | bytes 393224 | tf_op jit(solution)/shard_map/ppermute | solution.py:37
  201.9 5.0 %collective-permute-done.57 = bf16[64,1024]{1,0:T(8,128)(2,1)S(1)} collective-permute-done((bf16[64,1024]{1,0:T(8,128)(2,1)S(1)}, bf16[64,1024]{1,0:T(8,128)(2,1)S(1)}, u32[]{:S(2)}, u32[]{:S(2)}) %collective-permute-start.57) | collective-permute-done | bytes 131104 | tf_op jit(solution)/shard_map/ppermute | solution.py:37
  206.9 4.1 %collective-permute-start.58 = (bf16[512,1024]{1,0:T(8,128)(2,1)S(1)}, bf16[512,1024]{1,0:T(8,128)(2,1)S(1)}, u32[]{:S(2)}, u32[]{:S(2)}) collective-permute-start(bf16[512,1024]{1,0:T(8,128)(2,1)S(1)} %constant_dynamic-update-slice_fusion.20.hidden), channel_id=1, source_target_pairs={{0,8},{8,0},{16,24},{24,16},{32,40},{40,32},{48,56},{56,48},{64,72... | collective-permute-start | bytes 3145736 | tf_op jit(solution)/shard_map/ppermute | solution.py:37
  211.1 4.2 %shard_map.87 = (bf16[512,3584]{1,0:T(8,128)(2,1)}, bf16[512,3584]{1,0:T(8,128)(2,1)}, f32[512,512]{1,0:T(8,128)S(1)}) custom-call(s32[3]{0:T(128)S(1)} %pad_add_fusion.pos, bf16[2,512,768]{2,1,0:T(8,128)(2,1)S(1)} %constant_dynamic-update-slice_fusion.10.grads, bf16[512,512]{1,0:T(8,128)(2,1)S(1)} %get-tuple-element.45.tok_t, ...), custom_call_target="tpu_custom_call" | custom-call | flops 1610612736 | bytes 3145728 | tf_op jit(solution)/shard_map/pallas_call | solution.py:184
  215.2 5.3 %shard_map.88 = (bf16[512,3584]{1,0:T(8,128)(2,1)}, bf16[512,3584]{1,0:T(8,128)(2,1)}, f32[512,512]{1,0:T(8,128)S(1)}) custom-call(s32[3]{0:T(128)S(1)} %pad_add_fusion.pos, bf16[2,512,1024]{2,1,0:T(8,128)(2,1)S(1)} %constant_dynamic-update-slice_fusion.2.grads, ...), custom_call_target="tpu_custom_call", output_to_operand_aliasing={{0}: (6, {}), {1}: (7, {})} | custom-call | flops 2147483648 | bytes 4194304 | tf_op jit(solution)/shard_map/pallas_call | solution.py:184
  220.6 4.2 %shard_map.89 = (bf16[512,3584]{1,0:T(8,128)(2,1)}, bf16[512,3584]{1,0:T(8,128)(2,1)}, f32[512,512]{1,0:T(8,128)S(1)}) custom-call(s32[3]{0:T(128)S(1)} %pad_add_fusion.pos, bf16[2,512,768]{2,1,0:T(8,128)(2,1)S(1)} %collective-permute-done.43.grads, bf16[512,512]{1,0:T(8,128)(2,1)S(1)} %get-tuple-element.45.tok_t, ...), custom_call_target="tpu_custom_call", output_to_operand_aliasing={{0}: (6, {}), {1}: (7, {})} | custom-call | flops 1610612736 | bytes 3145728 | tf_op jit(solution)/shard_map/pallas_call | solution.py:184
  224.8 5.3 %shard_map.90 = (bf16[512,3584]{1,0:T(8,128)(2,1)}, bf16[512,3584]{1,0:T(8,128)(2,1)}, f32[64,512]{1,0:T(8,128)S(1)}, f32[64,512]{1,0:T(8,128)S(1)}, f32[64,512]...) custom-call(s32[3]{0:T(128)S(1)} %pad_add_fusion.pos, ...), custom_call_target="tpu_custom_call", output_to_operand_aliasing={{0}: (6, {}), {1}: (7, {})} | custom-call | flops 2147483648 | bytes 4194304 | tf_op jit(solution)/shard_map/pallas_call | solution.py:184
  235.3 4.1 %collective-permute-start.47 = (f32[64,512]{1,0:T(8,128)S(1)}, f32[64,512]{1,0:T(8,128)S(1)}, u32[]{:S(2)}, u32[]{:S(2)}) collective-permute-start(f32[64,512]{1,0:T(8,128)S(1)} %get-tuple-element.62), channel_id=1, source_target_pairs={{0,4},{1,5},{2,6},{3,7},{4,0},{5,1},{6,2},{7,3},{8,12},{9,13},{10,... | collective-permute-start | bytes 393224 | tf_op jit(solution)/shard_map/ppermute | solution.py:37
  245.1 3.1 %shard_map.92.refs_0_ = bf16[3584,512]{1,0:T(8,128)(2,1)} custom-call(s32[3]{0:T(128)S(1)} %pad_add_fusion.pos, bf16[512,1024]{1,0:T(8,128)(2,1)S(1)} %constant_dynamic-update-slice_fusion.20.hidden, bf16[512,1024]{1,0:T(8,128)(2,1)S(1)} %get-tuple-element.36.tg, bf16[3584,512]{1,0:T(8,128)(2,1)} %shard_map.91.refs_0_), custom_call_target="tpu_custom_call", output_to_operand_aliasing={{}: (3, {})} | custom-call | flops 536870912 | bytes 3145728 | tf_op jit(solution)/shard_map/pallas_call | solution.py:210
  250.8 3.1 %shard_map.94 = bf16[3584,512]{1,0:T(8,128)(2,1)} custom-call(s32[3]{0:T(128)S(1)} %pad_add_fusion.pos, bf16[512,1024]{1,0:T(8,128)(2,1)S(1)} %collective-permute-done.58.hidden, bf16[512,1024]{1,0:T(8,128)(2,1)S(1)} %get-tuple-element.36.tg, bf16[3584,512]{1,0:T(8,128)(2,1)} %shard_map.93.refs_0_), custom_call_target="tpu_custom_call", output_to_operand_aliasing={{}: (3, {})} | custom-call | flops 536870912 | bytes 3145728 | tf_op jit(solution)/shard_map/pallas_call | solution.py:210
  (190 shorter events, 91.0 us)
Async XLA Ops:
  3.7 46.7 %collective-permute-start.10 = (bf16[1792,512]{1,0:T(8,128)(2,1)}, bf16[1792,512]{1,0:T(8,128)(2,1)S(1)}, u32[]{:S(2)}, u32[]{:S(2)}) collective-permute-start(bf16[1792,512]{1,0:T(8,128)(2,1)} %constant_dynamic-slice_fusion), channel_id=1, source_target_pairs={{0,8},{8,0},{16,24},{24,16},{32,40},{40,32},{48,56},{56,48},{64,72... | collective-permute-start | bytes 5505032 | tf_op jit(solution)/shard_map/ppermute | solution.py:37
  6.4 43.9 %collective-permute-start.8 = (bf16[512,1792]{1,0:T(8,128)(2,1)}, bf16[512,1792]{1,0:T(8,128)(2,1)}, u32[]{:S(2)}, u32[]{:S(2)}) collective-permute-start(bf16[512,1792]{1,0:T(8,128)(2,1)} %constant_dynamic-slice_fusion.2), channel_id=1, source_target_pairs={{0,8},{8,0},{16,24},{24,16},{32,40},{40,32},{48,56},{56,48},{64,72... | collective-permute-start | bytes 5505032 | tf_op jit(solution)/shard_map/ppermute | solution.py:37
  7.8 42.5 %collective-permute-start.9 = (bf16[512,1792]{1,0:T(8,128)(2,1)}, bf16[512,1792]{1,0:T(8,128)(2,1)}, u32[]{:S(2)}, u32[]{:S(2)}) collective-permute-start(bf16[512,1792]{1,0:T(8,128)(2,1)} %constant_dynamic-slice_fusion.1), channel_id=1, source_target_pairs={{0,8},{8,0},{16,24},{24,16},{32,40},{40,32},{48,56},{56,48},{64,72... | collective-permute-start | bytes 5505032 | tf_op jit(solution)/shard_map/ppermute | solution.py:37
  55.7 31.6 %collective-permute-start.26 = (bf16[3,3,64,768]{3,2,1,0:T(8,128)(2,1)S(1)}, bf16[3,3,64,768]{3,2,1,0:T(8,128)(2,1)S(1)}, u32[]{:S(2)}, u32[]{:S(2)}) collective-permute-start(bf16[3,3,64,768]{3,2,1,0:T(8,128)(2,1)S(1)} %get-tuple-element.47), channel_id=1, source_target_pairs={{0,16},{8,24},{16,0},{24,8},{32,48},{40,56},{48,32},{56,40},{64,80... | collective-permute-start | bytes 2654216 | tf_op jit(solution)/shard_map/ppermute | solution.py:37
  56.5 26.4 %collective-permute-start.27 = (bf16[3,64,768]{2,1,0:T(8,128)(2,1)S(1)}, bf16[3,64,768]{2,1,0:T(8,128)(2,1)S(1)}, u32[]{:S(2)}, u32[]{:S(2)}) collective-permute-start(bf16[3,64,768]{2,1,0:T(8,128)(2,1)S(1)} %get-tuple-element.48), channel_id=1, source_target_pairs={{0,16},{8,24},{16,0},{24,8},{32,48},{40,56},{48,32},{56,40},{64,80... | collective-permute-start | bytes 884744 | tf_op jit(solution)/shard_map/ppermute | solution.py:37
  63.9 21.7 %collective-permute-start.12 = (bf16[3,64,1024]{2,1,0:T(8,128)(2,1)S(1)}, bf16[3,64,1024]{2,1,0:T(8,128)(2,1)S(1)}, u32[]{:S(2)}, u32[]{:S(2)}) collective-permute-start(bf16[3,64,1024]{2,1,0:T(8,128)(2,1)S(1)} %get-tuple-element.40), channel_id=1, source_target_pairs={{0,32},{8,40},{16,48},{24,56},{32,64},{40,72},{48,80},{56,88},{64,... | collective-permute-start | bytes 1179656 | tf_op jit(solution)/shard_map/ppermute | solution.py:37
  65.2 21.1 %collective-permute-start.15 = (bf16[3,64,1024]{2,1,0:T(8,128)(2,1)S(1)}, bf16[3,64,1024]{2,1,0:T(8,128)(2,1)S(1)}, u32[]{:S(2)}, u32[]{:S(2)}) collective-permute-start(bf16[3,64,1024]{2,1,0:T(8,128)(2,1)S(1)} %get-tuple-element.44), channel_id=1, source_target_pairs={{0,96},{8,104},{16,112},{24,120},{32,0},{40,8},{48,16},{56,24},{64... | collective-permute-start | bytes 1179656 | tf_op jit(solution)/shard_map/ppermute | solution.py:37
  66.6 32.9 %collective-permute-start.14 = (bf16[3,64,1024]{2,1,0:T(8,128)(2,1)S(1)}, bf16[3,64,1024]{2,1,0:T(8,128)(2,1)S(1)}, u32[]{:S(2)}, u32[]{:S(2)}) collective-permute-start(bf16[3,64,1024]{2,1,0:T(8,128)(2,1)S(1)} %get-tuple-element.42), channel_id=1, source_target_pairs={{0,32},{8,40},{16,48},{24,56},{32,64},{40,72},{48,80},{56,88},{64,... | collective-permute-start | bytes 1179656 | tf_op jit(solution)/shard_map/ppermute | solution.py:37
  83.0 45.4 %collective-permute-start.11 = (bf16[3,64,1024]{2,1,0:T(8,128)(2,1)S(1)}, bf16[3,64,1024]{2,1,0:T(8,128)(2,1)S(1)}, u32[]{:S(2)}, u32[]{:S(2)}) collective-permute-start(bf16[3,64,1024]{2,1,0:T(8,128)(2,1)S(1)} %get-tuple-element.38), channel_id=1, source_target_pairs={{0,96},{8,104},{16,112},{24,120},{32,0},{40,8},{48,16},{56,24},{64... | collective-permute-start | bytes 1179656 | tf_op jit(solution)/shard_map/ppermute | solution.py:37
  86.3 13.1 %collective-permute-start.28 = (bf16[3,32,768]{2,1,0:T(8,128)(2,1)S(1)}, bf16[3,32,768]{2,1,0:T(8,128)(2,1)S(1)}, u32[]{:S(2)}, u32[]{:S(2)}) collective-permute-start(bf16[3,32,768]{2,1,0:T(8,128)(2,1)S(1)} %get-tuple-element.82), channel_id=1, source_target_pairs={{0,32},{8,40},{16,48},{24,56},{32,64},{40,72},{48,80},{56,88},{64,... | collective-permute-start | bytes 442376 | tf_op jit(solution)/shard_map/ppermute | solution.py:37
  87.4 16.9 %collective-permute-start.16 = (bf16[3,64,1024]{2,1,0:T(8,128)(2,1)S(1)}, bf16[3,64,1024]{2,1,0:T(8,128)(2,1)S(1)}, u32[]{:S(2)}, u32[]{:S(2)}) collective-permute-start(bf16[3,64,1024]{2,1,0:T(8,128)(2,1)S(1)} %add_convert_fusion.1), channel_id=1, source_target_pairs={{0,96},{8,104},{16,112},{24,120},{32,0},{40,8},{48,16},{56,24},{64... | collective-permute-start | bytes 1179656 | tf_op jit(solution)/shard_map/ppermute | solution.py:37
  95.8 11.6 %collective-permute-start.33 = (bf16[3,32,768]{2,1,0:T(8,128)(2,1)S(1)}, bf16[3,32,768]{2,1,0:T(8,128)(2,1)S(1)}, u32[]{:S(2)}, u32[]{:S(2)}) collective-permute-start(bf16[3,32,768]{2,1,0:T(8,128)(2,1)S(1)} %fusion.1), channel_id=1, source_target_pairs={{0,96},{8,104},{16,112},{24,120},{32,0},{40,8},{48,16},{56,24},{64... | collective-permute-start | bytes 442376 | tf_op jit(solution)/shard_map/ppermute | solution.py:37
  107.4 21.1 %collective-permute-start.13 = (bf16[3,64,1024]{2,1,0:T(8,128)(2,1)S(1)}, bf16[3,64,1024]{2,1,0:T(8,128)(2,1)S(1)}, u32[]{:S(2)}, u32[]{:S(2)}) collective-permute-start(bf16[3,64,1024]{2,1,0:T(8,128)(2,1)S(1)} %add_convert_fusion.2), channel_id=1, source_target_pairs={{0,32},{8,40},{16,48},{24,56},{32,64},{40,72},{48,80},{56,88},{64,... | collective-permute-start | bytes 1179656 | tf_op jit(solution)/shard_map/ppermute | solution.py:37
  108.4 20.2 %collective-permute-start.17 = (bf16[3,64,1024]{2,1,0:T(8,128)(2,1)S(1)}, bf16[3,64,1024]{2,1,0:T(8,128)(2,1)S(1)}, u32[]{:S(2)}, u32[]{:S(2)}) collective-permute-start(bf16[3,64,1024]{2,1,0:T(8,128)(2,1)S(1)} %add_convert_fusion), channel_id=1, source_target_pairs={{0,16},{8,24},{16,0},{24,8},{32,48},{40,56},{48,32},{56,40},{64,80... | collective-permute-start | bytes 1179656 | tf_op jit(solution)/shard_map/ppermute | solution.py:37
  111.0 14.9 %collective-permute-start.59 = (bf16[64,768]{1,0:T(8,128)(2,1)S(1)}, bf16[64,768]{1,0:T(8,128)(2,1)S(1)}, u32[]{:S(2)}, u32[]{:S(2)}) collective-permute-start(bf16[64,768]{1,0:T(8,128)(2,1)S(1)} %get-tuple-element.69), channel_id=1, source_target_pairs={{0,16},{8,24},{16,0},{24,8},{32,48},{40,56},{48,32},{56,40},{64,80... | collective-permute-start | bytes 294920 | tf_op jit(solution)/shard_map/ppermute | solution.py:37
  132.6 21.3 %collective-permute-start.18 = (bf16[2,64,1024]{2,1,0:T(8,128)(2,1)S(1)}, bf16[2,64,1024]{2,1,0:T(8,128)(2,1)S(1)}, u32[]{:S(2)}, u32[]{:S(2)}) collective-permute-start(bf16[2,64,1024]{2,1,0:T(8,128)(2,1)S(1)} %get-tuple-element.84), channel_id=1, source_target_pairs={{0,16},{8,24},{16,0},{24,8},{32,48},{40,56},{48,32},{56,40},{64,80... | collective-permute-start | bytes 786440 | tf_op jit(solution)/shard_map/ppermute | solution.py:37
  135.6 22.6 %collective-permute-start.19 = (bf16[2,64,1024]{2,1,0:T(8,128)(2,1)S(1)}, bf16[2,64,1024]{2,1,0:T(8,128)(2,1)S(1)}, u32[]{:S(2)}, u32[]{:S(2)}) collective-permute-start(bf16[2,64,1024]{2,1,0:T(8,128)(2,1)S(1)} %get-tuple-element.84), channel_id=1, source_target_pairs={{0,96},{8,104},{16,112},{24,120},{32,0},{40,8},{48,16},{56,24},{64... | collective-permute-start | bytes 786440 | tf_op jit(solution)/shard_map/ppermute | solution.py:37
  138.9 18.9 %collective-permute-start.21 = (bf16[2,64,1024]{2,1,0:T(8,128)(2,1)S(1)}, bf16[2,64,1024]{2,1,0:T(8,128)(2,1)S(1)}, u32[]{:S(2)}, u32[]{:S(2)}) collective-permute-start(bf16[2,64,1024]{2,1,0:T(8,128)(2,1)S(1)} %get-tuple-element.84), channel_id=1, source_target_pairs={{0,32},{8,40},{16,48},{24,56},{32,64},{40,72},{48,80},{56,88},{64,... | collective-permute-start | bytes 786440 | tf_op jit(solution)/shard_map/ppermute | solution.py:37
  139.0 52.4 %collective-permute-start.51 = (bf16[64,1024]{1,0:T(8,128)(2,1)S(1)}, bf16[64,1024]{1,0:T(8,128)(2,1)S(1)}, u32[]{:S(2)}, u32[]{:S(2)}) collective-permute-start(bf16[64,1024]{1,0:T(8,128)(2,1)S(1)} %get-tuple-element.72), channel_id=1, source_target_pairs={{0,16},{8,24},{16,0},{24,8},{32,48},{40,56},{48,32},{56,40},{64,80... | collective-permute-start | bytes 393224 | tf_op jit(solution)/shard_map/ppermute | solution.py:37
  156.7 37.4 %collective-permute-start.52 = (bf16[64,1024]{1,0:T(8,128)(2,1)S(1)}, bf16[64,1024]{1,0:T(8,128)(2,1)S(1)}, u32[]{:S(2)}, u32[]{:S(2)}) collective-permute-start(bf16[64,1024]{1,0:T(8,128)(2,1)S(1)} %get-tuple-element.72), channel_id=1, source_target_pairs={{0,96},{8,104},{16,112},{24,120},{32,0},{40,8},{48,16},{56,24},{64... | collective-permute-start | bytes 393224 | tf_op jit(solution)/shard_map/ppermute | solution.py:37
  158.3 30.5 %collective-permute-start.65 = (bf16[32,768]{1,0:T(8,128)(2,1)S(1)}, bf16[32,768]{1,0:T(8,128)(2,1)S(1)}, u32[]{:S(2)}, u32[]{:S(2)}) collective-permute-start(bf16[32,768]{1,0:T(8,128)(2,1)S(1)} %collective-permute-done.63), channel_id=1, source_target_pairs={{0,16},{8,24},{16,0},{24,8},{32,48},{40,56},{48,32},{56,40},{64,80... | collective-permute-start | bytes 147464 | tf_op jit(solution)/shard_map/ppermute | solution.py:37
  166.9 21.0 %collective-permute-start.42 = (bf16[2,64,768]{2,1,0:T(8,128)(2,1)S(1)}, bf16[2,64,768]{2,1,0:T(8,128)(2,1)S(1)}, u32[]{:S(2)}, u32[]{:S(2)}) collective-permute-start(bf16[2,64,768]{2,1,0:T(8,128)(2,1)S(1)} %collective-permute-done.37), channel_id=1, source_target_pairs={{0,16},{8,24},{16,0},{24,8},{32,48},{40,56},{48,32},{56,40},{64,80... | collective-permute-start | bytes 589832 | tf_op jit(solution)/shard_map/ppermute | solution.py:37
  174.5 50.3 %collective-permute-start.25 = (bf16[2,512,1024]{2,1,0:T(8,128)(2,1)S(1)}, bf16[2,512,1024]{2,1,0:T(8,128)(2,1)S(1)}, u32[]{:S(2)}, u32[]{:S(2)}) collective-permute-start(bf16[2,512,1024]{2,1,0:T(8,128)(2,1)S(1)} %constant_dynamic-update-slice_fusion.2.grads), channel_id=1, source_target_pairs={{0,8},{8,0},{16,24},{24,16},{32,40},{40,32},{48,56},{56,48},{64,72... | collective-permute-start | bytes 6291464 | tf_op jit(solution)/shard_map/ppermute | solution.py:37
  188.7 31.8 %collective-permute-start.43 = (bf16[2,512,768]{2,1,0:T(8,128)(2,1)S(1)}, bf16[2,512,768]{2,1,0:T(8,128)(2,1)S(1)}, u32[]{:S(2)}, u32[]{:S(2)}) collective-permute-start(bf16[2,512,768]{2,1,0:T(8,128)(2,1)S(1)} %constant_dynamic-update-slice_fusion.10.grads), channel_id=1, source_target_pairs={{0,8},{8,0},{16,24},{24,16},{32,40},{40,32},{48,56},{56,48},{64,72... | collective-permute-start | bytes 4718600 | tf_op jit(solution)/shard_map/ppermute | solution.py:37
  194.1 16.8 %collective-permute-start.67 = (bf16[64,768]{1,0:T(8,128)(2,1)S(1)}, bf16[64,768]{1,0:T(8,128)(2,1)S(1)}, u32[]{:S(2)}, u32[]{:S(2)}) collective-permute-start(bf16[64,768]{1,0:T(8,128)(2,1)S(1)} %collective-permute-done.62), channel_id=1, source_target_pairs={{0,16},{8,24},{16,0},{24,8},{32,48},{40,56},{48,32},{56,40},{64,80... | collective-permute-start | bytes 294920 | tf_op jit(solution)/shard_map/ppermute | solution.py:37
  206.9 32.5 %collective-permute-start.58 = (bf16[512,1024]{1,0:T(8,128)(2,1)S(1)}, bf16[512,1024]{1,0:T(8,128)(2,1)S(1)}, u32[]{:S(2)}, u32[]{:S(2)}) collective-permute-start(bf16[512,1024]{1,0:T(8,128)(2,1)S(1)} %constant_dynamic-update-slice_fusion.20.hidden), channel_id=1, source_target_pairs={{0,8},{8,0},{16,24},{24,16},{32,40},{40,32},{48,56},{56,48},{64,72... | collective-permute-start | bytes 3145736 | tf_op jit(solution)/shard_map/ppermute | solution.py:37
  210.9 24.3 %collective-permute-start.68 = (bf16[512,768]{1,0:T(8,128)(2,1)S(1)}, bf16[512,768]{1,0:T(8,128)(2,1)S(1)}, u32[]{:S(2)}, u32[]{:S(2)}) collective-permute-start(bf16[512,768]{1,0:T(8,128)(2,1)S(1)} %constant_dynamic-update-slice_fusion.28.hidden), channel_id=1, source_target_pairs={{0,8},{8,0},{16,24},{24,16},{32,40},{40,32},{48,56},{56,48},{64,72... | collective-permute-start | bytes 2359304 | tf_op jit(solution)/shard_map/ppermute | solution.py:37
  230.7 11.9 %collective-permute-start.45 = (f32[64,512]{1,0:T(8,128)S(1)}, f32[64,512]{1,0:T(8,128)S(1)}, u32[]{:S(2)}, u32[]{:S(2)}) collective-permute-start(f32[64,512]{1,0:T(8,128)S(1)} %get-tuple-element.60), channel_id=1, source_target_pairs={{0,2},{1,3},{2,4},{3,5},{4,6},{5,7},{6,0},{7,1},{8,10},{9,11},{10,... | collective-permute-start | bytes 393224 | tf_op jit(solution)/shard_map/ppermute | solution.py:37
  233.4 20.5 %collective-permute-start.46 = (f32[64,512]{1,0:T(8,128)S(1)}, f32[64,512]{1,0:T(8,128)S(1)}, u32[]{:S(2)}, u32[]{:S(2)}) collective-permute-start(f32[64,512]{1,0:T(8,128)S(1)} %get-tuple-element.61), channel_id=1, source_target_pairs={{0,3},{1,2},{2,5},{3,4},{4,7},{5,6},{6,1},{7,0},{8,11},{9,10},{10,... | collective-permute-start | bytes 393224 | tf_op jit(solution)/shard_map/ppermute | solution.py:37
  235.3 18.7 %collective-permute-start.47 = (f32[64,512]{1,0:T(8,128)S(1)}, f32[64,512]{1,0:T(8,128)S(1)}, u32[]{:S(2)}, u32[]{:S(2)}) collective-permute-start(f32[64,512]{1,0:T(8,128)S(1)} %get-tuple-element.62), channel_id=1, source_target_pairs={{0,4},{1,5},{2,6},{3,7},{4,0},{5,1},{6,2},{7,3},{8,12},{9,13},{10,... | collective-permute-start | bytes 393224 | tf_op jit(solution)/shard_map/ppermute | solution.py:37
  239.4 14.6 %collective-permute-start.48 = (f32[64,512]{1,0:T(8,128)S(1)}, f32[64,512]{1,0:T(8,128)S(1)}, u32[]{:S(2)}, u32[]{:S(2)}) collective-permute-start(f32[64,512]{1,0:T(8,128)S(1)} %get-tuple-element.63), channel_id=1, source_target_pairs={{0,5},{1,4},{2,7},{3,6},{4,1},{5,0},{6,3},{7,2},{8,13},{9,12},{10,... | collective-permute-start | bytes 393224 | tf_op jit(solution)/shard_map/ppermute | solution.py:37
  240.5 13.4 %collective-permute-start.49 = (f32[64,512]{1,0:T(8,128)S(1)}, f32[64,512]{1,0:T(8,128)S(1)}, u32[]{:S(2)}, u32[]{:S(2)}) collective-permute-start(f32[64,512]{1,0:T(8,128)S(1)} %get-tuple-element.64), channel_id=1, source_target_pairs={{0,6},{1,7},{2,0},{3,1},{4,2},{5,3},{6,4},{7,5},{8,14},{9,15},{10,... | collective-permute-start | bytes 393224 | tf_op jit(solution)/shard_map/ppermute | solution.py:37
  (43 other events, 372.6 us)

commit v2 on v0

v2 whole, which is shorter than its diff:
```python
import functools

import jax
import jax.numpy as jnp
from jax import lax
from jax.experimental import pallas as pl
from jax.experimental.pallas import tpu as pltpu
from jax.sharding import PartitionSpec as P

BF, F32 = jnp.bfloat16, jnp.float32
BLK = 64
TILE = 256
HALF = 7 * TILE
CUTS = (512, 1152)
MID = HALF // 2
TURN = CUTS[0], CUTS[1] - CUTS[0], HALF - CUTS[1]
ORDER = ((2, 1), (2, 0), (1, 1), (3, 1), (1, 0), (3, 0), (0, 1), (0, 0))
PLACES = sum(i << 4 * (2 * jx + jz) for i, (jx, jz) in enumerate(ORDER))


def gx_perm(move):
    pairs = []
    for i in range(16):
        x, z, c = move(i // 4, (i // 2) % 2, i % 2)
        pairs.append((i, (x % 4) * 4 + (z % 2) * 2 + c % 2))
    return pairs


CORE = gx_perm(lambda x, z, c: (x, z, c + 1))
XP = gx_perm(lambda x, z, c: (x + 1, z, c))
XM = gx_perm(lambda x, z, c: (x - 1, z, c))
ZS = gx_perm(lambda x, z, c: (x, z + 1, c))


def send(a, pairs):
    return lax.ppermute(a, "gx", pairs)


def dot(a, b, ca, cb):
    return lax.dot_general(a, b, (((ca,), (cb,)), ((), ())), preferred_element_type=F32)


def place(pos, b):
    chip = ((b // 2 - pos[0]) & 3) * 2 + ((b & 1) ^ pos[1])
    row = ((PLACES >> (4 * chip)) & 7) * BLK
    return pl.ds(pl.multiple_of(row, BLK), BLK)


def whole(shape):
    return pl.BlockSpec(shape, lambda i, pos: (0,) * len(shape))


def params(mib):
    return pltpu.CompilerParams(vmem_limit_bytes=mib << 20, dimension_semantics=("arbitrary",))


def spread_kernel(tokens, out_grad, copies):
    for b in range(8):
        copies[b, :, :512] = tokens[...]
        copies[b, :, 512:] = out_grad[...]


def spread(tokens, out_grad):
    return pl.pallas_call(
        spread_kernel,
        out_shape=jax.ShapeDtypeStruct((8, BLK, 1024), BF),
        compiler_params=pltpu.CompilerParams(vmem_limit_bytes=16 << 20),
        cost_estimate=pl.CostEstimate(flops=0, bytes_accessed=1 << 20, transcendentals=0),
    )(tokens, out_grad)


def order_kernel(pos, blocks, tg, tok_t):
    for b in range(8):
        tg[place(pos, b), :] = blocks[b]
    tok_t[...] = tg[:, :512].T


def order(pos, blocks):
    return pl.pallas_call(
        order_kernel,
        grid_spec=pltpu.PrefetchScalarGridSpec(
            num_scalar_prefetch=1,
            grid=(1,),
            in_specs=[whole((8, BLK, 1024))],
            out_specs=[whole((512, 1024)), whole((512, 512))],
        ),
        out_shape=[jax.ShapeDtypeStruct((512, 1024), BF), jax.ShapeDtypeStruct((512, 512), BF)],
        compiler_params=params(40),
        cost_estimate=pl.CostEstimate(flops=0, bytes_accessed=4 << 20, transcendentals=0),
    )(pos, blocks)


def sums_kernel(part, pos, tg, tg_sib, gw, uw, dw, gw_sib, uw_sib, dw_sib, *outs):
    for a in range(3):
        if a < 2:
            own, sib = ((gw, gw_sib), (uw, uw_sib))[a]
            total = dot(tg[:, :512], own[...], 1, 0) + dot(tg_sib[:, :512], sib[...], 1, 0)
        else:
            total = dot(tg[:, 512:], dw[...], 1, 1) + dot(tg_sib[:, 512:], dw_sib[...], 1, 1)
        blocks = [total[i * BLK : (i + 1) * BLK] for i in range(4)]
        for block, out in zip(blocks[part == 0 :], outs):
            out[a] = block
        if part == 0:
            far, (z, up, down) = blocks[0].astype(BF), outs[3:]
            up_lo = MID - CUTS[0]

            @pl.when(pl.program_id(0) == 0)
            def _():
                z[a] = far[:, : CUTS[0]]
                up[a, :, :up_lo] = far[:, CUTS[0] :]

            @pl.when(pl.program_id(0) == 1)
            def _():
                up[a, :, up_lo:] = far[:, : CUTS[1] - MID]
                down[a] = far[:, CUTS[1] - MID :]


def sums(pos, tg, tg_sib, weights, weights_sib, part):
    tile = MID
    cols, rows = (512, tile), (tile, 512)
    own = lambda i, pos: (0, pos[2] * 2 + i)
    sib = lambda i, pos: (0, i)
    flip = lambda f: (lambda i, pos: f(i, pos)[::-1])
    tokens = pl.BlockSpec((256, 1024), lambda i, pos: (part, 0))
    kept = 3 if part == 0 else 4
    far = [(3, BLK, width) for width in TURN] if part == 0 else []
    return pl.pallas_call(
        functools.partial(sums_kernel, part),
        grid_spec=pltpu.PrefetchScalarGridSpec(
            num_scalar_prefetch=1,
            grid=(2,),
            in_specs=[
                tokens,
                tokens,
                pl.BlockSpec(cols, own),
                pl.BlockSpec(cols, own),
                pl.BlockSpec(rows, flip(own)),
                pl.BlockSpec(cols, sib),
                pl.BlockSpec(cols, sib),
                pl.BlockSpec(rows, flip(sib)),
            ],
            out_specs=[pl.BlockSpec((3, BLK, tile), lambda i, pos: (0, 0, i))] * kept
            + [whole(shape) for shape in far],
        ),
        out_shape=[jax.ShapeDtypeStruct((3, BLK, HALF), F32)] * kept
        + [jax.ShapeDtypeStruct(shape, BF) for shape in far],
        compiler_params=params(40),
        cost_estimate=pl.CostEstimate(
            flops=2 * 3 * 256 * 1024 * HALF, bytes_accessed=20 << 20, transcendentals=0
        ),
    )(pos, tg, tg_sib, *weights, *weights_sib)


def stack(half, grads, near, mids, far):
    up, down, flat = 0, 1, 2
    grads[:, :BLK] = far[...]
    grads[:, 4 * BLK :] = near[...]
    for i, piece in enumerate((down, flat, up) if half else (up, down, flat)):
        grads[:, (i + 1) * BLK : (i + 2) * BLK] = mids[:, piece * BLK : (piece + 1) * BLK]


def part_kernel(half, has_terms, has_weights, carried, last, pos, *refs):
    refs = list(refs)
    near, mids, far = (refs.pop(0) for _ in range(3))
    gw, uw = (refs.pop(0) for _ in range(2)) if has_terms else (None, None)
    before = refs.pop(0) if has_terms and carried else None
    tok_t, tg = (refs.pop(0) for _ in range(2)) if has_weights else (None, None)
    grads = refs.pop()
    acc = refs.pop() if has_terms else None
    stack(half, grads, near, mids, far)
    if has_weights:
        ggw, guw, gdw = refs[-3:]
        ggw[...] = dot(tok_t[...], grads[0], 1, 0).astype(BF)
        guw[...] = dot(tok_t[...], grads[1], 1, 0).astype(BF)
        gdw[...] = dot(grads[2], tg[:, 512:], 0, 0).astype(BF)
    if has_terms:
        out = refs[-4] if has_weights else refs[-1]
        term = dot(grads[0], gw[...], 1, 1) + dot(grads[1], uw[...], 1, 1)
        if carried:
            term += before[...]
        if not last:
            out[...] = term
        else:
            acc[...] = term
            for b in range(8):
                out[b] = acc[place(pos, b), :].astype(BF)


def part(pos, pieces, core, half, terms=None, weights=None, last=False):
    tile = lambda pos: (core ^ pos[2]) * 2 + half
    arrays = 3 if weights else 2
    column = pl.BlockSpec((512, MID), lambda i, pos: (0, tile(pos)))
    row = pl.BlockSpec((MID, 512), lambda i, pos: (tile(pos), 0))
    square = whole((512, 512))
    in_specs = [
        pl.BlockSpec((arrays, r, MID), lambda i, pos: (0, 0, half)) for r in (256, 192, 64)
    ]
    args, out_specs, out_shape, scratch, aliases = [*pieces], [], [], [], {}
    carried = False
    if terms:
        gw, uw, before = terms
        in_specs += [column, column]
        args += [gw, uw]
        carried = before is not None
        if carried:
            in_specs.append(square)
            args.append(before)
        if last:
            out_specs.append(whole((8, BLK, 512)))
            out_shape.append(jax.ShapeDtypeStruct((8, BLK, 512), BF))
        else:
            out_specs.append(square)
            out_shape.append(jax.ShapeDtypeStruct((512, 512), F32))
        scratch.append(pltpu.VMEM((512, 512), F32))
    if weights:
        tok_t, tg, beside = weights
        in_specs += [square, whole((512, 1024))]
        args += [tok_t, tg]
        if beside is not None:
            for k in range(3):
                aliases[len(args) + 1 + k] = len(out_specs) + k
            in_specs += [pl.BlockSpec(memory_space=pl.ANY)] * 3
            args += beside
        out_specs += [column, column, row]
        out_shape += [jax.ShapeDtypeStruct((512, 2 * HALF), BF)] * 2
        out_shape += [jax.ShapeDtypeStruct((2 * HALF, 512), BF)]
    scratch.append(pltpu.VMEM((arrays, 512, MID), BF))
    flops = 2 * 512 * 512 * MID * (2 * bool(terms) + 3 * bool(weights))
    return pl.pallas_call(
        functools.partial(part_kernel, half, bool(terms), bool(weights), carried, last),
        grid_spec=pltpu.PrefetchScalarGridSpec(
            num_scalar_prefetch=1,
            grid=(1,),
            in_specs=in_specs,
            out_specs=out_specs,
            scratch_shapes=scratch,
        ),
        out_shape=out_shape,
        input_output_aliases=aliases,
        compiler_params=params(32),
        cost_estimate=pl.CostEstimate(flops=flops, bytes_accessed=8 << 20, transcendentals=0),
    )(pos, *args)


def wide(a):
    return a.astype(F32)


def lo(a):
    return a[..., :MID]


def hi(a):
    return a[..., MID:]


def join(*parts):
    return jnp.concatenate(parts, axis=-1)


def merge_kernel(p20, p11, p31, rz, rp, rm, down, up, flat):
    z, x = CUTS
    for a in range(3):
        down[a, :, :z] = (p20[a, :, :z] + wide(rz[a])).astype(BF)
        down[a, :, z:MID] = p20[a, :, z:MID].astype(BF)
        down[a, :, MID:x] = p31[a, :, MID:x].astype(BF)
        down[a, :, x:] = (p31[a, :, x:] + wide(rm[a])).astype(BF)
        up[a, :, :z] = p11[a, :, :z].astype(BF)
        up[a, :, z:MID] = (p11[a, :, z:MID] + wide(rp[a, :, : MID - z])).astype(BF)
        up[a, :, MID:] = p20[a, :, MID:].astype(BF)
        flat[a, :, :MID] = p31[a, :, :MID].astype(BF)
        flat[a, :, MID:x] = (p11[a, :, MID:x] + wide(rp[a, :, MID - z :])).astype(BF)
        flat[a, :, x:] = p11[a, :, x:].astype(BF)


def scatter_far(p20, p11, p31, far_z, far_up, far_down):
    return pl.pallas_call(
        merge_kernel,
        out_shape=[jax.ShapeDtypeStruct((3, BLK, HALF), BF)] * 3,
        compiler_params=pltpu.CompilerParams(vmem_limit_bytes=32 << 20),
        cost_estimate=pl.CostEstimate(flops=0, bytes_accessed=6 << 20, transcendentals=0),
    )(p20, p11, p31, send(far_z, ZS), send(far_up, XP), send(far_down, XM))


def scatter_mid(down, up, flat, p10, p30, p01):
    rm, rp, rz = wide(send(down, XM)), wide(send(up, XP)), wide(send(flat, ZS))
    p10 = join(lo(p10), hi(p10) + hi(rp) + hi(rz))
    p30 = join(lo(p30) + lo(rm) + lo(rz), hi(p30))
    p01 = join(lo(p01) + lo(rp), hi(p01) + hi(rm))
    return p10.astype(BF), p30.astype(BF), p01.astype(BF)


def scatter_last(up, down, flat, p00):
    rp, rm, rz = send(up, XP), send(down, XM), send(flat, ZS)
    return p00 + wide(rp) + wide(rm) + wide(rz)


def rows(*blocks):
    return jnp.concatenate(blocks, axis=-2)


def after(*arrays):
    return lax.optimization_barrier(arrays)


def gather(e):
    z, x = CUTS
    g30, g10, g01 = send(e, XP), send(e, XM), send(e, ZS)
    rp = send(join(lo(g30), hi(g01)), XP)
    rm = send(join(lo(g01), hi(g10)), XM)
    rz = send(join(lo(g30), hi(g10)), ZS)
    turn_up = join(rz[..., z:MID], rp[..., MID:x])
    fz, fp, fm = send(rp[..., :z], ZS), send(turn_up, XP), send(rz[..., x:], XM)
    far, near, mids = after(join(fz, fp, fm), rows(g10, g30, g01, e), rows(rp, rm, rz))
    pieces = near, mids, far
    return pieces, [send(piece, CORE) for piece in pieces]


def local_grads(gate_sum, upper_sum, back_sum):
    sigmoid_gate = jax.nn.sigmoid(gate_sum)
    silu_gate = gate_sum * sigmoid_gate
    hidden = (silu_gate * upper_sum).astype(BF)
    grad_gate = (
        back_sum * upper_sum * sigmoid_gate * (1.0 + gate_sum * (1.0 - sigmoid_gate))
    ).astype(BF)
    grad_upper = (back_sum * silu_gate).astype(BF)
    return jnp.stack([grad_gate, grad_upper, hidden])


def shards(tokens, out_grad, gate_weight, up_weight, down_weight):
    gx = lax.axis_index("gx")
    core = gx % 2
    pos = jnp.stack([gx // 4, (gx // 2) % 2, core]).astype(jnp.int32)
    far_half = (1 - core) * HALF

    blocks = lax.all_to_all(spread(tokens, out_grad), "gy", 0, 0, tiled=True)
    weights = (gate_weight, up_weight, down_weight)
    weights_sib = [
        send(lax.dynamic_slice_in_dim(w, far_half, HALF, axis), CORE)
        for w, axis in zip(weights, (1, 1, 0))
    ]
    tg, tok_t = order(pos, blocks)
    tg_sib = send(tg, CORE)

    first = sums(pos, tg, tg_sib, weights, weights_sib, 0)
    p10, p30, p01, p00 = sums(pos, tg, tg_sib, weights, weights_sib, 1)
    mid = scatter_far(*first)
    last = scatter_mid(*mid, p10, p30, p01)
    total = scatter_last(*last, p00)
    own, sib = gather(local_grads(total[0], total[1], total[2]))

    gw, uw = gate_weight, up_weight
    terms, *grads = part(pos, own, 0, 0, (gw, uw, None), (tok_t, tg, None))
    terms, *grads = part(pos, own, 0, 1, (gw, uw, terms), (tok_t, tg, grads))
    (terms,) = part(pos, sib, 1, 0, (gw, uw, terms))
    (terms,) = part(pos, sib, 1, 1, (gw, uw, terms), None, True)
    grad_tokens = jnp.sum(wide(lax.all_to_all(terms, "gy", 0, 0, tiled=True)), axis=0).astype(BF)
    grads = part(pos, sib, 1, 0, None, (tok_t, tg, grads))
    ggw, guw, gdw = part(pos, sib, 1, 1, None, (tok_t, tg, grads))
    return grad_tokens, ggw, guw, gdw


def solution(mesh):
    return jax.shard_map(
        shards,
        mesh=mesh,
        in_specs=(P("gy", "gx"), P("gy", "gx"), P("gx", "gy"), P("gx", "gy"), P("gy", "gx")),
        out_specs=(P("gy", "gx"), P("gx", "gy"), P("gx", "gy"), P("gy", "gx")),
        check_vma=False,
    )
```

time: 490 us -> 161 us (0.33)
  waiting for transfers between devices: 352 us -> 57.8 us
  blocking collectives: 61.1 us -> 0 us
  starting transfers between devices: 0.3 us -> 48.1 us
  Pallas kernels: 0 us -> 37 us
  matrix products: 36.9 us -> 0 us
  between operations: 13.8 us -> 0.98 us
  other arithmetic: 11.7 us -> 4.02 us
    reduce_scatter x2 -> x0, waiting for transfers between devices: 287 us -> none  [the longest x1 246 us: shards(): lax.psum_scatter(jnp.concatenate([gate_term, upper_term, back_term], axis...]
    all_gather x1 -> x0, waiting for transfers between devices: 64.9 us -> none  [shards(): gathered = lax.all_gather(packed, 'gx', axis=0, tiled=True)]
    all_gather x2 -> x0, blocking collectives: 61.1 us -> none  [the longest x1 31.2 us: shards(): lax.all_gather(tokens, 'gy', axis=0, tiled=True)]
    ppermute x0 -> x25, waiting for transfers between devices: none -> 50.4 us  [send(): return lax.ppermute(a, 'gx', pairs)]
    pallas_call x0 -> x11, Pallas kernels: none -> 37 us  [the longest x6 20.2 us: part(): pl.pallas_call(functools.partial(part_kernel, half, bool(terms), bool(wei...]
    dot_general x8 -> x0, matrix products: 36.9 us -> none  [the longest x1 6 us: shards(): jnp.dot(hidden_t, grad_all, preferred_element_type=jnp.float32)]
    ppermute x0 -> x25, starting transfers between devices: none -> 34.9 us  [send(): return lax.ppermute(a, 'gx', pairs)]
    all_to_all x0 -> x2, starting transfers between devices: none -> 13.2 us  [the longest x1 8.33 us: shards(): blocks = lax.all_to_all(spread(tokens, out_grad), 'gy', 0, 0, tiled=True)]
  transfers between devices with their start and end apart: 3 -> 27, of which waited for: 3 -> 12; matrix products, arithmetic and copies ran while one was open for 6% -> 4% of each run, Pallas kernels for 0% -> 15%
where the time goes in v2:
time: 161 us; the launch traced here: 160 us
  waiting for transfers between devices  57.8 us (36%)
  starting transfers between devices  48.1 us (30%)
  Pallas kernels  37 us (23%)
  local copies, waits for them, and re-layouts  12.3 us (8%)
  other arithmetic  4.02 us (2%)
    ppermute x25, waiting for transfers between devices, send(): return lax.ppermute(a, 'gx', pairs)  50.4 us
    ppermute x25, starting transfers between devices, send(): return lax.ppermute(a, 'gx', pairs)  34.9 us
    pallas_call x6, Pallas kernels, part(): pl.pallas_call(functools.partial(part_kernel, half, bool(terms), bool(wei...  20.2 us
    pallas_call x2, Pallas kernels, sums(): pl.pallas_call(functools.partial(sums_kernel, part), grid_spec=pltpu.Pref...  14.6 us
    all_to_all x1, starting transfers between devices, shards(): blocks = lax.all_to_all(spread(tokens, out_grad), 'gy', 0, 0, tiled=True)  8.33 us
    all_to_all x1, waiting for transfers between devices, shards(): blocks = lax.all_to_all(spread(tokens, out_grad), 'gy', 0, 0, tiled=True)  7.4 us
    unnamed x26, local copies, waits for them, and re-layouts  6.33 us
    dynamic_slice x3, local copies, waits for them, and re-layouts, shards(): lax.dynamic_slice_in_dim(w, far_half, HALF, axis)  5.69 us
  transfers between devices with their start and end apart: 27, of which 12 were waited for; matrix products, arithmetic and copies ran while one was open for 4% of the time, Pallas kernels for 15%

profile of v2, /device:TPU:1, one launch (start us, length us, event | category | flops | bytes accessed | tf_op | source)
XLA Modules:
  0.0 160.2 jit_solution(12185966412385085412)
XLA Ops:
  3.4 8.3 %all-to-all-start = ((bf16[8,64,1024]{2,1,0:T(8,128)(2,1)}), bf16[8,64,1024]{2,1,0:T(8,128)(2,1)S(1)}, u32[]{:S(2)}, u32[]{:S(2)}) async-start(bf16[8,64,1024]{2,1,0:T(8,128)(2,1)} %shard_map.84), calls=%async_computation | async-start | bytes 2097152 | tf_op jit(solution)/shard_map/all_to_all | solution.py:336
  11.7 3.0 %constant_dynamic-slice_fusion.2 = bf16[512,1792]{1,0:T(8,128)(2,1)} fusion(bf16[512,3584]{1,0:T(8,128)(2,1)} %refs_3_.7, s32[]{:T(128)S(6)} %select_n.27), kind=kLoop, calls=%fused_computation.31 | loop fusion | bytes 3670020 | tf_op jit(solution)/shard_map/dynamic_slice | solution.py:339
  15.7 1.3 constant_dynamic-slice_fusion.1
  17.0 1.3 constant_dynamic-slice_fusion
  18.4 1.3 collective-permute-start.3
  19.8 7.4 %all-to-all-done.blocks = bf16[8,64,1024]{2,1,0:T(8,128)(2,1)S(1)} async-done(((bf16[8,64,1024]{2,1,0:T(8,128)(2,1)}), bf16[8,64,1024]{2,1,0:T(8,128)(2,1)S(1)}, u32[]{:S(2)}, u32[]{:S(2)}) %all-to-all-start) | async-done | bytes 1048608 | tf_op jit(solution)/shard_map/all_to_all | solution.py:336
  28.0 1.4 collective-permute-start
  29.5 2.3 %collective-permute-done.tg_sib = bf16[512,1024]{1,0:T(8,128)(2,1)S(1)} collective-permute-done((bf16[512,1024]{1,0:T(8,128)(2,1)S(1)}, bf16[512,1024]{1,0:T(8,128)(2,1)S(1)}, u32[]{:S(2)}, u32[]{:S(2)}) %collective-permute-start) | collective-permute-done | bytes 1048608 | tf_op jit(solution)/shard_map/ppermute | solution.py:36
  31.7 7.7 %shard_map.87 = (f32[3,64,1792]{2,1,0:T(8,128)S(1)}, f32[3,64,1792]{2,1,0:T(8,128)S(1)}, f32[3,64,1792]{2,1,0:T(8,128)S(1)}, bf16[3,64,512]{2,1,0:T(8,128)(2,1)S...) custom-call(s32[3]{0:T(128)S(1)} %pad_add_fusion.pos, ...), custom_call_target="tpu_custom_call" | custom-call | flops 2818572288 | bytes 20971520 | tf_op jit(solution)/shard_map/pallas_call | solution.py:127
  40.7 1.5 collective-permute-start.6
  42.9 4.7 %collective-permute-done.4.rz = bf16[3,64,512]{2,1,0:T(8,128)(2,1)S(1)} collective-permute-done((bf16[3,64,512]{2,1,0:T(8,128)(2,1)S(1)}, bf16[3,64,512]{2,1,0:T(8,128)(2,1)S(1)}, u32[]{:S(2)}, u32[]{:S(2)}) %collective-permute-start.4) | collective-permute-done | bytes 196640 | tf_op jit(solution)/shard_map/ppermute | solution.py:36
  49.8 1.8 %collective-permute-start.10 = (bf16[3,64,1792]{2,1,0:T(8,128)(2,1)S(1)}, bf16[3,64,1792]{2,1,0:T(8,128)(2,1)S(1)}, u32[]{:S(2)}, u32[]{:S(2)}) collective-permute-start(bf16[3,64,1792]{2,1,0:T(8,128)(2,1)S(1)} %get-tuple-element.48), channel_id=1, source_target_pairs={{0,96},{8,104},{16,112},{24,120},{32,0},{40,8},{48,16},{56,24},{64... | collective-permute-start | bytes 2064392 | tf_op jit(solution)/shard_map/ppermute | solution.py:36
  51.6 6.9 %shard_map.86 = (f32[3,64,1792]{2,1,0:T(8,128)S(1)}, f32[3,64,1792]{2,1,0:T(8,128)S(1)}, f32[3,64,1792]{2,1,0:T(8,128)S(1)}, f32[3,64,1792]{2,1,0:T(8,128)S(1)}) custom-call(s32[3]{0:T(128)S(1)} %pad_add_fusion.pos, bf16[512,1024]{1,0:T(8,128)(2,1)S(1)} %get-tuple-element.36.tg.refs_6_.refs_7_.refs_4_, bf16[512,1024]{1,0:T(8,128)(2,1)S(1)} %collective-permute-done.tg_sib, ...), custom_call_target="tpu_custom_call" | custom-call | flops 2818572288 | bytes 20971520 | tf_op jit(solution)/shard_map/pallas_call | solution.py:127
  58.6 6.1 %collective-permute-done.7 = bf16[3,64,1792]{2,1,0:T(8,128)(2,1)S(1)} collective-permute-done((bf16[3,64,1792]{2,1,0:T(8,128)(2,1)S(1)}, bf16[3,64,1792]{2,1,0:T(8,128)(2,1)S(1)}, u32[]{:S(2)}, u32[]{:S(2)}) %collective-permute-start.7) | collective-permute-done | bytes 688160 | tf_op jit(solution)/shard_map/ppermute | solution.py:36
  66.4 2.1 %collective-permute-start.11 = (bf16[3,64,1792]{2,1,0:T(8,128)(2,1)S(1)}, bf16[3,64,1792]{2,1,0:T(8,128)(2,1)S(1)}, u32[]{:S(2)}, u32[]{:S(2)}) collective-permute-start(bf16[3,64,1792]{2,1,0:T(8,128)(2,1)S(1)} %pad_maximum_fusion.5), channel_id=1, source_target_pairs={{0,96},{8,104},{16,112},{24,120},{32,0},{40,8},{48,16},{56,24},{64... | collective-permute-start | bytes 2064392 | tf_op jit(solution)/shard_map/ppermute | solution.py:36
  69.4 11.7 %collective-permute-done.9 = bf16[3,64,1792]{2,1,0:T(8,128)(2,1)S(1)} collective-permute-done((bf16[3,64,1792]{2,1,0:T(8,128)(2,1)S(1)}, bf16[3,64,1792]{2,1,0:T(8,128)(2,1)S(1)}, u32[]{:S(2)}, u32[]{:S(2)}) %collective-permute-start.9) | collective-permute-done | bytes 688160 | tf_op jit(solution)/shard_map/ppermute | solution.py:36
  83.8 2.6 %collective-permute-start.17 = (bf16[3,64,1792]{2,1,0:T(8,128)(2,1)S(1)}, bf16[3,64,1792]{2,1,0:T(8,128)(2,1)S(1)}, u32[]{:S(2)}, u32[]{:S(2)}) collective-permute-start(bf16[3,64,1792]{2,1,0:T(8,128)(2,1)S(1)} %pad_maximum_fusion.7), channel_id=1, source_target_pairs={{0,96},{8,104},{16,112},{24,120},{32,0},{40,8},{48,16},{56,24},{64... | collective-permute-start | bytes 2064392 | tf_op jit(solution)/shard_map/ppermute | solution.py:36
  86.3 10.0 %collective-permute-done.13 = bf16[3,64,1792]{2,1,0:T(8,128)(2,1)S(1)} collective-permute-done((bf16[3,64,1792]{2,1,0:T(8,128)(2,1)S(1)}, bf16[3,64,1792]{2,1,0:T(8,128)(2,1)S(1)}, u32[]{:S(2)}, u32[]{:S(2)}) %collective-permute-start.13) | collective-permute-done | bytes 688160 | tf_op jit(solution)/shard_map/ppermute | solution.py:36
  97.7 2.7 %collective-permute-start.21 = (bf16[3,64,1792]{2,1,0:T(8,128)(2,1)S(1)}, bf16[3,64,1792]{2,1,0:T(8,128)(2,1)S(1)}, u32[]{:S(2)}, u32[]{:S(2)}) collective-permute-start(bf16[3,64,1792]{2,1,0:T(8,128)(2,1)S(1)} %get-tuple-element.77), channel_id=1, source_target_pairs={{0,96},{8,104},{16,112},{24,120},{32,0},{40,8},{48,16},{56,24},{64... | collective-permute-start | bytes 2064392 | tf_op jit(solution)/shard_map/ppermute | solution.py:36
  100.6 9.6 %collective-permute-done.18 = bf16[3,64,1792]{2,1,0:T(8,128)(2,1)S(1)} collective-permute-done((bf16[3,64,1792]{2,1,0:T(8,128)(2,1)S(1)}, bf16[3,64,1792]{2,1,0:T(8,128)(2,1)S(1)}, u32[]{:S(2)}, u32[]{:S(2)}) %collective-permute-start.18) | collective-permute-done | bytes 688160 | tf_op jit(solution)/shard_map/ppermute | solution.py:36
  110.5 2.7 %collective-permute-start.20 = (bf16[3,64,640]{2,1,0:T(8,128)(2,1)S(1)}, bf16[3,64,640]{2,1,0:T(8,128)(2,1)S(1)}, u32[]{:S(2)}, u32[]{:S(2)}) collective-permute-start(bf16[3,64,640]{2,1,0:T(8,128)(2,1)S(1)} %slice.113), channel_id=1, source_target_pairs={{0,96},{8,104},{16,112},{24,120},{32,0},{40,8},{48,16},{56,24},{64... | collective-permute-start | bytes 737288 | tf_op jit(solution)/shard_map/ppermute | solution.py:36
  114.4 3.7 %collective-permute-done.16 = bf16[3,64,512]{2,1,0:T(8,128)(2,1)S(1)} collective-permute-done((bf16[3,64,512]{2,1,0:T(8,128)(2,1)S(1)}, bf16[3,64,512]{2,1,0:T(8,128)(2,1)S(1)}, u32[]{:S(2)}, u32[]{:S(2)}) %collective-permute-start.16) | collective-permute-done | bytes 196640 | tf_op jit(solution)/shard_map/ppermute | solution.py:36
  119.1 9.1 %collective-permute-start.22 = (bf16[3,256,1792]{2,1,0:T(8,128)(2,1)S(1)}, bf16[3,256,1792]{2,1,0:T(8,128)(2,1)S(1)}, u32[]{:S(2)}, u32[]{:S(2)}) collective-permute-start(bf16[3,256,1792]{2,1,0:T(8,128)(2,1)S(1)} %maximum_maximum_fusion.refs_0_), channel_id=1, source_target_pairs={{0,8},{8,0},{16,24},{24,16},{32,40},{40,32},{48,56},{56,48},{64,72... | collective-permute-start | bytes 8257544 | tf_op jit(solution)/shard_map/ppermute | solution.py:36
  128.6 4.7 %shard_map.89 = (f32[512,512]{1,0:T(8,128)S(1)}, bf16[512,3584]{1,0:T(8,128)(2,1)}, bf16[512,3584]{1,0:T(8,128)(2,1)}, bf16[3584,512]{1,0:T(8,128)(2,1)}) custom-call(s32[3]{0:T(128)S(1)} %pad_add_fusion.pos, bf16[3,256,1792]{2,1,0:T(8,128)(2,1)S(1)} %maximum_maximum_fusion.refs_0_, bf16[3,192,1792]{2,1,0:T(8,128)(2,1)S(1)} %pad_maximum_fusion.refs_1_, ...), custom_call_target="tpu_custom_call" | custom-call | flops 2348810240 | bytes 8388608 | tf_op jit(solution)/shard_map/pallas_call | solution.py:229
  133.3 4.4 %shard_map.90 = (f32[512,512]{1,0:T(8,128)S(1)}, bf16[512,3584]{1,0:T(8,128)(2,1)}, bf16[512,3584]{1,0:T(8,128)(2,1)}, bf16[3584,512]{1,0:T(8,128)(2,1)}) custom-call(s32[3]{0:T(128)S(1)} %pad_add_fusion.pos, bf16[3,256,1792]{2,1,0:T(8,128)(2,1)S(1)} %maximum_maximum_fusion.refs_0_, ...), custom_call_target="tpu_custom_call", output_to_operand_aliasing={{1}: (9, {}), {2}: (10, {}), {3}: (11, {})} | custom-call | flops 2348810240 | bytes 8388608 | tf_op jit(solution)/shard_map/pallas_call | solution.py:229
  137.7 1.9 %shard_map.91.refs_5_ = f32[512,512]{1,0:T(8,128)S(1)} custom-call(s32[3]{0:T(128)S(1)} %pad_add_fusion.pos, bf16[3,256,1792]{2,1,0:T(8,128)(2,1)S(1)} %collective-permute-done.22.refs_0_, bf16[3,192,1792]{2,1,0:T(8,128)(2,1)S(1)} %collective-permute-done.23.refs_1_, bf16[3,64,1792]{2,1,0:T(8,128)(2,1)S(1)} %collective-permute-done.24.refs_2_, ...), custom_call_target="tpu_custom_call" | custom-call | flops 939524096 | bytes 8388608 | tf_op jit(solution)/shard_map/pallas_call | solution.py:229
  139.6 2.0 %shard_map.92 = bf16[8,64,512]{2,1,0:T(8,128)(2,1)S(1)} custom-call(s32[3]{0:T(128)S(1)} %pad_add_fusion.pos, bf16[3,256,1792]{2,1,0:T(8,128)(2,1)S(1)} %collective-permute-done.22.refs_0_, bf16[3,192,1792]{2,1,0:T(8,128)(2,1)S(1)} %collective-permute-done.23.refs_1_, bf16[3,64,1792]{2,1,0:T(8,128)(2,1)S(1)} %collective-permute-done.24.refs_2_, ...), custom_call_target="tpu_custom_call" | custom-call | flops 939524096 | bytes 8388608 | tf_op jit(solution)/shard_map/pallas_call | solution.py:229
  142.4 4.9 %all-to-all-start.1 = ((bf16[8,64,512]{2,1,0:T(8,128)(2,1)}), bf16[8,64,512]{2,1,0:T(8,128)(2,1)}, u32[]{:S(2)}, u32[]{:S(2)}) async-start(bf16[8,64,512]{2,1,0:T(8,128)(2,1)} %copy-done.9), calls=%async_computation.1 | async-start | bytes 1048576 | tf_op jit(solution)/shard_map/all_to_all | solution.py:357
  148.5 1.6 copy-done.6
  151.1 3.6 %shard_map.93 = (bf16[512,3584]{1,0:T(8,128)(2,1)}, bf16[512,3584]{1,0:T(8,128)(2,1)}, bf16[3584,512]{1,0:T(8,128)(2,1)}) custom-call(s32[3]{0:T(128)S(1)} %pad_add_fusion.pos, bf16[3,256,1792]{2,1,0:T(8,128)(2,1)S(1)} %collective-permute-done.22.refs_0_, ...), custom_call_target="tpu_custom_call", output_to_operand_aliasing={{0}: (6, {}), {1}: (7, {}), {2}: (8, {})} | custom-call | flops 1409286144 | bytes 8388608 | tf_op jit(solution)/shard_map/pallas_call | solution.py:229
  154.8 3.6 %shard_map.94 = (bf16[512,3584]{1,0:T(8,128)(2,1)}, bf16[512,3584]{1,0:T(8,128)(2,1)}, bf16[3584,512]{1,0:T(8,128)(2,1)}) custom-call(s32[3]{0:T(128)S(1)} %pad_add_fusion.pos, bf16[3,256,1792]{2,1,0:T(8,128)(2,1)S(1)} %collective-permute-done.22.refs_0_, ...), custom_call_target="tpu_custom_call", output_to_operand_aliasing={{0}: (6, {}), {1}: (7, {}), {2}: (8, {})} | custom-call | flops 1409286144 | bytes 8388608 | tf_op jit(solution)/shard_map/pallas_call | solution.py:229
  158.4 1.8 %reduce_sum.12 = bf16[64,512]{1,0:T(8,128)(2,1)} reduce(bf16[8,64,512]{2,1,0:T(8,128)(2,1)} %all-to-all-done.1, bf16[]{:T(256)} %constant.54.clone.1), dimensions={0}, to_apply=%region_0.1 | reduce | flops 229376 | bytes 589826 | tf_op jit(solution)/shard_map/reduce_sum | solution.py:357
  (88 shorter events, 21.6 us)
Async XLA Ops:
  3.4 23.8 %all-to-all-start = ((bf16[8,64,1024]{2,1,0:T(8,128)(2,1)}), bf16[8,64,1024]{2,1,0:T(8,128)(2,1)S(1)}, u32[]{:S(2)}, u32[]{:S(2)}) async-start(bf16[8,64,1024]{2,1,0:T(8,128)(2,1)} %shard_map.84), calls=%async_computation | async-start | bytes 2097152 | tf_op jit(solution)/shard_map/all_to_all | solution.py:336
  11.7 4.0 %copy-start.1 = (bf16[512,3584]{1,0:T(8,128)(2,1)S(1)}, bf16[512,3584]{1,0:T(8,128)(2,1)}, u32[]{:S(2)}) copy-start(bf16[512,3584]{1,0:T(8,128)(2,1)} %refs_4_.7) | copy-start | bytes 11010052
  14.7 14.7 %collective-permute-start.1 = (bf16[512,1792]{1,0:T(8,128)(2,1)}, bf16[512,1792]{1,0:T(8,128)(2,1)S(1)}, u32[]{:S(2)}, u32[]{:S(2)}) collective-permute-start(bf16[512,1792]{1,0:T(8,128)(2,1)} %constant_dynamic-slice_fusion.2), channel_id=1, source_target_pairs={{0,8},{8,0},{16,24},{24,16},{32,40},{40,32},{48,56},{56,48},{64,72... | collective-permute-start | bytes 5505032 | tf_op jit(solution)/shard_map/ppermute | solution.py:36
  17.0 12.4 %collective-permute-start.2 = (bf16[512,1792]{1,0:T(8,128)(2,1)}, bf16[512,1792]{1,0:T(8,128)(2,1)}, u32[]{:S(2)}, u32[]{:S(2)}) collective-permute-start(bf16[512,1792]{1,0:T(8,128)(2,1)} %constant_dynamic-slice_fusion.1), channel_id=1, source_target_pairs={{0,8},{8,0},{16,24},{24,16},{32,40},{40,32},{48,56},{56,48},{64,72... | collective-permute-start | bytes 5505032 | tf_op jit(solution)/shard_map/ppermute | solution.py:36
  18.4 11.1 %collective-permute-start.3 = (bf16[1792,512]{1,0:T(8,128)(2,1)}, bf16[1792,512]{1,0:T(8,128)(2,1)}, u32[]{:S(2)}, u32[]{:S(2)}) collective-permute-start(bf16[1792,512]{1,0:T(8,128)(2,1)} %constant_dynamic-slice_fusion), channel_id=1, source_target_pairs={{0,8},{8,0},{16,24},{24,16},{32,40},{40,32},{48,56},{56,48},{64,72... | collective-permute-start | bytes 5505032 | tf_op jit(solution)/shard_map/ppermute | solution.py:36
  28.0 105.3 %copy-start.3 = (bf16[512,1024]{1,0:T(8,128)(2,1)}, bf16[512,1024]{1,0:T(8,128)(2,1)S(1)}, u32[]{:S(2)}) copy-start(bf16[512,1024]{1,0:T(8,128)(2,1)S(1)} %get-tuple-element.36.tg.refs_6_.refs_7_.refs_4_) | copy-start | bytes 3145732
  28.0 105.3 %copy-start.7 = (bf16[512,512]{1,0:T(8,128)(2,1)}, bf16[512,512]{1,0:T(8,128)(2,1)S(1)}, u32[]{:S(2)}) copy-start(bf16[512,512]{1,0:T(8,128)(2,1)S(1)} %get-tuple-element.53.refs_5_.refs_6_.refs_3_) | copy-start | bytes 1572868
  28.0 3.7 %collective-permute-start = (bf16[512,1024]{1,0:T(8,128)(2,1)S(1)}, bf16[512,1024]{1,0:T(8,128)(2,1)S(1)}, u32[]{:S(2)}, u32[]{:S(2)}) collective-permute-start(bf16[512,1024]{1,0:T(8,128)(2,1)S(1)} %get-tuple-element.36.tg.refs_6_.refs_7_.refs_4_), channel_id=1, source_target_pairs={{0,8},{8,0},{16,24},{24,16},{32,40},{40,32},{48,56},{56,48},{64,72... | collective-permute-start | bytes 3145736 | tf_op jit(solution)/shard_map/ppermute | solution.py:36
  39.4 8.4 %collective-permute-start.5 = (bf16[3,64,640]{2,1,0:T(8,128)(2,1)S(1)}, bf16[3,64,640]{2,1,0:T(8,128)(2,1)S(1)}, u32[]{:S(2)}, u32[]{:S(2)}) collective-permute-start(bf16[3,64,640]{2,1,0:T(8,128)(2,1)S(1)} %get-tuple-element.43), channel_id=1, source_target_pairs={{0,32},{8,40},{16,48},{24,56},{32,64},{40,72},{48,80},{56,88},{64,... | collective-permute-start | bytes 737288 | tf_op jit(solution)/shard_map/ppermute | solution.py:36
  40.7 7.2 %collective-permute-start.6 = (bf16[3,64,640]{2,1,0:T(8,128)(2,1)S(1)}, bf16[3,64,640]{2,1,0:T(8,128)(2,1)S(1)}, u32[]{:S(2)}, u32[]{:S(2)}) collective-permute-start(bf16[3,64,640]{2,1,0:T(8,128)(2,1)S(1)} %get-tuple-element.44), channel_id=1, source_target_pairs={{0,96},{8,104},{16,112},{24,120},{32,0},{40,8},{48,16},{56,24},{64... | collective-permute-start | bytes 737288 | tf_op jit(solution)/shard_map/ppermute | solution.py:36
  42.1 5.5 %collective-permute-start.4 = (bf16[3,64,512]{2,1,0:T(8,128)(2,1)S(1)}, bf16[3,64,512]{2,1,0:T(8,128)(2,1)S(1)}, u32[]{:S(2)}, u32[]{:S(2)}) collective-permute-start(bf16[3,64,512]{2,1,0:T(8,128)(2,1)S(1)} %get-tuple-element.42), channel_id=1, source_target_pairs={{0,16},{8,24},{16,0},{24,8},{32,48},{40,56},{48,32},{56,40},{64,80... | collective-permute-start | bytes 589832 | tf_op jit(solution)/shard_map/ppermute | solution.py:36
  48.1 16.6 %collective-permute-start.7 = (bf16[3,64,1792]{2,1,0:T(8,128)(2,1)S(1)}, bf16[3,64,1792]{2,1,0:T(8,128)(2,1)S(1)}, u32[]{:S(2)}, u32[]{:S(2)}) collective-permute-start(bf16[3,64,1792]{2,1,0:T(8,128)(2,1)S(1)} %get-tuple-element.45), channel_id=1, source_target_pairs={{0,32},{8,40},{16,48},{24,56},{32,64},{40,72},{48,80},{56,88},{64,... | collective-permute-start | bytes 2064392 | tf_op jit(solution)/shard_map/ppermute | solution.py:36
  49.1 15.7 %collective-permute-start.8 = (bf16[3,64,1792]{2,1,0:T(8,128)(2,1)S(1)}, bf16[3,64,1792]{2,1,0:T(8,128)(2,1)S(1)}, u32[]{:S(2)}, u32[]{:S(2)}) collective-permute-start(bf16[3,64,1792]{2,1,0:T(8,128)(2,1)S(1)} %get-tuple-element.46), channel_id=1, source_target_pairs={{0,16},{8,24},{16,0},{24,8},{32,48},{40,56},{48,32},{56,40},{64,80... | collective-permute-start | bytes 2064392 | tf_op jit(solution)/shard_map/ppermute | solution.py:36
  49.8 15.1 %collective-permute-start.10 = (bf16[3,64,1792]{2,1,0:T(8,128)(2,1)S(1)}, bf16[3,64,1792]{2,1,0:T(8,128)(2,1)S(1)}, u32[]{:S(2)}, u32[]{:S(2)}) collective-permute-start(bf16[3,64,1792]{2,1,0:T(8,128)(2,1)S(1)} %get-tuple-element.48), channel_id=1, source_target_pairs={{0,96},{8,104},{16,112},{24,120},{32,0},{40,8},{48,16},{56,24},{64... | collective-permute-start | bytes 2064392 | tf_op jit(solution)/shard_map/ppermute | solution.py:36
  65.6 15.4 %collective-permute-start.9 = (bf16[3,64,1792]{2,1,0:T(8,128)(2,1)S(1)}, bf16[3,64,1792]{2,1,0:T(8,128)(2,1)S(1)}, u32[]{:S(2)}, u32[]{:S(2)}) collective-permute-start(bf16[3,64,1792]{2,1,0:T(8,128)(2,1)S(1)} %pad_maximum_fusion.4), channel_id=1, source_target_pairs={{0,32},{8,40},{16,48},{24,56},{32,64},{40,72},{48,80},{56,88},{64,... | collective-permute-start | bytes 2064392 | tf_op jit(solution)/shard_map/ppermute | solution.py:36
  66.4 14.6 %collective-permute-start.11 = (bf16[3,64,1792]{2,1,0:T(8,128)(2,1)S(1)}, bf16[3,64,1792]{2,1,0:T(8,128)(2,1)S(1)}, u32[]{:S(2)}, u32[]{:S(2)}) collective-permute-start(bf16[3,64,1792]{2,1,0:T(8,128)(2,1)S(1)} %pad_maximum_fusion.5), channel_id=1, source_target_pairs={{0,96},{8,104},{16,112},{24,120},{32,0},{40,8},{48,16},{56,24},{64... | collective-permute-start | bytes 2064392 | tf_op jit(solution)/shard_map/ppermute | solution.py:36
  68.6 13.6 %collective-permute-start.12 = (bf16[3,64,1792]{2,1,0:T(8,128)(2,1)S(1)}, bf16[3,64,1792]{2,1,0:T(8,128)(2,1)S(1)}, u32[]{:S(2)}, u32[]{:S(2)}) collective-permute-start(bf16[3,64,1792]{2,1,0:T(8,128)(2,1)S(1)} %pad_maximum_fusion.6), channel_id=1, source_target_pairs={{0,16},{8,24},{16,0},{24,8},{32,48},{40,56},{48,32},{56,40},{64,80... | collective-permute-start | bytes 2064392 | tf_op jit(solution)/shard_map/ppermute | solution.py:36
  82.8 13.6 %collective-permute-start.13 = (bf16[3,64,1792]{2,1,0:T(8,128)(2,1)S(1)}, bf16[3,64,1792]{2,1,0:T(8,128)(2,1)S(1)}, u32[]{:S(2)}, u32[]{:S(2)}) collective-permute-start(bf16[3,64,1792]{2,1,0:T(8,128)(2,1)S(1)} %pad_maximum_fusion.7), channel_id=1, source_target_pairs={{0,32},{8,40},{16,48},{24,56},{32,64},{40,72},{48,80},{56,88},{64,... | collective-permute-start | bytes 2064392 | tf_op jit(solution)/shard_map/ppermute | solution.py:36
  82.9 13.5 %collective-permute-start.14 = (bf16[3,64,1792]{2,1,0:T(8,128)(2,1)S(1)}, bf16[3,64,1792]{2,1,0:T(8,128)(2,1)S(1)}, u32[]{:S(2)}, u32[]{:S(2)}) collective-permute-start(bf16[3,64,1792]{2,1,0:T(8,128)(2,1)S(1)} %pad_maximum_fusion.7), channel_id=1, source_target_pairs={{0,16},{8,24},{16,0},{24,8},{32,48},{40,56},{48,32},{56,40},{64,80... | collective-permute-start | bytes 2064392 | tf_op jit(solution)/shard_map/ppermute | solution.py:36
  83.8 12.8 %collective-permute-start.17 = (bf16[3,64,1792]{2,1,0:T(8,128)(2,1)S(1)}, bf16[3,64,1792]{2,1,0:T(8,128)(2,1)S(1)}, u32[]{:S(2)}, u32[]{:S(2)}) collective-permute-start(bf16[3,64,1792]{2,1,0:T(8,128)(2,1)S(1)} %pad_maximum_fusion.7), channel_id=1, source_target_pairs={{0,96},{8,104},{16,112},{24,120},{32,0},{40,8},{48,16},{56,24},{64... | collective-permute-start | bytes 2064392 | tf_op jit(solution)/shard_map/ppermute | solution.py:36
  96.7 13.5 %collective-permute-start.18 = (bf16[3,64,1792]{2,1,0:T(8,128)(2,1)S(1)}, bf16[3,64,1792]{2,1,0:T(8,128)(2,1)S(1)}, u32[]{:S(2)}, u32[]{:S(2)}) collective-permute-start(bf16[3,64,1792]{2,1,0:T(8,128)(2,1)S(1)} %get-tuple-element.78), channel_id=1, source_target_pairs={{0,16},{8,24},{16,0},{24,8},{32,48},{40,56},{48,32},{56,40},{64,80... | collective-permute-start | bytes 2064392 | tf_op jit(solution)/shard_map/ppermute | solution.py:36
  97.7 12.6 %collective-permute-start.15 = (bf16[3,64,1792]{2,1,0:T(8,128)(2,1)S(1)}, bf16[3,64,1792]{2,1,0:T(8,128)(2,1)S(1)}, u32[]{:S(2)}, u32[]{:S(2)}) collective-permute-start(bf16[3,64,1792]{2,1,0:T(8,128)(2,1)S(1)} %get-tuple-element.79), channel_id=1, source_target_pairs={{0,32},{8,40},{16,48},{24,56},{32,64},{40,72},{48,80},{56,88},{64,... | collective-permute-start | bytes 2064392 | tf_op jit(solution)/shard_map/ppermute | solution.py:36
  97.7 16.5 %collective-permute-start.21 = (bf16[3,64,1792]{2,1,0:T(8,128)(2,1)S(1)}, bf16[3,64,1792]{2,1,0:T(8,128)(2,1)S(1)}, u32[]{:S(2)}, u32[]{:S(2)}) collective-permute-start(bf16[3,64,1792]{2,1,0:T(8,128)(2,1)S(1)} %get-tuple-element.77), channel_id=1, source_target_pairs={{0,96},{8,104},{16,112},{24,120},{32,0},{40,8},{48,16},{56,24},{64... | collective-permute-start | bytes 2064392 | tf_op jit(solution)/shard_map/ppermute | solution.py:36
  110.2 18.4 %copy-start.2 = (bf16[512,3584]{1,0:T(8,128)(2,1)S(1)}, bf16[512,3584]{1,0:T(8,128)(2,1)}, u32[]{:S(2)}) copy-start(bf16[512,3584]{1,0:T(8,128)(2,1)} %refs_4_.7) | copy-start | bytes 11010052
  110.3 8.4 %collective-permute-start.19 = (bf16[3,64,640]{2,1,0:T(8,128)(2,1)S(1)}, bf16[3,64,640]{2,1,0:T(8,128)(2,1)S(1)}, u32[]{:S(2)}, u32[]{:S(2)}) collective-permute-start(bf16[3,64,640]{2,1,0:T(8,128)(2,1)S(1)} %pad_maximum_fusion.9), channel_id=1, source_target_pairs={{0,32},{8,40},{16,48},{24,56},{32,64},{40,72},{48,80},{56,88},{64,... | collective-permute-start | bytes 737288 | tf_op jit(solution)/shard_map/ppermute | solution.py:36
  110.5 8.5 %collective-permute-start.20 = (bf16[3,64,640]{2,1,0:T(8,128)(2,1)S(1)}, bf16[3,64,640]{2,1,0:T(8,128)(2,1)S(1)}, u32[]{:S(2)}, u32[]{:S(2)}) collective-permute-start(bf16[3,64,640]{2,1,0:T(8,128)(2,1)S(1)} %slice.113), channel_id=1, source_target_pairs={{0,96},{8,104},{16,112},{24,120},{32,0},{40,8},{48,16},{56,24},{64... | collective-permute-start | bytes 737288 | tf_op jit(solution)/shard_map/ppermute | solution.py:36
  113.2 15.5 %copy-start = (bf16[512,3584]{1,0:T(8,128)(2,1)S(1)}, bf16[512,3584]{1,0:T(8,128)(2,1)}, u32[]{:S(2)}) copy-start(bf16[512,3584]{1,0:T(8,128)(2,1)} %refs_3_.7) | copy-start | bytes 11010052
  113.2 4.9 %collective-permute-start.16 = (bf16[3,64,512]{2,1,0:T(8,128)(2,1)S(1)}, bf16[3,64,512]{2,1,0:T(8,128)(2,1)S(1)}, u32[]{:S(2)}, u32[]{:S(2)}) collective-permute-start(bf16[3,64,512]{2,1,0:T(8,128)(2,1)S(1)} %slice.109), channel_id=1, source_target_pairs={{0,16},{8,24},{16,0},{24,8},{32,48},{40,56},{48,32},{56,40},{64,80... | collective-permute-start | bytes 589832 | tf_op jit(solution)/shard_map/ppermute | solution.py:36
  119.1 18.6 %collective-permute-start.22 = (bf16[3,256,1792]{2,1,0:T(8,128)(2,1)S(1)}, bf16[3,256,1792]{2,1,0:T(8,128)(2,1)S(1)}, u32[]{:S(2)}, u32[]{:S(2)}) collective-permute-start(bf16[3,256,1792]{2,1,0:T(8,128)(2,1)S(1)} %maximum_maximum_fusion.refs_0_), channel_id=1, source_target_pairs={{0,8},{8,0},{16,24},{24,16},{32,40},{40,32},{48,56},{56,48},{64,72... | collective-permute-start | bytes 8257544 | tf_op jit(solution)/shard_map/ppermute | solution.py:36
  128.1 9.6 %collective-permute-start.23 = (bf16[3,192,1792]{2,1,0:T(8,128)(2,1)S(1)}, bf16[3,192,1792]{2,1,0:T(8,128)(2,1)S(1)}, u32[]{:S(2)}, u32[]{:S(2)}) collective-permute-start(bf16[3,192,1792]{2,1,0:T(8,128)(2,1)S(1)} %pad_maximum_fusion.refs_1_), channel_id=1, source_target_pairs={{0,8},{8,0},{16,24},{24,16},{32,40},{40,32},{48,56},{56,48},{64,72... | collective-permute-start | bytes 6193160 | tf_op jit(solution)/shard_map/ppermute | solution.py:36
  128.2 9.5 %collective-permute-start.24 = (bf16[3,64,1792]{2,1,0:T(8,128)(2,1)S(1)}, bf16[3,64,1792]{2,1,0:T(8,128)(2,1)S(1)}, u32[]{:S(2)}, u32[]{:S(2)}) collective-permute-start(bf16[3,64,1792]{2,1,0:T(8,128)(2,1)S(1)} %pad_maximum_fusion.8.refs_2_), channel_id=1, source_target_pairs={{0,8},{8,0},{16,24},{24,16},{32,40},{40,32},{48,56},{56,48},{64,72... | collective-permute-start | bytes 2064392 | tf_op jit(solution)/shard_map/ppermute | solution.py:36
  142.4 16.0 %all-to-all-start.1 = ((bf16[8,64,512]{2,1,0:T(8,128)(2,1)}), bf16[8,64,512]{2,1,0:T(8,128)(2,1)}, u32[]{:S(2)}, u32[]{:S(2)}) async-start(bf16[8,64,512]{2,1,0:T(8,128)(2,1)} %copy-done.9), calls=%async_computation.1 | async-start | bytes 1048576 | tf_op jit(solution)/shard_map/all_to_all | solution.py:357
  (8 other events, 10.6 us)

commit v3 on v2

--- a/solution.py
+++ b/solution.py
@@ -64,7 +64,7 @@
     return pl.pallas_call(
         spread_kernel,
         out_shape=jax.ShapeDtypeStruct((8, BLK, 1024), BF),
-        compiler_params=pltpu.CompilerParams(vmem_limit_bytes=16 << 20),
+        compiler_params=pltpu.CompilerParams(vmem_limit_bytes=58 << 20),
         cost_estimate=pl.CostEstimate(flops=0, bytes_accessed=1 << 20, transcendentals=0),
     )(tokens, out_grad)
 
@@ -151,12 +151,31 @@
     )(pos, tg, tg_sib, *weights, *weights_sib)
 
 
-def stack(half, grads, near, mids, far):
+PIECES = [pl.BlockSpec(memory_space=pl.ANY)] * 3
+COPIES = 5
+
+
+def stack(half, grads, near, mids, far, sems):
+    arrays = pl.ds(0, grads.shape[0])
+    columns = pl.ds(half * MID, MID)
     up, down, flat = 0, 1, 2
-    grads[:, :BLK] = far[...]
-    grads[:, 4 * BLK :] = near[...]
+    ways = [(far, 0, 0, BLK), (near, 0, 4 * BLK, 4 * BLK)]
     for i, piece in enumerate((down, flat, up) if half else (up, down, flat)):
-        grads[:, (i + 1) * BLK : (i + 2) * BLK] = mids[:, piece * BLK : (piece + 1) * BLK]
+        ways.append((mids, piece * BLK, (i + 1) * BLK, BLK))
+    copies = [
+        pltpu.make_async_copy(
+            source.at[arrays, pl.ds(at, size), columns], grads.at[:, pl.ds(to, size), :], sems.at[k]
+        )
+        for k, (source, at, to, size) in enumerate(ways)
+    ]
+    for copy in copies:
+        copy.start()
+    return copies
+
+
+def wait(copies):
+    for copy in copies:
+        copy.wait()
 
 
 def part_kernel(half, has_terms, has_weights, carried, last, pos, *refs):
@@ -165,9 +184,9 @@
     gw, uw = (refs.pop(0) for _ in range(2)) if has_terms else (None, None)
     before = refs.pop(0) if has_terms and carried else None
     tok_t, tg = (refs.pop(0) for _ in range(2)) if has_weights else (None, None)
-    grads = refs.pop()
+    sems, grads = refs.pop(), refs.pop()
     acc = refs.pop() if has_terms else None
-    stack(half, grads, near, mids, far)
+    wait(stack(half, grads, near, mids, far, sems))
     if has_weights:
         ggw, guw, gdw = refs[-3:]
         ggw[...] = dot(tok_t[...], grads[0], 1, 0).astype(BF)
@@ -192,9 +211,7 @@
     column = pl.BlockSpec((512, MID), lambda i, pos: (0, tile(pos)))
     row = pl.BlockSpec((MID, 512), lambda i, pos: (tile(pos), 0))
     square = whole((512, 512))
-    in_specs = [
-        pl.BlockSpec((arrays, r, MID), lambda i, pos: (0, 0, half)) for r in (256, 192, 64)
-    ]
+    in_specs = [*PIECES]
     args, out_specs, out_shape, scratch, aliases = [*pieces], [], [], [], {}
     carried = False
     if terms:
@@ -224,7 +241,7 @@
         out_specs += [column, column, row]
         out_shape += [jax.ShapeDtypeStruct((512, 2 * HALF), BF)] * 2
         out_shape += [jax.ShapeDtypeStruct((2 * HALF, 512), BF)]
-    scratch.append(pltpu.VMEM((arrays, 512, MID), BF))
+    scratch += [pltpu.VMEM((arrays, 512, MID), BF), pltpu.SemaphoreType.DMA((COPIES,))]
     flops = 2 * 512 * 512 * MID * (2 * bool(terms) + 3 * bool(weights))
     return pl.pallas_call(
         functools.partial(part_kernel, half, bool(terms), bool(weights), carried, last),
@@ -237,9 +254,25 @@
         ),
         out_shape=out_shape,
         input_output_aliases=aliases,
-        compiler_params=params(32),
+        compiler_params=params(32 if terms else 48),
         cost_estimate=pl.CostEstimate(flops=flops, bytes_accessed=8 << 20, transcendentals=0),
     )(pos, *args)
+
+
+def total_kernel(terms, out):
+    total = wide(terms[0])
+    for b in range(1, 8):
+        total += wide(terms[b])
+    out[...] = total.astype(BF)
+
+
+def total_of(terms):
+    return pl.pallas_call(
+        total_kernel,
+        out_shape=jax.ShapeDtypeStruct((BLK, 512), BF),
+        compiler_params=pltpu.CompilerParams(vmem_limit_bytes=8 << 20),
+        cost_estimate=pl.CostEstimate(flops=1 << 18, bytes_accessed=1 << 19, transcendentals=0),
+    )(terms)
 
 
 def wide(a):
@@ -309,9 +342,10 @@
     rp = send(join(lo(g30), hi(g01)), XP)
     rm = send(join(lo(g01), hi(g10)), XM)
     rz = send(join(lo(g30), hi(g10)), ZS)
+    rp, rm, rz, near = after(rp, rm, rz, rows(g10, g30, g01, e))
     turn_up = join(rz[..., z:MID], rp[..., MID:x])
     fz, fp, fm = send(rp[..., :z], ZS), send(turn_up, XP), send(rz[..., x:], XM)
-    far, near, mids = after(join(fz, fp, fm), rows(g10, g30, g01, e), rows(rp, rm, rz))
+    far, mids = after(join(fz, fp, fm), rows(rp, rm, rz))
     pieces = near, mids, far
     return pieces, [send(piece, CORE) for piece in pieces]
 
@@ -354,7 +388,7 @@
     terms, *grads = part(pos, own, 0, 1, (gw, uw, terms), (tok_t, tg, grads))
     (terms,) = part(pos, sib, 1, 0, (gw, uw, terms))
     (terms,) = part(pos, sib, 1, 1, (gw, uw, terms), None, True)
-    grad_tokens = jnp.sum(wide(lax.all_to_all(terms, "gy", 0, 0, tiled=True)), axis=0).astype(BF)
+    grad_tokens = total_of(lax.all_to_all(terms, "gy", 0, 0, tiled=True))
     grads = part(pos, sib, 1, 0, None, (tok_t, tg, grads))
     ggw, guw, gdw = part(pos, sib, 1, 1, None, (tok_t, tg, grads))
     return grad_tokens, ggw, guw, gdw

time: 161 us -> 160 us (level)
  Pallas kernels: 37 us -> 40.6 us
  local copies, waits for them, and re-layouts: 12.3 us -> 9.85 us
  other arithmetic: 4.02 us -> 2.14 us
    unnamed x26 -> x22, local copies, waits for them, and re-layouts: 6.33 us -> 3.88 us
    pallas_call x6, Pallas kernels: 20.2 us -> 22.4 us  [part(): pl.pallas_call(functools.partial(part_kernel, half, bool(terms), bool(wei...]
    reduce_sum x1 -> x0, other arithmetic: 1.76 us -> none  [shards(): jnp.sum(wide(lax.all_to_all(terms, 'gy', 0, 0, tiled=True)), axis=0)]
  transfers between devices with their start and end apart: 27 -> 27, of which waited for: 12 -> 12; matrix products, arithmetic and copies ran while one was open for 4% -> 4% of each run, Pallas kernels for 15% -> 16%
where the time goes in v3:
time: 160 us; the launch traced here: 159 us
  waiting for transfers between devices  58.5 us (37%)
  starting transfers between devices  47 us (29%)
  Pallas kernels  40.6 us (25%)
  local copies, waits for them, and re-layouts  9.85 us (6%)
  other arithmetic  2.14 us (1%)
    ppermute x25, waiting for transfers between devices, send(): return lax.ppermute(a, 'gx', pairs)  51.1 us
    ppermute x25, starting transfers between devices, send(): return lax.ppermute(a, 'gx', pairs)  34.3 us
    pallas_call x6, Pallas kernels, part(): pl.pallas_call(functools.partial(part_kernel, half, bool(terms), bool(wei...  22.4 us
    pallas_call x2, Pallas kernels, sums(): pl.pallas_call(functools.partial(sums_kernel, part), grid_spec=pltpu.Pref...  14.5 us
    all_to_all x1, starting transfers between devices, shards(): blocks = lax.all_to_all(spread(tokens, out_grad), 'gy', 0, 0, tiled=True)  8.33 us
    all_to_all x1, waiting for transfers between devices, shards(): blocks = lax.all_to_all(spread(tokens, out_grad), 'gy', 0, 0, tiled=True)  7.4 us
    dynamic_slice x3, local copies, waits for them, and re-layouts, shards(): lax.dynamic_slice_in_dim(w, far_half, HALF, axis)  5.69 us
    all_to_all x1, starting transfers between devices, shards(): grad_tokens = total_of(lax.all_to_all(terms, 'gy', 0, 0, tiled=True))  4.43 us
  transfers between devices with their start and end apart: 27, of which 12 were waited for; matrix products, arithmetic and copies ran while one was open for 4% of the time, Pallas kernels for 16%

profile of v3, /device:TPU:1, one launch (start us, length us, event | category | flops | bytes accessed | tf_op | source)
XLA Modules:
  0.0 159.2 jit_solution(94714962268164601)
XLA Ops:
  0.6 1.9 %shard_map.84 = bf16[8,64,1024]{2,1,0:T(8,128)(2,1)} custom-call(bf16[64,512]{1,0:T(8,128)(2,1)} %tokens.1, bf16[64,512]{1,0:T(8,128)(2,1)} %out_grad.1), custom_call_target="tpu_custom_call" | custom-call | bytes 1048576 | tf_op jit(solution)/shard_map/pallas_call | solution.py:64
  2.6 8.3 %all-to-all-start = ((bf16[8,64,1024]{2,1,0:T(8,128)(2,1)}), bf16[8,64,1024]{2,1,0:T(8,128)(2,1)S(1)}, u32[]{:S(2)}, u32[]{:S(2)}) async-start(bf16[8,64,1024]{2,1,0:T(8,128)(2,1)} %shard_map.84), calls=%async_computation | async-start | bytes 2097152 | tf_op jit(solution)/shard_map/all_to_all | solution.py:370
  10.9 3.0 %constant_dynamic-slice_fusion.2 = bf16[512,1792]{1,0:T(8,128)(2,1)} fusion(bf16[512,3584]{1,0:T(8,128)(2,1)} %refs_3_.7, s32[]{:T(128)S(6)} %select_n.27), kind=kLoop, calls=%fused_computation.31 | loop fusion | bytes 3670020 | tf_op jit(solution)/shard_map/dynamic_slice | solution.py:373
  14.9 1.3 constant_dynamic-slice_fusion.1
  16.2 1.3 constant_dynamic-slice_fusion
  17.6 1.3 collective-permute-start.3
  19.0 7.4 %all-to-all-done.blocks = bf16[8,64,1024]{2,1,0:T(8,128)(2,1)S(1)} async-done(((bf16[8,64,1024]{2,1,0:T(8,128)(2,1)}), bf16[8,64,1024]{2,1,0:T(8,128)(2,1)S(1)}, u32[]{:S(2)}, u32[]{:S(2)}) %all-to-all-start) | async-done | bytes 1048608 | tf_op jit(solution)/shard_map/all_to_all | solution.py:370
  27.2 1.4 collective-permute-start
  28.6 2.3 %collective-permute-done.tg_sib = bf16[512,1024]{1,0:T(8,128)(2,1)S(1)} collective-permute-done((bf16[512,1024]{1,0:T(8,128)(2,1)S(1)}, bf16[512,1024]{1,0:T(8,128)(2,1)S(1)}, u32[]{:S(2)}, u32[]{:S(2)}) %collective-permute-start) | collective-permute-done | bytes 1048608 | tf_op jit(solution)/shard_map/ppermute | solution.py:36
  30.9 7.6 %shard_map.87 = (f32[3,64,1792]{2,1,0:T(8,128)S(1)}, f32[3,64,1792]{2,1,0:T(8,128)S(1)}, f32[3,64,1792]{2,1,0:T(8,128)S(1)}, bf16[3,64,512]{2,1,0:T(8,128)(2,1)S...) custom-call(s32[3]{0:T(128)S(1)} %pad_add_fusion.pos, ...), custom_call_target="tpu_custom_call" | custom-call | flops 2818572288 | bytes 20971520 | tf_op jit(solution)/shard_map/pallas_call | solution.py:127
  39.8 1.5 collective-permute-start.6
  42.1 4.7 %collective-permute-done.4.rz = bf16[3,64,512]{2,1,0:T(8,128)(2,1)S(1)} collective-permute-done((bf16[3,64,512]{2,1,0:T(8,128)(2,1)S(1)}, bf16[3,64,512]{2,1,0:T(8,128)(2,1)S(1)}, u32[]{:S(2)}, u32[]{:S(2)}) %collective-permute-start.4) | collective-permute-done | bytes 196640 | tf_op jit(solution)/shard_map/ppermute | solution.py:36
  49.0 1.8 %collective-permute-start.10 = (bf16[3,64,1792]{2,1,0:T(8,128)(2,1)S(1)}, bf16[3,64,1792]{2,1,0:T(8,128)(2,1)S(1)}, u32[]{:S(2)}, u32[]{:S(2)}) collective-permute-start(bf16[3,64,1792]{2,1,0:T(8,128)(2,1)S(1)} %get-tuple-element.51), channel_id=1, source_target_pairs={{0,96},{8,104},{16,112},{24,120},{32,0},{40,8},{48,16},{56,24},{64... | collective-permute-start | bytes 2064392 | tf_op jit(solution)/shard_map/ppermute | solution.py:36
  50.8 6.9 %shard_map.86 = (f32[3,64,1792]{2,1,0:T(8,128)S(1)}, f32[3,64,1792]{2,1,0:T(8,128)S(1)}, f32[3,64,1792]{2,1,0:T(8,128)S(1)}, f32[3,64,1792]{2,1,0:T(8,128)S(1)}) custom-call(s32[3]{0:T(128)S(1)} %pad_add_fusion.pos, bf16[512,1024]{1,0:T(8,128)(2,1)S(1)} %get-tuple-element.39.tg.refs_6_.refs_7_.refs_4_, bf16[512,1024]{1,0:T(8,128)(2,1)S(1)} %collective-permute-done.tg_sib, ...), custom_call_target="tpu_custom_call" | custom-call | flops 2818572288 | bytes 20971520 | tf_op jit(solution)/shard_map/pallas_call | solution.py:127
  57.8 6.1 %collective-permute-done.7 = bf16[3,64,1792]{2,1,0:T(8,128)(2,1)S(1)} collective-permute-done((bf16[3,64,1792]{2,1,0:T(8,128)(2,1)S(1)}, bf16[3,64,1792]{2,1,0:T(8,128)(2,1)S(1)}, u32[]{:S(2)}, u32[]{:S(2)}) %collective-permute-start.7) | collective-permute-done | bytes 688160 | tf_op jit(solution)/shard_map/ppermute | solution.py:36
  65.5 2.1 %collective-permute-start.11 = (bf16[3,64,1792]{2,1,0:T(8,128)(2,1)S(1)}, bf16[3,64,1792]{2,1,0:T(8,128)(2,1)S(1)}, u32[]{:S(2)}, u32[]{:S(2)}) collective-permute-start(bf16[3,64,1792]{2,1,0:T(8,128)(2,1)S(1)} %pad_maximum_fusion.5), channel_id=1, source_target_pairs={{0,96},{8,104},{16,112},{24,120},{32,0},{40,8},{48,16},{56,24},{64... | collective-permute-start | bytes 2064392 | tf_op jit(solution)/shard_map/ppermute | solution.py:36
  68.4 11.7 %collective-permute-done.9 = bf16[3,64,1792]{2,1,0:T(8,128)(2,1)S(1)} collective-permute-done((bf16[3,64,1792]{2,1,0:T(8,128)(2,1)S(1)}, bf16[3,64,1792]{2,1,0:T(8,128)(2,1)S(1)}, u32[]{:S(2)}, u32[]{:S(2)}) %collective-permute-start.9) | collective-permute-done | bytes 688160 | tf_op jit(solution)/shard_map/ppermute | solution.py:36
  82.8 2.6 %collective-permute-start.16 = (bf16[3,64,1792]{2,1,0:T(8,128)(2,1)S(1)}, bf16[3,64,1792]{2,1,0:T(8,128)(2,1)S(1)}, u32[]{:S(2)}, u32[]{:S(2)}) collective-permute-start(bf16[3,64,1792]{2,1,0:T(8,128)(2,1)S(1)} %pad_maximum_fusion.7), channel_id=1, source_target_pairs={{0,96},{8,104},{16,112},{24,120},{32,0},{40,8},{48,16},{56,24},{64... | collective-permute-start | bytes 2064392 | tf_op jit(solution)/shard_map/ppermute | solution.py:36
  85.4 10.0 %collective-permute-done.13 = bf16[3,64,1792]{2,1,0:T(8,128)(2,1)S(1)} collective-permute-done((bf16[3,64,1792]{2,1,0:T(8,128)(2,1)S(1)}, bf16[3,64,1792]{2,1,0:T(8,128)(2,1)S(1)}, u32[]{:S(2)}, u32[]{:S(2)}) %collective-permute-start.13) | collective-permute-done | bytes 688160 | tf_op jit(solution)/shard_map/ppermute | solution.py:36
  95.8 2.9 %collective-permute-start.17 = (bf16[3,64,1792]{2,1,0:T(8,128)(2,1)S(1)}, bf16[3,64,1792]{2,1,0:T(8,128)(2,1)S(1)}, u32[]{:S(2)}, u32[]{:S(2)}) collective-permute-start(bf16[3,64,1792]{2,1,0:T(8,128)(2,1)S(1)} %get-tuple-element.84), channel_id=1, source_target_pairs={{0,96},{8,104},{16,112},{24,120},{32,0},{40,8},{48,16},{56,24},{64... | collective-permute-start | bytes 2064392 | tf_op jit(solution)/shard_map/ppermute | solution.py:36
  99.6 8.8 %collective-permute-done.15 = bf16[3,64,1792]{2,1,0:T(8,128)(2,1)S(1)} collective-permute-done((bf16[3,64,1792]{2,1,0:T(8,128)(2,1)S(1)}, bf16[3,64,1792]{2,1,0:T(8,128)(2,1)S(1)}, u32[]{:S(2)}, u32[]{:S(2)}) %collective-permute-start.15) | collective-permute-done | bytes 688160 | tf_op jit(solution)/shard_map/ppermute | solution.py:36
  109.3 8.0 %collective-permute-start.19 = (bf16[3,256,1792]{2,1,0:T(8,128)(2,1)S(1)}, bf16[3,256,1792]{2,1,0:T(8,128)(2,1)S(1)}, u32[]{:S(2)}, u32[]{:S(2)}) collective-permute-start(bf16[3,256,1792]{2,1,0:T(8,128)(2,1)S(1)} %maximum_maximum_fusion.refs_0_), channel_id=1, source_target_pairs={{0,8},{8,0},{16,24},{24,16},{32,40},{40,32},{48,56},{56,48},{64,72... | collective-permute-start | bytes 8257544 | tf_op jit(solution)/shard_map/ppermute | solution.py:36
  117.5 2.7 %collective-permute-start.22 = (bf16[3,64,640]{2,1,0:T(8,128)(2,1)S(1)}, bf16[3,64,640]{2,1,0:T(8,128)(2,1)S(1)}, u32[]{:S(2)}, u32[]{:S(2)}) collective-permute-start(bf16[3,64,640]{2,1,0:T(8,128)(2,1)S(1)} %slice.95), channel_id=1, source_target_pairs={{0,96},{8,104},{16,112},{24,120},{32,0},{40,8},{48,16},{56,24},{64... | collective-permute-start | bytes 737288 | tf_op jit(solution)/shard_map/ppermute | solution.py:36
  121.1 5.0 %collective-permute-done.20 = bf16[3,64,512]{2,1,0:T(8,128)(2,1)S(1)} collective-permute-done((bf16[3,64,512]{2,1,0:T(8,128)(2,1)S(1)}, bf16[3,64,512]{2,1,0:T(8,128)(2,1)S(1)}, u32[]{:S(2)}, u32[]{:S(2)}) %collective-permute-start.20) | collective-permute-done | bytes 196640 | tf_op jit(solution)/shard_map/ppermute | solution.py:36
  127.8 3.8 %shard_map.89 = (f32[512,512]{1,0:T(8,128)S(1)}, bf16[512,3584]{1,0:T(8,128)(2,1)}, bf16[512,3584]{1,0:T(8,128)(2,1)}, bf16[3584,512]{1,0:T(8,128)(2,1)}) custom-call(s32[3]{0:T(128)S(1)} %pad_add_fusion.pos, bf16[3,256,1792]{2,1,0:T(8,128)(2,1)S(1)} %maximum_maximum_fusion.refs_0_, bf16[3,192,1792]{2,1,0:T(8,128)(2,1)S(1)} %pad_maximum_fusion.refs_1_, ...), custom_call_target="tpu_custom_call" | custom-call | flops 2348810240 | bytes 8388608 | tf_op jit(solution)/shard_map/pallas_call | solution.py:246
  131.6 3.8 %shard_map.90 = (f32[512,512]{1,0:T(8,128)S(1)}, bf16[512,3584]{1,0:T(8,128)(2,1)}, bf16[512,3584]{1,0:T(8,128)(2,1)}, bf16[3584,512]{1,0:T(8,128)(2,1)}) custom-call(s32[3]{0:T(128)S(1)} %pad_add_fusion.pos, bf16[3,256,1792]{2,1,0:T(8,128)(2,1)S(1)} %maximum_maximum_fusion.refs_0_, ...), custom_call_target="tpu_custom_call", output_to_operand_aliasing={{1}: (9, {}), {2}: (10, {}), {3}: (11, {})} | custom-call | flops 2348810240 | bytes 8388608 | tf_op jit(solution)/shard_map/pallas_call | solution.py:246
  135.4 2.2 %shard_map.91.refs_5_ = f32[512,512]{1,0:T(8,128)S(1)} custom-call(s32[3]{0:T(128)S(1)} %pad_add_fusion.pos, bf16[3,256,1792]{2,1,0:T(8,128)(2,1)S(1)} %collective-permute-done.19.refs_0_, bf16[3,192,1792]{2,1,0:T(8,128)(2,1)S(1)} %collective-permute-done.23.refs_1_, bf16[3,64,1792]{2,1,0:T(8,128)(2,1)S(1)} %collective-permute-done.24.refs_2_, ...), custom_call_target="tpu_custom_call" | custom-call | flops 939524096 | bytes 8388608 | tf_op jit(solution)/shard_map/pallas_call | solution.py:246
  137.7 3.1 %shard_map.92 = bf16[8,64,512]{2,1,0:T(8,128)(2,1)} custom-call(s32[3]{0:T(128)S(1)} %pad_add_fusion.pos, bf16[3,256,1792]{2,1,0:T(8,128)(2,1)S(1)} %collective-permute-done.19.refs_0_, bf16[3,192,1792]{2,1,0:T(8,128)(2,1)S(1)} %collective-permute-done.23.refs_1_, bf16[3,64,1792]{2,1,0:T(8,128)(2,1)S(1)} %collective-permute-done.24.refs_2_, ...), custom_call_target="tpu_custom_call" | custom-call | flops 939524096 | bytes 8388608 | tf_op jit(solution)/shard_map/pallas_call | solution.py:246
  140.7 4.4 %all-to-all-start.1 = ((bf16[8,64,512]{2,1,0:T(8,128)(2,1)}), bf16[8,64,512]{2,1,0:T(8,128)(2,1)S(1)}, u32[]{:S(2)}, u32[]{:S(2)}) async-start(bf16[8,64,512]{2,1,0:T(8,128)(2,1)} %shard_map.92), calls=%async_computation.1 | async-start | bytes 1048576 | tf_op jit(solution)/shard_map/all_to_all | solution.py:391
  146.4 1.6 copy-done.7
  149.0 4.8 %shard_map.94 = (bf16[512,3584]{1,0:T(8,128)(2,1)}, bf16[512,3584]{1,0:T(8,128)(2,1)}, bf16[3584,512]{1,0:T(8,128)(2,1)}) custom-call(s32[3]{0:T(128)S(1)} %pad_add_fusion.pos, bf16[3,256,1792]{2,1,0:T(8,128)(2,1)} %copy-done.3, bf16[3,192,1792]{2,1,0:T(8,128)(2,1)S(1)} %copy-done.7, ...), custom_call_target="tpu_custom_call", output_to_operand_aliasing={{0}: (6, {}), {1}: (7, {}), {2}: (8, {})} | custom-call | flops 1409286144 | bytes 8388608 | tf_op jit(solution)/shard_map/pallas_call | solution.py:246
  153.8 4.8 %shard_map.95 = (bf16[512,3584]{1,0:T(8,128)(2,1)}, bf16[512,3584]{1,0:T(8,128)(2,1)}, bf16[3584,512]{1,0:T(8,128)(2,1)}) custom-call(s32[3]{0:T(128)S(1)} %pad_add_fusion.pos, bf16[3,256,1792]{2,1,0:T(8,128)(2,1)} %copy-done.3, bf16[3,192,1792]{2,1,0:T(8,128)(2,1)S(1)} %copy-done.7, ...), custom_call_target="tpu_custom_call", output_to_operand_aliasing={{0}: (6, {}), {1}: (7, {}), {2}: (8, {})} | custom-call | flops 1409286144 | bytes 8388608 | tf_op jit(solution)/shard_map/pallas_call | solution.py:246
  (84 shorter events, 19.1 us)
Async XLA Ops:
  2.6 23.8 %all-to-all-start = ((bf16[8,64,1024]{2,1,0:T(8,128)(2,1)}), bf16[8,64,1024]{2,1,0:T(8,128)(2,1)S(1)}, u32[]{:S(2)}, u32[]{:S(2)}) async-start(bf16[8,64,1024]{2,1,0:T(8,128)(2,1)} %shard_map.84), calls=%async_computation | async-start | bytes 2097152 | tf_op jit(solution)/shard_map/all_to_all | solution.py:370
  10.9 4.0 %copy-start.1 = (bf16[512,3584]{1,0:T(8,128)(2,1)S(1)}, bf16[512,3584]{1,0:T(8,128)(2,1)}, u32[]{:S(2)}) copy-start(bf16[512,3584]{1,0:T(8,128)(2,1)} %refs_4_.7) | copy-start | bytes 11010052
  13.9 14.7 %collective-permute-start.1 = (bf16[512,1792]{1,0:T(8,128)(2,1)}, bf16[512,1792]{1,0:T(8,128)(2,1)S(1)}, u32[]{:S(2)}, u32[]{:S(2)}) collective-permute-start(bf16[512,1792]{1,0:T(8,128)(2,1)} %constant_dynamic-slice_fusion.2), channel_id=1, source_target_pairs={{0,8},{8,0},{16,24},{24,16},{32,40},{40,32},{48,56},{56,48},{64,72... | collective-permute-start | bytes 5505032 | tf_op jit(solution)/shard_map/ppermute | solution.py:36
  16.2 12.4 %collective-permute-start.2 = (bf16[512,1792]{1,0:T(8,128)(2,1)}, bf16[512,1792]{1,0:T(8,128)(2,1)}, u32[]{:S(2)}, u32[]{:S(2)}) collective-permute-start(bf16[512,1792]{1,0:T(8,128)(2,1)} %constant_dynamic-slice_fusion.1), channel_id=1, source_target_pairs={{0,8},{8,0},{16,24},{24,16},{32,40},{40,32},{48,56},{56,48},{64,72... | collective-permute-start | bytes 5505032 | tf_op jit(solution)/shard_map/ppermute | solution.py:36
  17.6 11.1 %collective-permute-start.3 = (bf16[1792,512]{1,0:T(8,128)(2,1)}, bf16[1792,512]{1,0:T(8,128)(2,1)}, u32[]{:S(2)}, u32[]{:S(2)}) collective-permute-start(bf16[1792,512]{1,0:T(8,128)(2,1)} %constant_dynamic-slice_fusion), channel_id=1, source_target_pairs={{0,8},{8,0},{16,24},{24,16},{32,40},{40,32},{48,56},{56,48},{64,72... | collective-permute-start | bytes 5505032 | tf_op jit(solution)/shard_map/ppermute | solution.py:36
  27.2 104.4 %copy-start.4 = (bf16[512,1024]{1,0:T(8,128)(2,1)}, bf16[512,1024]{1,0:T(8,128)(2,1)S(1)}, u32[]{:S(2)}) copy-start(bf16[512,1024]{1,0:T(8,128)(2,1)S(1)} %get-tuple-element.39.tg.refs_6_.refs_7_.refs_4_) | copy-start | bytes 3145732
  27.2 104.4 %copy-start.8 = (bf16[512,512]{1,0:T(8,128)(2,1)}, bf16[512,512]{1,0:T(8,128)(2,1)S(1)}, u32[]{:S(2)}) copy-start(bf16[512,512]{1,0:T(8,128)(2,1)S(1)} %get-tuple-element.59.refs_5_.refs_6_.refs_3_) | copy-start | bytes 1572868
  27.2 3.7 %collective-permute-start = (bf16[512,1024]{1,0:T(8,128)(2,1)S(1)}, bf16[512,1024]{1,0:T(8,128)(2,1)S(1)}, u32[]{:S(2)}, u32[]{:S(2)}) collective-permute-start(bf16[512,1024]{1,0:T(8,128)(2,1)S(1)} %get-tuple-element.39.tg.refs_6_.refs_7_.refs_4_), channel_id=1, source_target_pairs={{0,8},{8,0},{16,24},{24,16},{32,40},{40,32},{48,56},{56,48},{64,72... | collective-permute-start | bytes 3145736 | tf_op jit(solution)/shard_map/ppermute | solution.py:36
  38.6 8.4 %collective-permute-start.5 = (bf16[3,64,640]{2,1,0:T(8,128)(2,1)S(1)}, bf16[3,64,640]{2,1,0:T(8,128)(2,1)S(1)}, u32[]{:S(2)}, u32[]{:S(2)}) collective-permute-start(bf16[3,64,640]{2,1,0:T(8,128)(2,1)S(1)} %get-tuple-element.46), channel_id=1, source_target_pairs={{0,32},{8,40},{16,48},{24,56},{32,64},{40,72},{48,80},{56,88},{64,... | collective-permute-start | bytes 737288 | tf_op jit(solution)/shard_map/ppermute | solution.py:36
  39.8 7.2 %collective-permute-start.6 = (bf16[3,64,640]{2,1,0:T(8,128)(2,1)S(1)}, bf16[3,64,640]{2,1,0:T(8,128)(2,1)S(1)}, u32[]{:S(2)}, u32[]{:S(2)}) collective-permute-start(bf16[3,64,640]{2,1,0:T(8,128)(2,1)S(1)} %get-tuple-element.47), channel_id=1, source_target_pairs={{0,96},{8,104},{16,112},{24,120},{32,0},{40,8},{48,16},{56,24},{64... | collective-permute-start | bytes 737288 | tf_op jit(solution)/shard_map/ppermute | solution.py:36
  41.3 5.5 %collective-permute-start.4 = (bf16[3,64,512]{2,1,0:T(8,128)(2,1)S(1)}, bf16[3,64,512]{2,1,0:T(8,128)(2,1)S(1)}, u32[]{:S(2)}, u32[]{:S(2)}) collective-permute-start(bf16[3,64,512]{2,1,0:T(8,128)(2,1)S(1)} %get-tuple-element.45), channel_id=1, source_target_pairs={{0,16},{8,24},{16,0},{24,8},{32,48},{40,56},{48,32},{56,40},{64,80... | collective-permute-start | bytes 589832 | tf_op jit(solution)/shard_map/ppermute | solution.py:36
  47.3 16.6 %collective-permute-start.7 = (bf16[3,64,1792]{2,1,0:T(8,128)(2,1)S(1)}, bf16[3,64,1792]{2,1,0:T(8,128)(2,1)S(1)}, u32[]{:S(2)}, u32[]{:S(2)}) collective-permute-start(bf16[3,64,1792]{2,1,0:T(8,128)(2,1)S(1)} %get-tuple-element.48), channel_id=1, source_target_pairs={{0,32},{8,40},{16,48},{24,56},{32,64},{40,72},{48,80},{56,88},{64,... | collective-permute-start | bytes 2064392 | tf_op jit(solution)/shard_map/ppermute | solution.py:36
  48.2 15.7 %collective-permute-start.8 = (bf16[3,64,1792]{2,1,0:T(8,128)(2,1)S(1)}, bf16[3,64,1792]{2,1,0:T(8,128)(2,1)S(1)}, u32[]{:S(2)}, u32[]{:S(2)}) collective-permute-start(bf16[3,64,1792]{2,1,0:T(8,128)(2,1)S(1)} %get-tuple-element.49), channel_id=1, source_target_pairs={{0,16},{8,24},{16,0},{24,8},{32,48},{40,56},{48,32},{56,40},{64,80... | collective-permute-start | bytes 2064392 | tf_op jit(solution)/shard_map/ppermute | solution.py:36
  49.0 15.1 %collective-permute-start.10 = (bf16[3,64,1792]{2,1,0:T(8,128)(2,1)S(1)}, bf16[3,64,1792]{2,1,0:T(8,128)(2,1)S(1)}, u32[]{:S(2)}, u32[]{:S(2)}) collective-permute-start(bf16[3,64,1792]{2,1,0:T(8,128)(2,1)S(1)} %get-tuple-element.51), channel_id=1, source_target_pairs={{0,96},{8,104},{16,112},{24,120},{32,0},{40,8},{48,16},{56,24},{64... | collective-permute-start | bytes 2064392 | tf_op jit(solution)/shard_map/ppermute | solution.py:36
  64.7 15.4 %collective-permute-start.9 = (bf16[3,64,1792]{2,1,0:T(8,128)(2,1)S(1)}, bf16[3,64,1792]{2,1,0:T(8,128)(2,1)S(1)}, u32[]{:S(2)}, u32[]{:S(2)}) collective-permute-start(bf16[3,64,1792]{2,1,0:T(8,128)(2,1)S(1)} %pad_maximum_fusion.4), channel_id=1, source_target_pairs={{0,32},{8,40},{16,48},{24,56},{32,64},{40,72},{48,80},{56,88},{64,... | collective-permute-start | bytes 2064392 | tf_op jit(solution)/shard_map/ppermute | solution.py:36
  65.5 14.6 %collective-permute-start.11 = (bf16[3,64,1792]{2,1,0:T(8,128)(2,1)S(1)}, bf16[3,64,1792]{2,1,0:T(8,128)(2,1)S(1)}, u32[]{:S(2)}, u32[]{:S(2)}) collective-permute-start(bf16[3,64,1792]{2,1,0:T(8,128)(2,1)S(1)} %pad_maximum_fusion.5), channel_id=1, source_target_pairs={{0,96},{8,104},{16,112},{24,120},{32,0},{40,8},{48,16},{56,24},{64... | collective-permute-start | bytes 2064392 | tf_op jit(solution)/shard_map/ppermute | solution.py:36
  67.6 13.6 %collective-permute-start.12 = (bf16[3,64,1792]{2,1,0:T(8,128)(2,1)S(1)}, bf16[3,64,1792]{2,1,0:T(8,128)(2,1)S(1)}, u32[]{:S(2)}, u32[]{:S(2)}) collective-permute-start(bf16[3,64,1792]{2,1,0:T(8,128)(2,1)S(1)} %pad_maximum_fusion.6), channel_id=1, source_target_pairs={{0,16},{8,24},{16,0},{24,8},{32,48},{40,56},{48,32},{56,40},{64,80... | collective-permute-start | bytes 2064392 | tf_op jit(solution)/shard_map/ppermute | solution.py:36
  81.8 13.6 %collective-permute-start.13 = (bf16[3,64,1792]{2,1,0:T(8,128)(2,1)S(1)}, bf16[3,64,1792]{2,1,0:T(8,128)(2,1)S(1)}, u32[]{:S(2)}, u32[]{:S(2)}) collective-permute-start(bf16[3,64,1792]{2,1,0:T(8,128)(2,1)S(1)} %pad_maximum_fusion.7), channel_id=1, source_target_pairs={{0,32},{8,40},{16,48},{24,56},{32,64},{40,72},{48,80},{56,88},{64,... | collective-permute-start | bytes 2064392 | tf_op jit(solution)/shard_map/ppermute | solution.py:36
  81.9 13.5 %collective-permute-start.14 = (bf16[3,64,1792]{2,1,0:T(8,128)(2,1)S(1)}, bf16[3,64,1792]{2,1,0:T(8,128)(2,1)S(1)}, u32[]{:S(2)}, u32[]{:S(2)}) collective-permute-start(bf16[3,64,1792]{2,1,0:T(8,128)(2,1)S(1)} %pad_maximum_fusion.7), channel_id=1, source_target_pairs={{0,16},{8,24},{16,0},{24,8},{32,48},{40,56},{48,32},{56,40},{64,80... | collective-permute-start | bytes 2064392 | tf_op jit(solution)/shard_map/ppermute | solution.py:36
  82.8 12.8 %collective-permute-start.16 = (bf16[3,64,1792]{2,1,0:T(8,128)(2,1)S(1)}, bf16[3,64,1792]{2,1,0:T(8,128)(2,1)S(1)}, u32[]{:S(2)}, u32[]{:S(2)}) collective-permute-start(bf16[3,64,1792]{2,1,0:T(8,128)(2,1)S(1)} %pad_maximum_fusion.7), channel_id=1, source_target_pairs={{0,96},{8,104},{16,112},{24,120},{32,0},{40,8},{48,16},{56,24},{64... | collective-permute-start | bytes 2064392 | tf_op jit(solution)/shard_map/ppermute | solution.py:36
  95.8 12.6 %collective-permute-start.15 = (bf16[3,64,1792]{2,1,0:T(8,128)(2,1)S(1)}, bf16[3,64,1792]{2,1,0:T(8,128)(2,1)S(1)}, u32[]{:S(2)}, u32[]{:S(2)}) collective-permute-start(bf16[3,64,1792]{2,1,0:T(8,128)(2,1)S(1)} %get-tuple-element.85), channel_id=1, source_target_pairs={{0,32},{8,40},{16,48},{24,56},{32,64},{40,72},{48,80},{56,88},{64,... | collective-permute-start | bytes 2064392 | tf_op jit(solution)/shard_map/ppermute | solution.py:36
  95.8 13.5 %collective-permute-start.17 = (bf16[3,64,1792]{2,1,0:T(8,128)(2,1)S(1)}, bf16[3,64,1792]{2,1,0:T(8,128)(2,1)S(1)}, u32[]{:S(2)}, u32[]{:S(2)}) collective-permute-start(bf16[3,64,1792]{2,1,0:T(8,128)(2,1)S(1)} %get-tuple-element.84), channel_id=1, source_target_pairs={{0,96},{8,104},{16,112},{24,120},{32,0},{40,8},{48,16},{56,24},{64... | collective-permute-start | bytes 2064392 | tf_op jit(solution)/shard_map/ppermute | solution.py:36
  98.7 10.6 %collective-permute-start.18 = (bf16[3,64,1792]{2,1,0:T(8,128)(2,1)S(1)}, bf16[3,64,1792]{2,1,0:T(8,128)(2,1)S(1)}, u32[]{:S(2)}, u32[]{:S(2)}) collective-permute-start(bf16[3,64,1792]{2,1,0:T(8,128)(2,1)S(1)} %get-tuple-element.83), channel_id=1, source_target_pairs={{0,16},{8,24},{16,0},{24,8},{32,48},{40,56},{48,32},{56,40},{64,80... | collective-permute-start | bytes 2064392 | tf_op jit(solution)/shard_map/ppermute | solution.py:36
  109.3 26.1 %collective-permute-start.19 = (bf16[3,256,1792]{2,1,0:T(8,128)(2,1)S(1)}, bf16[3,256,1792]{2,1,0:T(8,128)(2,1)S(1)}, u32[]{:S(2)}, u32[]{:S(2)}) collective-permute-start(bf16[3,256,1792]{2,1,0:T(8,128)(2,1)S(1)} %maximum_maximum_fusion.refs_0_), channel_id=1, source_target_pairs={{0,8},{8,0},{16,24},{24,16},{32,40},{40,32},{48,56},{56,48},{64,72... | collective-permute-start | bytes 8257544 | tf_op jit(solution)/shard_map/ppermute | solution.py:36
  117.3 10.4 %copy-start.2 = (bf16[512,3584]{1,0:T(8,128)(2,1)S(1)}, bf16[512,3584]{1,0:T(8,128)(2,1)}, u32[]{:S(2)}) copy-start(bf16[512,3584]{1,0:T(8,128)(2,1)} %refs_4_.7) | copy-start | bytes 11010052
  117.4 10.3 %copy-start = (bf16[512,3584]{1,0:T(8,128)(2,1)S(1)}, bf16[512,3584]{1,0:T(8,128)(2,1)}, u32[]{:S(2)}) copy-start(bf16[512,3584]{1,0:T(8,128)(2,1)} %refs_3_.7) | copy-start | bytes 11010052
  117.5 8.9 %collective-permute-start.21 = (bf16[3,64,640]{2,1,0:T(8,128)(2,1)S(1)}, bf16[3,64,640]{2,1,0:T(8,128)(2,1)S(1)}, u32[]{:S(2)}, u32[]{:S(2)}) collective-permute-start(bf16[3,64,640]{2,1,0:T(8,128)(2,1)S(1)} %pad_maximum_fusion.9), channel_id=1, source_target_pairs={{0,32},{8,40},{16,48},{24,56},{32,64},{40,72},{48,80},{56,88},{64,... | collective-permute-start | bytes 737288 | tf_op jit(solution)/shard_map/ppermute | solution.py:36
  117.5 8.8 %collective-permute-start.22 = (bf16[3,64,640]{2,1,0:T(8,128)(2,1)S(1)}, bf16[3,64,640]{2,1,0:T(8,128)(2,1)S(1)}, u32[]{:S(2)}, u32[]{:S(2)}) collective-permute-start(bf16[3,64,640]{2,1,0:T(8,128)(2,1)S(1)} %slice.95), channel_id=1, source_target_pairs={{0,96},{8,104},{16,112},{24,120},{32,0},{40,8},{48,16},{56,24},{64... | collective-permute-start | bytes 737288 | tf_op jit(solution)/shard_map/ppermute | solution.py:36
  120.2 5.9 %collective-permute-start.20 = (bf16[3,64,512]{2,1,0:T(8,128)(2,1)S(1)}, bf16[3,64,512]{2,1,0:T(8,128)(2,1)S(1)}, u32[]{:S(2)}, u32[]{:S(2)}) collective-permute-start(bf16[3,64,512]{2,1,0:T(8,128)(2,1)S(1)} %slice.92), channel_id=1, source_target_pairs={{0,16},{8,24},{16,0},{24,8},{32,48},{40,56},{48,32},{56,40},{64,80... | collective-permute-start | bytes 589832 | tf_op jit(solution)/shard_map/ppermute | solution.py:36
  126.4 9.0 %collective-permute-start.23 = (bf16[3,192,1792]{2,1,0:T(8,128)(2,1)S(1)}, bf16[3,192,1792]{2,1,0:T(8,128)(2,1)S(1)}, u32[]{:S(2)}, u32[]{:S(2)}) collective-permute-start(bf16[3,192,1792]{2,1,0:T(8,128)(2,1)S(1)} %pad_maximum_fusion.refs_1_), channel_id=1, source_target_pairs={{0,8},{8,0},{16,24},{24,16},{32,40},{40,32},{48,56},{56,48},{64,72... | collective-permute-start | bytes 6193160 | tf_op jit(solution)/shard_map/ppermute | solution.py:36
  127.7 7.7 %collective-permute-start.24 = (bf16[3,64,1792]{2,1,0:T(8,128)(2,1)S(1)}, bf16[3,64,1792]{2,1,0:T(8,128)(2,1)S(1)}, u32[]{:S(2)}, u32[]{:S(2)}) collective-permute-start(bf16[3,64,1792]{2,1,0:T(8,128)(2,1)S(1)} %pad_maximum_fusion.8.refs_2_), channel_id=1, source_target_pairs={{0,8},{8,0},{16,24},{24,16},{32,40},{40,32},{48,56},{56,48},{64,72... | collective-permute-start | bytes 2064392 | tf_op jit(solution)/shard_map/ppermute | solution.py:36
  140.7 17.8 %all-to-all-start.1 = ((bf16[8,64,512]{2,1,0:T(8,128)(2,1)}), bf16[8,64,512]{2,1,0:T(8,128)(2,1)S(1)}, u32[]{:S(2)}, u32[]{:S(2)}) async-start(bf16[8,64,512]{2,1,0:T(8,128)(2,1)} %shard_map.92), calls=%async_computation.1 | async-start | bytes 1048576 | tf_op jit(solution)/shard_map/all_to_all | solution.py:391
  (6 other events, 10.6 us)

commit v4 on v3

--- a/solution.py
+++ b/solution.py
@@ -254,7 +254,7 @@
         ),
         out_shape=out_shape,
         input_output_aliases=aliases,
-        compiler_params=params(32 if terms else 48),
+        compiler_params=params(32),
         cost_estimate=pl.CostEstimate(flops=flops, bytes_accessed=8 << 20, transcendentals=0),
     )(pos, *args)
 
@@ -342,7 +342,7 @@
     rp = send(join(lo(g30), hi(g01)), XP)
     rm = send(join(lo(g01), hi(g10)), XM)
     rz = send(join(lo(g30), hi(g10)), ZS)
-    rp, rm, rz, near = after(rp, rm, rz, rows(g10, g30, g01, e))
+    rm, near = after(rm, rows(g10, g30, g01, e))
     turn_up = join(rz[..., z:MID], rp[..., MID:x])
     fz, fp, fm = send(rp[..., :z], ZS), send(turn_up, XP), send(rz[..., x:], XM)
     far, mids = after(join(fz, fp, fm), rows(rp, rm, rz))

time: 160 us -> 158 us (0.988)
  Pallas kernels: 40.6 us -> 38.5 us
    pallas_call x6, Pallas kernels: 22.4 us -> 19.3 us  [part(): pl.pallas_call(functools.partial(part_kernel, half, bool(terms), bool(wei...]
  transfers between devices with their start and end apart: 27 -> 27, of which waited for: 12 -> 12; matrix products, arithmetic and copies ran while one was open for 4% -> 4% of each run, Pallas kernels for 16% -> 14%
where the time goes in v4:
time: 158 us
  waiting for transfers between devices  58.4 us (37%)
  starting transfers between devices  47.1 us (30%)
  Pallas kernels  38.5 us (24%)
  local copies, waits for them, and re-layouts  10.6 us (7%)
  other arithmetic  2.14 us (1%)
    ppermute x25, waiting for transfers between devices, send(): return lax.ppermute(a, 'gx', pairs)  51 us
    ppermute x25, starting transfers between devices, send(): return lax.ppermute(a, 'gx', pairs)  34.1 us
    pallas_call x6, Pallas kernels, part(): pl.pallas_call(functools.partial(part_kernel, half, bool(terms), bool(wei...  19.3 us
    pallas_call x2, Pallas kernels, sums(): pl.pallas_call(functools.partial(sums_kernel, part), grid_spec=pltpu.Pref...  14.5 us
    all_to_all x1, starting transfers between devices, shards(): blocks = lax.all_to_all(spread(tokens, out_grad), 'gy', 0, 0, tiled=True)  8.33 us
    all_to_all x1, waiting for transfers between devices, shards(): blocks = lax.all_to_all(spread(tokens, out_grad), 'gy', 0, 0, tiled=True)  7.4 us
    dynamic_slice x3, local copies, waits for them, and re-layouts, shards(): lax.dynamic_slice_in_dim(w, far_half, HALF, axis)  5.69 us
    all_to_all x1, starting transfers between devices, shards(): grad_tokens = total_of(lax.all_to_all(terms, 'gy', 0, 0, tiled=True))  4.73 us
  transfers between devices with their start and end apart: 27, of which 12 were waited for; matrix products, arithmetic and copies ran while one was open for 4% of the time, Pallas kernels for 14%

profile of v4, /device:TPU:1, one launch (start us, length us, event | category | flops | bytes accessed | tf_op | source)
XLA Modules:
  0.0 157.8 jit_solution(9688095458517749275)
XLA Ops:
  0.6 1.9 %shard_map.84 = bf16[8,64,1024]{2,1,0:T(8,128)(2,1)} custom-call(bf16[64,512]{1,0:T(8,128)(2,1)} %tokens.1, bf16[64,512]{1,0:T(8,128)(2,1)} %out_grad.1), custom_call_target="tpu_custom_call" | custom-call | bytes 1048576 | tf_op jit(solution)/shard_map/pallas_call | solution.py:64
  2.6 8.3 %all-to-all-start = ((bf16[8,64,1024]{2,1,0:T(8,128)(2,1)}), bf16[8,64,1024]{2,1,0:T(8,128)(2,1)S(1)}, u32[]{:S(2)}, u32[]{:S(2)}) async-start(bf16[8,64,1024]{2,1,0:T(8,128)(2,1)} %shard_map.84), calls=%async_computation | async-start | bytes 2097152 | tf_op jit(solution)/shard_map/all_to_all | solution.py:370
  10.9 3.0 %constant_dynamic-slice_fusion.2 = bf16[512,1792]{1,0:T(8,128)(2,1)} fusion(bf16[512,3584]{1,0:T(8,128)(2,1)} %refs_3_.7, s32[]{:T(128)S(6)} %select_n.27), kind=kLoop, calls=%fused_computation.31 | loop fusion | bytes 3670020 | tf_op jit(solution)/shard_map/dynamic_slice | solution.py:373
  14.9 1.3 constant_dynamic-slice_fusion.1
  19.0 7.4 %all-to-all-done.blocks = bf16[8,64,1024]{2,1,0:T(8,128)(2,1)S(1)} async-done(((bf16[8,64,1024]{2,1,0:T(8,128)(2,1)}), bf16[8,64,1024]{2,1,0:T(8,128)(2,1)S(1)}, u32[]{:S(2)}, u32[]{:S(2)}) %all-to-all-start) | async-done | bytes 1048608 | tf_op jit(solution)/shard_map/all_to_all | solution.py:370
  27.2 1.4 collective-permute-start
  28.6 2.3 %collective-permute-done.tg_sib = bf16[512,1024]{1,0:T(8,128)(2,1)S(1)} collective-permute-done((bf16[512,1024]{1,0:T(8,128)(2,1)S(1)}, bf16[512,1024]{1,0:T(8,128)(2,1)S(1)}, u32[]{:S(2)}, u32[]{:S(2)}) %collective-permute-start) | collective-permute-done | bytes 1048608 | tf_op jit(solution)/shard_map/ppermute | solution.py:36
  30.9 7.6 %shard_map.87 = (f32[3,64,1792]{2,1,0:T(8,128)S(1)}, f32[3,64,1792]{2,1,0:T(8,128)S(1)}, f32[3,64,1792]{2,1,0:T(8,128)S(1)}, bf16[3,64,512]{2,1,0:T(8,128)(2,1)S...) custom-call(s32[3]{0:T(128)S(1)} %pad_add_fusion.pos, ...), custom_call_target="tpu_custom_call" | custom-call | flops 2818572288 | bytes 20971520 | tf_op jit(solution)/shard_map/pallas_call | solution.py:127
  39.8 1.5 collective-permute-start.6
  42.1 4.7 %collective-permute-done.4.rz = bf16[3,64,512]{2,1,0:T(8,128)(2,1)S(1)} collective-permute-done((bf16[3,64,512]{2,1,0:T(8,128)(2,1)S(1)}, bf16[3,64,512]{2,1,0:T(8,128)(2,1)S(1)}, u32[]{:S(2)}, u32[]{:S(2)}) %collective-permute-start.4) | collective-permute-done | bytes 196640 | tf_op jit(solution)/shard_map/ppermute | solution.py:36
  49.0 1.8 %collective-permute-start.10 = (bf16[3,64,1792]{2,1,0:T(8,128)(2,1)S(1)}, bf16[3,64,1792]{2,1,0:T(8,128)(2,1)S(1)}, u32[]{:S(2)}, u32[]{:S(2)}) collective-permute-start(bf16[3,64,1792]{2,1,0:T(8,128)(2,1)S(1)} %get-tuple-element.49), channel_id=1, source_target_pairs={{0,96},{8,104},{16,112},{24,120},{32,0},{40,8},{48,16},{56,24},{64... | collective-permute-start | bytes 2064392 | tf_op jit(solution)/shard_map/ppermute | solution.py:36
  50.8 6.9 %shard_map.86 = (f32[3,64,1792]{2,1,0:T(8,128)S(1)}, f32[3,64,1792]{2,1,0:T(8,128)S(1)}, f32[3,64,1792]{2,1,0:T(8,128)S(1)}, f32[3,64,1792]{2,1,0:T(8,128)S(1)}) custom-call(s32[3]{0:T(128)S(1)} %pad_add_fusion.pos, bf16[512,1024]{1,0:T(8,128)(2,1)S(1)} %get-tuple-element.37.tg.refs_6_.refs_7_.refs_4_, bf16[512,1024]{1,0:T(8,128)(2,1)S(1)} %collective-permute-done.tg_sib, ...), custom_call_target="tpu_custom_call" | custom-call | flops 2818572288 | bytes 20971520 | tf_op jit(solution)/shard_map/pallas_call | solution.py:127
  57.8 6.1 %collective-permute-done.7 = bf16[3,64,1792]{2,1,0:T(8,128)(2,1)S(1)} collective-permute-done((bf16[3,64,1792]{2,1,0:T(8,128)(2,1)S(1)}, bf16[3,64,1792]{2,1,0:T(8,128)(2,1)S(1)}, u32[]{:S(2)}, u32[]{:S(2)}) %collective-permute-start.7) | collective-permute-done | bytes 688160 | tf_op jit(solution)/shard_map/ppermute | solution.py:36
  65.5 2.1 %collective-permute-start.11 = (bf16[3,64,1792]{2,1,0:T(8,128)(2,1)S(1)}, bf16[3,64,1792]{2,1,0:T(8,128)(2,1)S(1)}, u32[]{:S(2)}, u32[]{:S(2)}) collective-permute-start(bf16[3,64,1792]{2,1,0:T(8,128)(2,1)S(1)} %pad_maximum_fusion.5), channel_id=1, source_target_pairs={{0,96},{8,104},{16,112},{24,120},{32,0},{40,8},{48,16},{56,24},{64... | collective-permute-start | bytes 2064392 | tf_op jit(solution)/shard_map/ppermute | solution.py:36
  68.4 11.7 %collective-permute-done.9 = bf16[3,64,1792]{2,1,0:T(8,128)(2,1)S(1)} collective-permute-done((bf16[3,64,1792]{2,1,0:T(8,128)(2,1)S(1)}, bf16[3,64,1792]{2,1,0:T(8,128)(2,1)S(1)}, u32[]{:S(2)}, u32[]{:S(2)}) %collective-permute-start.9) | collective-permute-done | bytes 688160 | tf_op jit(solution)/shard_map/ppermute | solution.py:36
  81.8 1.4 collective-permute-start.14
  84.2 10.4 %collective-permute-done.14 = bf16[3,64,1792]{2,1,0:T(8,128)(2,1)S(1)} collective-permute-done((bf16[3,64,1792]{2,1,0:T(8,128)(2,1)S(1)}, bf16[3,64,1792]{2,1,0:T(8,128)(2,1)S(1)}, u32[]{:S(2)}, u32[]{:S(2)}) %collective-permute-start.14) | collective-permute-done | bytes 688160 | tf_op jit(solution)/shard_map/ppermute | solution.py:36
  95.3 1.8 %collective-permute-done.16 = bf16[3,64,1792]{2,1,0:T(8,128)(2,1)S(1)} collective-permute-done((bf16[3,64,1792]{2,1,0:T(8,128)(2,1)S(1)}, bf16[3,64,1792]{2,1,0:T(8,128)(2,1)S(1)}, u32[]{:S(2)}, u32[]{:S(2)}) %collective-permute-start.16) | collective-permute-done | bytes 688160 | tf_op jit(solution)/shard_map/ppermute | solution.py:36
  99.5 7.9 %collective-permute-done.15 = bf16[3,64,1792]{2,1,0:T(8,128)(2,1)S(1)} collective-permute-done((bf16[3,64,1792]{2,1,0:T(8,128)(2,1)S(1)}, bf16[3,64,1792]{2,1,0:T(8,128)(2,1)S(1)}, u32[]{:S(2)}, u32[]{:S(2)}) %collective-permute-start.15) | collective-permute-done | bytes 688160 | tf_op jit(solution)/shard_map/ppermute | solution.py:36
  107.4 7.7 %collective-permute-start.17 = (bf16[3,256,1792]{2,1,0:T(8,128)(2,1)S(1)}, bf16[3,256,1792]{2,1,0:T(8,128)(2,1)S(1)}, u32[]{:S(2)}, u32[]{:S(2)}) collective-permute-start(bf16[3,256,1792]{2,1,0:T(8,128)(2,1)S(1)} %maximum_maximum_fusion.refs_0_), channel_id=1, source_target_pairs={{0,8},{8,0},{16,24},{24,16},{32,40},{40,32},{48,56},{56,48},{64,72... | collective-permute-start | bytes 8257544 | tf_op jit(solution)/shard_map/ppermute | solution.py:36
  115.4 2.7 %collective-permute-start.22 = (bf16[3,64,640]{2,1,0:T(8,128)(2,1)S(1)}, bf16[3,64,640]{2,1,0:T(8,128)(2,1)S(1)}, u32[]{:S(2)}, u32[]{:S(2)}) collective-permute-start(bf16[3,64,640]{2,1,0:T(8,128)(2,1)S(1)} %slice.114), channel_id=1, source_target_pairs={{0,96},{8,104},{16,112},{24,120},{32,0},{40,8},{48,16},{56,24},{64... | collective-permute-start | bytes 737288 | tf_op jit(solution)/shard_map/ppermute | solution.py:36
  118.8 4.2 %collective-permute-done.19 = bf16[3,64,512]{2,1,0:T(8,128)(2,1)S(1)} collective-permute-done((bf16[3,64,512]{2,1,0:T(8,128)(2,1)S(1)}, bf16[3,64,512]{2,1,0:T(8,128)(2,1)S(1)}, u32[]{:S(2)}, u32[]{:S(2)}) %collective-permute-start.19) | collective-permute-done | bytes 196640 | tf_op jit(solution)/shard_map/ppermute | solution.py:36
  123.1 4.2 %collective-permute-start.23 = (bf16[3,192,1792]{2,1,0:T(8,128)(2,1)S(1)}, bf16[3,192,1792]{2,1,0:T(8,128)(2,1)S(1)}, u32[]{:S(2)}, u32[]{:S(2)}) collective-permute-start(bf16[3,192,1792]{2,1,0:T(8,128)(2,1)S(1)} %pad_maximum_fusion.refs_1_), channel_id=1, source_target_pairs={{0,8},{8,0},{16,24},{24,16},{32,40},{40,32},{48,56},{56,48},{64,72... | collective-permute-start | bytes 6193160 | tf_op jit(solution)/shard_map/ppermute | solution.py:36
  127.3 3.8 %shard_map.89 = (f32[512,512]{1,0:T(8,128)S(1)}, bf16[512,3584]{1,0:T(8,128)(2,1)}, bf16[512,3584]{1,0:T(8,128)(2,1)}, bf16[3584,512]{1,0:T(8,128)(2,1)}) custom-call(s32[3]{0:T(128)S(1)} %pad_add_fusion.pos, bf16[3,256,1792]{2,1,0:T(8,128)(2,1)S(1)} %maximum_maximum_fusion.refs_0_, bf16[3,192,1792]{2,1,0:T(8,128)(2,1)S(1)} %pad_maximum_fusion.refs_1_, ...), custom_call_target="tpu_custom_call" | custom-call | flops 2348810240 | bytes 8388608 | tf_op jit(solution)/shard_map/pallas_call | solution.py:246
  131.2 3.8 %shard_map.90 = (f32[512,512]{1,0:T(8,128)S(1)}, bf16[512,3584]{1,0:T(8,128)(2,1)}, bf16[512,3584]{1,0:T(8,128)(2,1)}, bf16[3584,512]{1,0:T(8,128)(2,1)}) custom-call(s32[3]{0:T(128)S(1)} %pad_add_fusion.pos, bf16[3,256,1792]{2,1,0:T(8,128)(2,1)S(1)} %maximum_maximum_fusion.refs_0_, ...), custom_call_target="tpu_custom_call", output_to_operand_aliasing={{1}: (9, {}), {2}: (10, {}), {3}: (11, {})} | custom-call | flops 2348810240 | bytes 8388608 | tf_op jit(solution)/shard_map/pallas_call | solution.py:246
  135.0 2.2 %shard_map.91.refs_5_ = f32[512,512]{1,0:T(8,128)S(1)} custom-call(s32[3]{0:T(128)S(1)} %pad_add_fusion.pos, bf16[3,256,1792]{2,1,0:T(8,128)(2,1)S(1)} %collective-permute-done.17.refs_0_, bf16[3,192,1792]{2,1,0:T(8,128)(2,1)S(1)} %collective-permute-done.23.refs_1_, bf16[3,64,1792]{2,1,0:T(8,128)(2,1)S(1)} %collective-permute-done.24.refs_2_, ...), custom_call_target="tpu_custom_call" | custom-call | flops 939524096 | bytes 8388608 | tf_op jit(solution)/shard_map/pallas_call | solution.py:246
  137.2 2.3 %shard_map.92 = bf16[8,64,512]{2,1,0:T(8,128)(2,1)S(1)} custom-call(s32[3]{0:T(128)S(1)} %pad_add_fusion.pos, bf16[3,256,1792]{2,1,0:T(8,128)(2,1)S(1)} %collective-permute-done.17.refs_0_, bf16[3,192,1792]{2,1,0:T(8,128)(2,1)S(1)} %collective-permute-done.23.refs_1_, bf16[3,64,1792]{2,1,0:T(8,128)(2,1)S(1)} %collective-permute-done.24.refs_2_, ...), custom_call_target="tpu_custom_call" | custom-call | flops 939524096 | bytes 8388608 | tf_op jit(solution)/shard_map/pallas_call | solution.py:246
  140.3 4.7 %all-to-all-start.1 = ((bf16[8,64,512]{2,1,0:T(8,128)(2,1)}), bf16[8,64,512]{2,1,0:T(8,128)(2,1)}, u32[]{:S(2)}, u32[]{:S(2)}) async-start(bf16[8,64,512]{2,1,0:T(8,128)(2,1)} %copy-done.9), calls=%async_computation.1 | async-start | bytes 1048576 | tf_op jit(solution)/shard_map/all_to_all | solution.py:391
  146.2 1.6 copy-done.6
  148.9 3.6 %shard_map.94 = (bf16[512,3584]{1,0:T(8,128)(2,1)}, bf16[512,3584]{1,0:T(8,128)(2,1)}, bf16[3584,512]{1,0:T(8,128)(2,1)}) custom-call(s32[3]{0:T(128)S(1)} %pad_add_fusion.pos, bf16[3,256,1792]{2,1,0:T(8,128)(2,1)S(1)} %collective-permute-done.17.refs_0_, ...), custom_call_target="tpu_custom_call", output_to_operand_aliasing={{0}: (6, {}), {1}: (7, {}), {2}: (8, {})} | custom-call | flops 1409286144 | bytes 8388608 | tf_op jit(solution)/shard_map/pallas_call | solution.py:246
  152.5 3.6 %shard_map.95 = (bf16[512,3584]{1,0:T(8,128)(2,1)}, bf16[512,3584]{1,0:T(8,128)(2,1)}, bf16[3584,512]{1,0:T(8,128)(2,1)}) custom-call(s32[3]{0:T(128)S(1)} %pad_add_fusion.pos, bf16[3,256,1792]{2,1,0:T(8,128)(2,1)S(1)} %collective-permute-done.17.refs_0_, ...), custom_call_target="tpu_custom_call", output_to_operand_aliasing={{0}: (6, {}), {1}: (7, {}), {2}: (8, {})} | custom-call | flops 1409286144 | bytes 8388608 | tf_op jit(solution)/shard_map/pallas_call | solution.py:246
  156.1 1.7 %shard_map.93 = bf16[64,512]{1,0:T(8,128)(2,1)} custom-call(bf16[8,64,512]{2,1,0:T(8,128)(2,1)} %all-to-all-done.1.terms), custom_call_target="tpu_custom_call" | custom-call | flops 262144 | bytes 524288 | tf_op jit(solution)/shard_map/pallas_call | solution.py:270
  (84 shorter events, 21.1 us)
Async XLA Ops:
  2.6 23.8 %all-to-all-start = ((bf16[8,64,1024]{2,1,0:T(8,128)(2,1)}), bf16[8,64,1024]{2,1,0:T(8,128)(2,1)S(1)}, u32[]{:S(2)}, u32[]{:S(2)}) async-start(bf16[8,64,1024]{2,1,0:T(8,128)(2,1)} %shard_map.84), calls=%async_computation | async-start | bytes 2097152 | tf_op jit(solution)/shard_map/all_to_all | solution.py:370
  10.9 4.0 %copy-start.1 = (bf16[512,3584]{1,0:T(8,128)(2,1)S(1)}, bf16[512,3584]{1,0:T(8,128)(2,1)}, u32[]{:S(2)}) copy-start(bf16[512,3584]{1,0:T(8,128)(2,1)} %refs_4_.7) | copy-start | bytes 11010052
  13.9 14.7 %collective-permute-start.1 = (bf16[512,1792]{1,0:T(8,128)(2,1)}, bf16[512,1792]{1,0:T(8,128)(2,1)S(1)}, u32[]{:S(2)}, u32[]{:S(2)}) collective-permute-start(bf16[512,1792]{1,0:T(8,128)(2,1)} %constant_dynamic-slice_fusion.2), channel_id=1, source_target_pairs={{0,8},{8,0},{16,24},{24,16},{32,40},{40,32},{48,56},{56,48},{64,72... | collective-permute-start | bytes 5505032 | tf_op jit(solution)/shard_map/ppermute | solution.py:36
  16.2 12.4 %collective-permute-start.2 = (bf16[512,1792]{1,0:T(8,128)(2,1)}, bf16[512,1792]{1,0:T(8,128)(2,1)}, u32[]{:S(2)}, u32[]{:S(2)}) collective-permute-start(bf16[512,1792]{1,0:T(8,128)(2,1)} %constant_dynamic-slice_fusion.1), channel_id=1, source_target_pairs={{0,8},{8,0},{16,24},{24,16},{32,40},{40,32},{48,56},{56,48},{64,72... | collective-permute-start | bytes 5505032 | tf_op jit(solution)/shard_map/ppermute | solution.py:36
  17.6 11.1 %collective-permute-start.3 = (bf16[1792,512]{1,0:T(8,128)(2,1)}, bf16[1792,512]{1,0:T(8,128)(2,1)}, u32[]{:S(2)}, u32[]{:S(2)}) collective-permute-start(bf16[1792,512]{1,0:T(8,128)(2,1)} %constant_dynamic-slice_fusion), channel_id=1, source_target_pairs={{0,8},{8,0},{16,24},{24,16},{32,40},{40,32},{48,56},{56,48},{64,72... | collective-permute-start | bytes 5505032 | tf_op jit(solution)/shard_map/ppermute | solution.py:36
  27.2 103.9 %copy-start.3 = (bf16[512,1024]{1,0:T(8,128)(2,1)}, bf16[512,1024]{1,0:T(8,128)(2,1)S(1)}, u32[]{:S(2)}) copy-start(bf16[512,1024]{1,0:T(8,128)(2,1)S(1)} %get-tuple-element.37.tg.refs_6_.refs_7_.refs_4_) | copy-start | bytes 3145732
  27.2 103.9 %copy-start.7 = (bf16[512,512]{1,0:T(8,128)(2,1)}, bf16[512,512]{1,0:T(8,128)(2,1)S(1)}, u32[]{:S(2)}) copy-start(bf16[512,512]{1,0:T(8,128)(2,1)S(1)} %get-tuple-element.55.refs_5_.refs_6_.refs_3_) | copy-start | bytes 1572868
  27.2 3.7 %collective-permute-start = (bf16[512,1024]{1,0:T(8,128)(2,1)S(1)}, bf16[512,1024]{1,0:T(8,128)(2,1)S(1)}, u32[]{:S(2)}, u32[]{:S(2)}) collective-permute-start(bf16[512,1024]{1,0:T(8,128)(2,1)S(1)} %get-tuple-element.37.tg.refs_6_.refs_7_.refs_4_), channel_id=1, source_target_pairs={{0,8},{8,0},{16,24},{24,16},{32,40},{40,32},{48,56},{56,48},{64,72... | collective-permute-start | bytes 3145736 | tf_op jit(solution)/shard_map/ppermute | solution.py:36
  38.6 8.4 %collective-permute-start.5 = (bf16[3,64,640]{2,1,0:T(8,128)(2,1)S(1)}, bf16[3,64,640]{2,1,0:T(8,128)(2,1)S(1)}, u32[]{:S(2)}, u32[]{:S(2)}) collective-permute-start(bf16[3,64,640]{2,1,0:T(8,128)(2,1)S(1)} %get-tuple-element.44), channel_id=1, source_target_pairs={{0,32},{8,40},{16,48},{24,56},{32,64},{40,72},{48,80},{56,88},{64,... | collective-permute-start | bytes 737288 | tf_op jit(solution)/shard_map/ppermute | solution.py:36
  39.8 7.2 %collective-permute-start.6 = (bf16[3,64,640]{2,1,0:T(8,128)(2,1)S(1)}, bf16[3,64,640]{2,1,0:T(8,128)(2,1)S(1)}, u32[]{:S(2)}, u32[]{:S(2)}) collective-permute-start(bf16[3,64,640]{2,1,0:T(8,128)(2,1)S(1)} %get-tuple-element.45), channel_id=1, source_target_pairs={{0,96},{8,104},{16,112},{24,120},{32,0},{40,8},{48,16},{56,24},{64... | collective-permute-start | bytes 737288 | tf_op jit(solution)/shard_map/ppermute | solution.py:36
  41.3 5.5 %collective-permute-start.4 = (bf16[3,64,512]{2,1,0:T(8,128)(2,1)S(1)}, bf16[3,64,512]{2,1,0:T(8,128)(2,1)S(1)}, u32[]{:S(2)}, u32[]{:S(2)}) collective-permute-start(bf16[3,64,512]{2,1,0:T(8,128)(2,1)S(1)} %get-tuple-element.43), channel_id=1, source_target_pairs={{0,16},{8,24},{16,0},{24,8},{32,48},{40,56},{48,32},{56,40},{64,80... | collective-permute-start | bytes 589832 | tf_op jit(solution)/shard_map/ppermute | solution.py:36
  47.3 16.6 %collective-permute-start.7 = (bf16[3,64,1792]{2,1,0:T(8,128)(2,1)S(1)}, bf16[3,64,1792]{2,1,0:T(8,128)(2,1)S(1)}, u32[]{:S(2)}, u32[]{:S(2)}) collective-permute-start(bf16[3,64,1792]{2,1,0:T(8,128)(2,1)S(1)} %get-tuple-element.46), channel_id=1, source_target_pairs={{0,32},{8,40},{16,48},{24,56},{32,64},{40,72},{48,80},{56,88},{64,... | collective-permute-start | bytes 2064392 | tf_op jit(solution)/shard_map/ppermute | solution.py:36
  48.2 15.7 %collective-permute-start.8 = (bf16[3,64,1792]{2,1,0:T(8,128)(2,1)S(1)}, bf16[3,64,1792]{2,1,0:T(8,128)(2,1)S(1)}, u32[]{:S(2)}, u32[]{:S(2)}) collective-permute-start(bf16[3,64,1792]{2,1,0:T(8,128)(2,1)S(1)} %get-tuple-element.47), channel_id=1, source_target_pairs={{0,16},{8,24},{16,0},{24,8},{32,48},{40,56},{48,32},{56,40},{64,80... | collective-permute-start | bytes 2064392 | tf_op jit(solution)/shard_map/ppermute | solution.py:36
  49.0 15.1 %collective-permute-start.10 = (bf16[3,64,1792]{2,1,0:T(8,128)(2,1)S(1)}, bf16[3,64,1792]{2,1,0:T(8,128)(2,1)S(1)}, u32[]{:S(2)}, u32[]{:S(2)}) collective-permute-start(bf16[3,64,1792]{2,1,0:T(8,128)(2,1)S(1)} %get-tuple-element.49), channel_id=1, source_target_pairs={{0,96},{8,104},{16,112},{24,120},{32,0},{40,8},{48,16},{56,24},{64... | collective-permute-start | bytes 2064392 | tf_op jit(solution)/shard_map/ppermute | solution.py:36
  64.7 15.4 %collective-permute-start.9 = (bf16[3,64,1792]{2,1,0:T(8,128)(2,1)S(1)}, bf16[3,64,1792]{2,1,0:T(8,128)(2,1)S(1)}, u32[]{:S(2)}, u32[]{:S(2)}) collective-permute-start(bf16[3,64,1792]{2,1,0:T(8,128)(2,1)S(1)} %pad_maximum_fusion.4), channel_id=1, source_target_pairs={{0,32},{8,40},{16,48},{24,56},{32,64},{40,72},{48,80},{56,88},{64,... | collective-permute-start | bytes 2064392 | tf_op jit(solution)/shard_map/ppermute | solution.py:36
  65.5 14.6 %collective-permute-start.11 = (bf16[3,64,1792]{2,1,0:T(8,128)(2,1)S(1)}, bf16[3,64,1792]{2,1,0:T(8,128)(2,1)S(1)}, u32[]{:S(2)}, u32[]{:S(2)}) collective-permute-start(bf16[3,64,1792]{2,1,0:T(8,128)(2,1)S(1)} %pad_maximum_fusion.5), channel_id=1, source_target_pairs={{0,96},{8,104},{16,112},{24,120},{32,0},{40,8},{48,16},{56,24},{64... | collective-permute-start | bytes 2064392 | tf_op jit(solution)/shard_map/ppermute | solution.py:36
  67.6 13.6 %collective-permute-start.12 = (bf16[3,64,1792]{2,1,0:T(8,128)(2,1)S(1)}, bf16[3,64,1792]{2,1,0:T(8,128)(2,1)S(1)}, u32[]{:S(2)}, u32[]{:S(2)}) collective-permute-start(bf16[3,64,1792]{2,1,0:T(8,128)(2,1)S(1)} %pad_maximum_fusion.6), channel_id=1, source_target_pairs={{0,16},{8,24},{16,0},{24,8},{32,48},{40,56},{48,32},{56,40},{64,80... | collective-permute-start | bytes 2064392 | tf_op jit(solution)/shard_map/ppermute | solution.py:36
  81.8 12.7 %collective-permute-start.14 = (bf16[3,64,1792]{2,1,0:T(8,128)(2,1)S(1)}, bf16[3,64,1792]{2,1,0:T(8,128)(2,1)S(1)}, u32[]{:S(2)}, u32[]{:S(2)}) collective-permute-start(bf16[3,64,1792]{2,1,0:T(8,128)(2,1)S(1)} %pad_maximum_fusion.7), channel_id=1, source_target_pairs={{0,96},{8,104},{16,112},{24,120},{32,0},{40,8},{48,16},{56,24},{64... | collective-permute-start | bytes 2064392 | tf_op jit(solution)/shard_map/ppermute | solution.py:36
  83.3 11.9 %collective-permute-start.13 = (bf16[3,64,1792]{2,1,0:T(8,128)(2,1)S(1)}, bf16[3,64,1792]{2,1,0:T(8,128)(2,1)S(1)}, u32[]{:S(2)}, u32[]{:S(2)}) collective-permute-start(bf16[3,64,1792]{2,1,0:T(8,128)(2,1)S(1)} %pad_maximum_fusion.7), channel_id=1, source_target_pairs={{0,16},{8,24},{16,0},{24,8},{32,48},{40,56},{48,32},{56,40},{64,80... | collective-permute-start | bytes 2064392 | tf_op jit(solution)/shard_map/ppermute | solution.py:36
  84.1 13.0 %collective-permute-start.16 = (bf16[3,64,1792]{2,1,0:T(8,128)(2,1)S(1)}, bf16[3,64,1792]{2,1,0:T(8,128)(2,1)S(1)}, u32[]{:S(2)}, u32[]{:S(2)}) collective-permute-start(bf16[3,64,1792]{2,1,0:T(8,128)(2,1)S(1)} %pad_maximum_fusion.7), channel_id=1, source_target_pairs={{0,32},{8,40},{16,48},{24,56},{32,64},{40,72},{48,80},{56,88},{64,... | collective-permute-start | bytes 2064392 | tf_op jit(solution)/shard_map/ppermute | solution.py:36
  97.2 10.2 %collective-permute-start.15 = (bf16[3,64,1792]{2,1,0:T(8,128)(2,1)S(1)}, bf16[3,64,1792]{2,1,0:T(8,128)(2,1)S(1)}, u32[]{:S(2)}, u32[]{:S(2)}) collective-permute-start(bf16[3,64,1792]{2,1,0:T(8,128)(2,1)S(1)} %get-tuple-element.81), channel_id=1, source_target_pairs={{0,96},{8,104},{16,112},{24,120},{32,0},{40,8},{48,16},{56,24},{64... | collective-permute-start | bytes 2064392 | tf_op jit(solution)/shard_map/ppermute | solution.py:36
  97.3 17.8 %collective-permute-start.20 = (bf16[3,64,1792]{2,1,0:T(8,128)(2,1)S(1)}, bf16[3,64,1792]{2,1,0:T(8,128)(2,1)S(1)}, u32[]{:S(2)}, u32[]{:S(2)}) collective-permute-start(bf16[3,64,1792]{2,1,0:T(8,128)(2,1)S(1)} %get-tuple-element.80), channel_id=1, source_target_pairs={{0,16},{8,24},{16,0},{24,8},{32,48},{40,56},{48,32},{56,40},{64,80... | collective-permute-start | bytes 2064392 | tf_op jit(solution)/shard_map/ppermute | solution.py:36
  98.0 17.2 %collective-permute-start.18 = (bf16[3,64,1792]{2,1,0:T(8,128)(2,1)S(1)}, bf16[3,64,1792]{2,1,0:T(8,128)(2,1)S(1)}, u32[]{:S(2)}, u32[]{:S(2)}) collective-permute-start(bf16[3,64,1792]{2,1,0:T(8,128)(2,1)S(1)} %get-tuple-element.79), channel_id=1, source_target_pairs={{0,32},{8,40},{16,48},{24,56},{32,64},{40,72},{48,80},{56,88},{64,... | collective-permute-start | bytes 2064392 | tf_op jit(solution)/shard_map/ppermute | solution.py:36
  107.4 27.6 %collective-permute-start.17 = (bf16[3,256,1792]{2,1,0:T(8,128)(2,1)S(1)}, bf16[3,256,1792]{2,1,0:T(8,128)(2,1)S(1)}, u32[]{:S(2)}, u32[]{:S(2)}) collective-permute-start(bf16[3,256,1792]{2,1,0:T(8,128)(2,1)S(1)} %maximum_maximum_fusion.refs_0_), channel_id=1, source_target_pairs={{0,8},{8,0},{16,24},{24,16},{32,40},{40,32},{48,56},{56,48},{64,72... | collective-permute-start | bytes 8257544 | tf_op jit(solution)/shard_map/ppermute | solution.py:36
  115.2 12.2 %copy-start.2 = (bf16[512,3584]{1,0:T(8,128)(2,1)S(1)}, bf16[512,3584]{1,0:T(8,128)(2,1)}, u32[]{:S(2)}) copy-start(bf16[512,3584]{1,0:T(8,128)(2,1)} %refs_4_.7) | copy-start | bytes 11010052
  115.2 7.8 %collective-permute-start.21 = (bf16[3,64,640]{2,1,0:T(8,128)(2,1)S(1)}, bf16[3,64,640]{2,1,0:T(8,128)(2,1)S(1)}, u32[]{:S(2)}, u32[]{:S(2)}) collective-permute-start(bf16[3,64,640]{2,1,0:T(8,128)(2,1)S(1)} %pad_maximum_fusion.9), channel_id=1, source_target_pairs={{0,32},{8,40},{16,48},{24,56},{32,64},{40,72},{48,80},{56,88},{64,... | collective-permute-start | bytes 737288 | tf_op jit(solution)/shard_map/ppermute | solution.py:36
  115.4 7.7 %collective-permute-start.22 = (bf16[3,64,640]{2,1,0:T(8,128)(2,1)S(1)}, bf16[3,64,640]{2,1,0:T(8,128)(2,1)S(1)}, u32[]{:S(2)}, u32[]{:S(2)}) collective-permute-start(bf16[3,64,640]{2,1,0:T(8,128)(2,1)S(1)} %slice.114), channel_id=1, source_target_pairs={{0,96},{8,104},{16,112},{24,120},{32,0},{40,8},{48,16},{56,24},{64... | collective-permute-start | bytes 737288 | tf_op jit(solution)/shard_map/ppermute | solution.py:36
  118.1 9.2 %copy-start = (bf16[512,3584]{1,0:T(8,128)(2,1)S(1)}, bf16[512,3584]{1,0:T(8,128)(2,1)}, u32[]{:S(2)}) copy-start(bf16[512,3584]{1,0:T(8,128)(2,1)} %refs_3_.7) | copy-start | bytes 11010052
  118.1 4.9 %collective-permute-start.19 = (bf16[3,64,512]{2,1,0:T(8,128)(2,1)S(1)}, bf16[3,64,512]{2,1,0:T(8,128)(2,1)S(1)}, u32[]{:S(2)}, u32[]{:S(2)}) collective-permute-start(bf16[3,64,512]{2,1,0:T(8,128)(2,1)S(1)} %slice.111), channel_id=1, source_target_pairs={{0,16},{8,24},{16,0},{24,8},{32,48},{40,56},{48,32},{56,40},{64,80... | collective-permute-start | bytes 589832 | tf_op jit(solution)/shard_map/ppermute | solution.py:36
  123.1 11.9 %collective-permute-start.23 = (bf16[3,192,1792]{2,1,0:T(8,128)(2,1)S(1)}, bf16[3,192,1792]{2,1,0:T(8,128)(2,1)S(1)}, u32[]{:S(2)}, u32[]{:S(2)}) collective-permute-start(bf16[3,192,1792]{2,1,0:T(8,128)(2,1)S(1)} %pad_maximum_fusion.refs_1_), channel_id=1, source_target_pairs={{0,8},{8,0},{16,24},{24,16},{32,40},{40,32},{48,56},{56,48},{64,72... | collective-permute-start | bytes 6193160 | tf_op jit(solution)/shard_map/ppermute | solution.py:36
  127.3 7.7 %collective-permute-start.24 = (bf16[3,64,1792]{2,1,0:T(8,128)(2,1)S(1)}, bf16[3,64,1792]{2,1,0:T(8,128)(2,1)S(1)}, u32[]{:S(2)}, u32[]{:S(2)}) collective-permute-start(bf16[3,64,1792]{2,1,0:T(8,128)(2,1)S(1)} %pad_maximum_fusion.8.refs_2_), channel_id=1, source_target_pairs={{0,8},{8,0},{16,24},{24,16},{32,40},{40,32},{48,56},{56,48},{64,72... | collective-permute-start | bytes 2064392 | tf_op jit(solution)/shard_map/ppermute | solution.py:36
  140.3 15.8 %all-to-all-start.1 = ((bf16[8,64,512]{2,1,0:T(8,128)(2,1)}), bf16[8,64,512]{2,1,0:T(8,128)(2,1)}, u32[]{:S(2)}, u32[]{:S(2)}) async-start(bf16[8,64,512]{2,1,0:T(8,128)(2,1)} %copy-done.9), calls=%async_computation.1 | async-start | bytes 1048576 | tf_op jit(solution)/shard_map/all_to_all | solution.py:391
  (6 other events, 9.2 us)

commit v5 on v4

--- a/solution.py
+++ b/solution.py
@@ -202,7 +202,7 @@
         else:
             acc[...] = term
             for b in range(8):
-                out[b] = acc[place(pos, b), :].astype(BF)
+                out[b] = acc[place(pos, b), :]
 
 
 def part(pos, pieces, core, half, terms=None, weights=None, last=False):
@@ -224,7 +224,7 @@
             args.append(before)
         if last:
             out_specs.append(whole((8, BLK, 512)))
-            out_shape.append(jax.ShapeDtypeStruct((8, BLK, 512), BF))
+            out_shape.append(jax.ShapeDtypeStruct((8, BLK, 512), F32))
         else:
             out_specs.append(square)
             out_shape.append(jax.ShapeDtypeStruct((512, 512), F32))

time: 158 us -> 163 us (1.032)
  waiting for transfers between devices: 58.4 us -> 63.1 us
    all_to_all x1, waiting for transfers between devices: 0.01 us -> 4.71 us  [shards(): grad_tokens = total_of(lax.all_to_all(terms, 'gy', 0, 0, tiled=True))]
  transfers between devices with their start and end apart: 27 -> 27, of which waited for: 12 -> 13; matrix products, arithmetic and copies ran while one was open for 4% -> 4% of each run, Pallas kernels for 14% -> 14%
where the time goes in v5:
time: 163 us
  waiting for transfers between devices  63.1 us (39%)
  starting transfers between devices  47.1 us (29%)
  Pallas kernels  38.7 us (24%)
  local copies, waits for them, and re-layouts  10.8 us (7%)
  other arithmetic  2.14 us (1%)
    ppermute x25, waiting for transfers between devices, send(): return lax.ppermute(a, 'gx', pairs)  51 us
    ppermute x25, starting transfers between devices, send(): return lax.ppermute(a, 'gx', pairs)  34.1 us
    pallas_call x6, Pallas kernels, part(): pl.pallas_call(functools.partial(part_kernel, half, bool(terms), bool(wei...  19.3 us
    pallas_call x2, Pallas kernels, sums(): pl.pallas_call(functools.partial(sums_kernel, part), grid_spec=pltpu.Pref...  14.5 us
    all_to_all x1, starting transfers between devices, shards(): blocks = lax.all_to_all(spread(tokens, out_grad), 'gy', 0, 0, tiled=True)  8.33 us
    all_to_all x1, waiting for transfers between devices, shards(): blocks = lax.all_to_all(spread(tokens, out_grad), 'gy', 0, 0, tiled=True)  7.4 us
    dynamic_slice x3, local copies, waits for them, and re-layouts, shards(): lax.dynamic_slice_in_dim(w, far_half, HALF, axis)  5.69 us
    unnamed x22, local copies, waits for them, and re-layouts  4.87 us
  transfers between devices with their start and end apart: 27, of which 13 were waited for; matrix products, arithmetic and copies ran while one was open for 4% of the time, Pallas kernels for 14%

profile of v5, /device:TPU:1, one launch (start us, length us, event | category | flops | bytes accessed | tf_op | source)
XLA Modules:
  0.0 162.9 jit_solution(15725057590378344322)
XLA Ops:
  0.6 1.9 %shard_map.84 = bf16[8,64,1024]{2,1,0:T(8,128)(2,1)} custom-call(bf16[64,512]{1,0:T(8,128)(2,1)} %tokens.1, bf16[64,512]{1,0:T(8,128)(2,1)} %out_grad.1), custom_call_target="tpu_custom_call" | custom-call | bytes 1048576 | tf_op jit(solution)/shard_map/pallas_call | solution.py:64
  2.6 8.3 %all-to-all-start = ((bf16[8,64,1024]{2,1,0:T(8,128)(2,1)}), bf16[8,64,1024]{2,1,0:T(8,128)(2,1)S(1)}, u32[]{:S(2)}, u32[]{:S(2)}) async-start(bf16[8,64,1024]{2,1,0:T(8,128)(2,1)} %shard_map.84), calls=%async_computation | async-start | bytes 2097152 | tf_op jit(solution)/shard_map/all_to_all | solution.py:370
  10.9 3.0 %constant_dynamic-slice_fusion.2 = bf16[512,1792]{1,0:T(8,128)(2,1)} fusion(bf16[512,3584]{1,0:T(8,128)(2,1)} %refs_3_.7, s32[]{:T(128)S(6)} %select_n.27), kind=kLoop, calls=%fused_computation.31 | loop fusion | bytes 3670020 | tf_op jit(solution)/shard_map/dynamic_slice | solution.py:373
  19.0 7.4 %all-to-all-done.blocks = bf16[8,64,1024]{2,1,0:T(8,128)(2,1)S(1)} async-done(((bf16[8,64,1024]{2,1,0:T(8,128)(2,1)}), bf16[8,64,1024]{2,1,0:T(8,128)(2,1)S(1)}, u32[]{:S(2)}, u32[]{:S(2)}) %all-to-all-start) | async-done | bytes 1048608 | tf_op jit(solution)/shard_map/all_to_all | solution.py:370
  27.2 1.4 collective-permute-start
  28.6 2.3 %collective-permute-done.tg_sib = bf16[512,1024]{1,0:T(8,128)(2,1)S(1)} collective-permute-done((bf16[512,1024]{1,0:T(8,128)(2,1)S(1)}, bf16[512,1024]{1,0:T(8,128)(2,1)S(1)}, u32[]{:S(2)}, u32[]{:S(2)}) %collective-permute-start) | collective-permute-done | bytes 1048608 | tf_op jit(solution)/shard_map/ppermute | solution.py:36
  30.9 7.6 %shard_map.87 = (f32[3,64,1792]{2,1,0:T(8,128)S(1)}, f32[3,64,1792]{2,1,0:T(8,128)S(1)}, f32[3,64,1792]{2,1,0:T(8,128)S(1)}, bf16[3,64,512]{2,1,0:T(8,128)(2,1)S...) custom-call(s32[3]{0:T(128)S(1)} %pad_add_fusion.pos, ...), custom_call_target="tpu_custom_call" | custom-call | flops 2818572288 | bytes 20971520 | tf_op jit(solution)/shard_map/pallas_call | solution.py:127
  39.8 1.5 collective-permute-start.6
  42.1 4.7 %collective-permute-done.4.rz = bf16[3,64,512]{2,1,0:T(8,128)(2,1)S(1)} collective-permute-done((bf16[3,64,512]{2,1,0:T(8,128)(2,1)S(1)}, bf16[3,64,512]{2,1,0:T(8,128)(2,1)S(1)}, u32[]{:S(2)}, u32[]{:S(2)}) %collective-permute-start.4) | collective-permute-done | bytes 196640 | tf_op jit(solution)/shard_map/ppermute | solution.py:36
  49.0 1.8 %collective-permute-start.10 = (bf16[3,64,1792]{2,1,0:T(8,128)(2,1)S(1)}, bf16[3,64,1792]{2,1,0:T(8,128)(2,1)S(1)}, u32[]{:S(2)}, u32[]{:S(2)}) collective-permute-start(bf16[3,64,1792]{2,1,0:T(8,128)(2,1)S(1)} %get-tuple-element.49), channel_id=1, source_target_pairs={{0,96},{8,104},{16,112},{24,120},{32,0},{40,8},{48,16},{56,24},{64... | collective-permute-start | bytes 2064392 | tf_op jit(solution)/shard_map/ppermute | solution.py:36
  50.8 6.9 %shard_map.86 = (f32[3,64,1792]{2,1,0:T(8,128)S(1)}, f32[3,64,1792]{2,1,0:T(8,128)S(1)}, f32[3,64,1792]{2,1,0:T(8,128)S(1)}, f32[3,64,1792]{2,1,0:T(8,128)S(1)}) custom-call(s32[3]{0:T(128)S(1)} %pad_add_fusion.pos, bf16[512,1024]{1,0:T(8,128)(2,1)S(1)} %get-tuple-element.37.tg.refs_6_.refs_7_.refs_4_, bf16[512,1024]{1,0:T(8,128)(2,1)S(1)} %collective-permute-done.tg_sib, ...), custom_call_target="tpu_custom_call" | custom-call | flops 2818572288 | bytes 20971520 | tf_op jit(solution)/shard_map/pallas_call | solution.py:127
  57.8 6.1 %collective-permute-done.7 = bf16[3,64,1792]{2,1,0:T(8,128)(2,1)S(1)} collective-permute-done((bf16[3,64,1792]{2,1,0:T(8,128)(2,1)S(1)}, bf16[3,64,1792]{2,1,0:T(8,128)(2,1)S(1)}, u32[]{:S(2)}, u32[]{:S(2)}) %collective-permute-start.7) | collective-permute-done | bytes 688160 | tf_op jit(solution)/shard_map/ppermute | solution.py:36
  65.5 2.1 %collective-permute-start.11 = (bf16[3,64,1792]{2,1,0:T(8,128)(2,1)S(1)}, bf16[3,64,1792]{2,1,0:T(8,128)(2,1)S(1)}, u32[]{:S(2)}, u32[]{:S(2)}) collective-permute-start(bf16[3,64,1792]{2,1,0:T(8,128)(2,1)S(1)} %pad_maximum_fusion.5), channel_id=1, source_target_pairs={{0,96},{8,104},{16,112},{24,120},{32,0},{40,8},{48,16},{56,24},{64... | collective-permute-start | bytes 2064392 | tf_op jit(solution)/shard_map/ppermute | solution.py:36
  68.4 11.7 %collective-permute-done.9 = bf16[3,64,1792]{2,1,0:T(8,128)(2,1)S(1)} collective-permute-done((bf16[3,64,1792]{2,1,0:T(8,128)(2,1)S(1)}, bf16[3,64,1792]{2,1,0:T(8,128)(2,1)S(1)}, u32[]{:S(2)}, u32[]{:S(2)}) %collective-permute-start.9) | collective-permute-done | bytes 688160 | tf_op jit(solution)/shard_map/ppermute | solution.py:36
  81.8 1.4 collective-permute-start.14
  84.2 10.4 %collective-permute-done.14 = bf16[3,64,1792]{2,1,0:T(8,128)(2,1)S(1)} collective-permute-done((bf16[3,64,1792]{2,1,0:T(8,128)(2,1)S(1)}, bf16[3,64,1792]{2,1,0:T(8,128)(2,1)S(1)}, u32[]{:S(2)}, u32[]{:S(2)}) %collective-permute-start.14) | collective-permute-done | bytes 688160 | tf_op jit(solution)/shard_map/ppermute | solution.py:36
  95.3 1.8 %collective-permute-done.16 = bf16[3,64,1792]{2,1,0:T(8,128)(2,1)S(1)} collective-permute-done((bf16[3,64,1792]{2,1,0:T(8,128)(2,1)S(1)}, bf16[3,64,1792]{2,1,0:T(8,128)(2,1)S(1)}, u32[]{:S(2)}, u32[]{:S(2)}) %collective-permute-start.16) | collective-permute-done | bytes 688160 | tf_op jit(solution)/shard_map/ppermute | solution.py:36
  99.5 7.9 %collective-permute-done.15 = bf16[3,64,1792]{2,1,0:T(8,128)(2,1)S(1)} collective-permute-done((bf16[3,64,1792]{2,1,0:T(8,128)(2,1)S(1)}, bf16[3,64,1792]{2,1,0:T(8,128)(2,1)S(1)}, u32[]{:S(2)}, u32[]{:S(2)}) %collective-permute-start.15) | collective-permute-done | bytes 688160 | tf_op jit(solution)/shard_map/ppermute | solution.py:36
  107.4 7.7 %collective-permute-start.17 = (bf16[3,256,1792]{2,1,0:T(8,128)(2,1)S(1)}, bf16[3,256,1792]{2,1,0:T(8,128)(2,1)S(1)}, u32[]{:S(2)}, u32[]{:S(2)}) collective-permute-start(bf16[3,256,1792]{2,1,0:T(8,128)(2,1)S(1)} %maximum_maximum_fusion.refs_0_), channel_id=1, source_target_pairs={{0,8},{8,0},{16,24},{24,16},{32,40},{40,32},{48,56},{56,48},{64,72... | collective-permute-start | bytes 8257544 | tf_op jit(solution)/shard_map/ppermute | solution.py:36
  115.4 2.7 %collective-permute-start.22 = (bf16[3,64,640]{2,1,0:T(8,128)(2,1)S(1)}, bf16[3,64,640]{2,1,0:T(8,128)(2,1)S(1)}, u32[]{:S(2)}, u32[]{:S(2)}) collective-permute-start(bf16[3,64,640]{2,1,0:T(8,128)(2,1)S(1)} %slice.114), channel_id=1, source_target_pairs={{0,96},{8,104},{16,112},{24,120},{32,0},{40,8},{48,16},{56,24},{64... | collective-permute-start | bytes 737288 | tf_op jit(solution)/shard_map/ppermute | solution.py:36
  118.8 4.2 %collective-permute-done.19 = bf16[3,64,512]{2,1,0:T(8,128)(2,1)S(1)} collective-permute-done((bf16[3,64,512]{2,1,0:T(8,128)(2,1)S(1)}, bf16[3,64,512]{2,1,0:T(8,128)(2,1)S(1)}, u32[]{:S(2)}, u32[]{:S(2)}) %collective-permute-start.19) | collective-permute-done | bytes 196640 | tf_op jit(solution)/shard_map/ppermute | solution.py:36
  123.1 4.2 %collective-permute-start.23 = (bf16[3,192,1792]{2,1,0:T(8,128)(2,1)S(1)}, bf16[3,192,1792]{2,1,0:T(8,128)(2,1)S(1)}, u32[]{:S(2)}, u32[]{:S(2)}) collective-permute-start(bf16[3,192,1792]{2,1,0:T(8,128)(2,1)S(1)} %pad_maximum_fusion.refs_1_), channel_id=1, source_target_pairs={{0,8},{8,0},{16,24},{24,16},{32,40},{40,32},{48,56},{56,48},{64,72... | collective-permute-start | bytes 6193160 | tf_op jit(solution)/shard_map/ppermute | solution.py:36
  127.3 3.8 %shard_map.89 = (f32[512,512]{1,0:T(8,128)S(1)}, bf16[512,3584]{1,0:T(8,128)(2,1)}, bf16[512,3584]{1,0:T(8,128)(2,1)}, bf16[3584,512]{1,0:T(8,128)(2,1)}) custom-call(s32[3]{0:T(128)S(1)} %pad_add_fusion.pos, bf16[3,256,1792]{2,1,0:T(8,128)(2,1)S(1)} %maximum_maximum_fusion.refs_0_, bf16[3,192,1792]{2,1,0:T(8,128)(2,1)S(1)} %pad_maximum_fusion.refs_1_, ...), custom_call_target="tpu_custom_call" | custom-call | flops 2348810240 | bytes 8388608 | tf_op jit(solution)/shard_map/pallas_call | solution.py:246
  131.2 3.8 %shard_map.90 = (f32[512,512]{1,0:T(8,128)S(1)}, bf16[512,3584]{1,0:T(8,128)(2,1)}, bf16[512,3584]{1,0:T(8,128)(2,1)}, bf16[3584,512]{1,0:T(8,128)(2,1)}) custom-call(s32[3]{0:T(128)S(1)} %pad_add_fusion.pos, bf16[3,256,1792]{2,1,0:T(8,128)(2,1)S(1)} %maximum_maximum_fusion.refs_0_, ...), custom_call_target="tpu_custom_call", output_to_operand_aliasing={{1}: (9, {}), {2}: (10, {}), {3}: (11, {})} | custom-call | flops 2348810240 | bytes 8388608 | tf_op jit(solution)/shard_map/pallas_call | solution.py:246
  135.0 2.2 %shard_map.91.refs_5_ = f32[512,512]{1,0:T(8,128)S(1)} custom-call(s32[3]{0:T(128)S(1)} %pad_add_fusion.pos, bf16[3,256,1792]{2,1,0:T(8,128)(2,1)S(1)} %collective-permute-done.17.refs_0_, bf16[3,192,1792]{2,1,0:T(8,128)(2,1)S(1)} %collective-permute-done.23.refs_1_, bf16[3,64,1792]{2,1,0:T(8,128)(2,1)S(1)} %collective-permute-done.24.refs_2_, ...), custom_call_target="tpu_custom_call" | custom-call | flops 939524096 | bytes 8388608 | tf_op jit(solution)/shard_map/pallas_call | solution.py:246
  137.2 2.3 %shard_map.92 = f32[8,64,512]{2,1,0:T(8,128)S(1)} custom-call(s32[3]{0:T(128)S(1)} %pad_add_fusion.pos, bf16[3,256,1792]{2,1,0:T(8,128)(2,1)S(1)} %collective-permute-done.17.refs_0_, bf16[3,192,1792]{2,1,0:T(8,128)(2,1)S(1)} %collective-permute-done.23.refs_1_, bf16[3,64,1792]{2,1,0:T(8,128)(2,1)S(1)} %collective-permute-done.24.refs_2_, ...), custom_call_target="tpu_custom_call" | custom-call | flops 939524096 | bytes 8388608 | tf_op jit(solution)/shard_map/pallas_call | solution.py:246
  140.5 4.7 %all-to-all-start.1 = ((f32[8,64,512]{2,1,0:T(8,128)}), f32[8,64,512]{2,1,0:T(8,128)}, u32[]{:S(2)}, u32[]{:S(2)}) async-start(f32[8,64,512]{2,1,0:T(8,128)} %copy-done.9), calls=%async_computation.1 | async-start | bytes 2097152 | tf_op jit(solution)/shard_map/all_to_all | solution.py:391
  146.5 1.6 copy-done.6
  149.1 3.6 %shard_map.94 = (bf16[512,3584]{1,0:T(8,128)(2,1)}, bf16[512,3584]{1,0:T(8,128)(2,1)}, bf16[3584,512]{1,0:T(8,128)(2,1)}) custom-call(s32[3]{0:T(128)S(1)} %pad_add_fusion.pos, bf16[3,256,1792]{2,1,0:T(8,128)(2,1)S(1)} %collective-permute-done.17.refs_0_, ...), custom_call_target="tpu_custom_call", output_to_operand_aliasing={{0}: (6, {}), {1}: (7, {}), {2}: (8, {})} | custom-call | flops 1409286144 | bytes 8388608 | tf_op jit(solution)/shard_map/pallas_call | solution.py:246
  152.7 3.6 %shard_map.95 = (bf16[512,3584]{1,0:T(8,128)(2,1)}, bf16[512,3584]{1,0:T(8,128)(2,1)}, bf16[3584,512]{1,0:T(8,128)(2,1)}) custom-call(s32[3]{0:T(128)S(1)} %pad_add_fusion.pos, bf16[3,256,1792]{2,1,0:T(8,128)(2,1)S(1)} %collective-permute-done.17.refs_0_, ...), custom_call_target="tpu_custom_call", output_to_operand_aliasing={{0}: (6, {}), {1}: (7, {}), {2}: (8, {})} | custom-call | flops 1409286144 | bytes 8388608 | tf_op jit(solution)/shard_map/pallas_call | solution.py:246
  156.3 4.7 %all-to-all-done.1.terms = f32[8,64,512]{2,1,0:T(8,128)} async-done(((f32[8,64,512]{2,1,0:T(8,128)}), f32[8,64,512]{2,1,0:T(8,128)}, u32[]{:S(2)}, u32[]{:S(2)}) %all-to-all-start.1) | async-done | bytes 1048608 | tf_op jit(solution)/shard_map/all_to_all | solution.py:391
  161.0 1.9 %shard_map.93 = bf16[64,512]{1,0:T(8,128)(2,1)} custom-call(f32[8,64,512]{2,1,0:T(8,128)} %all-to-all-done.1.terms), custom_call_target="tpu_custom_call" | custom-call | flops 262144 | bytes 524288 | tf_op jit(solution)/shard_map/pallas_call | solution.py:270
  (84 shorter events, 22.7 us)
Async XLA Ops:
  2.6 23.8 %all-to-all-start = ((bf16[8,64,1024]{2,1,0:T(8,128)(2,1)}), bf16[8,64,1024]{2,1,0:T(8,128)(2,1)S(1)}, u32[]{:S(2)}, u32[]{:S(2)}) async-start(bf16[8,64,1024]{2,1,0:T(8,128)(2,1)} %shard_map.84), calls=%async_computation | async-start | bytes 2097152 | tf_op jit(solution)/shard_map/all_to_all | solution.py:370
  10.9 4.0 %copy-start.1 = (bf16[512,3584]{1,0:T(8,128)(2,1)S(1)}, bf16[512,3584]{1,0:T(8,128)(2,1)}, u32[]{:S(2)}) copy-start(bf16[512,3584]{1,0:T(8,128)(2,1)} %refs_4_.7) | copy-start | bytes 11010052
  13.9 14.7 %collective-permute-start.1 = (bf16[512,1792]{1,0:T(8,128)(2,1)}, bf16[512,1792]{1,0:T(8,128)(2,1)S(1)}, u32[]{:S(2)}, u32[]{:S(2)}) collective-permute-start(bf16[512,1792]{1,0:T(8,128)(2,1)} %constant_dynamic-slice_fusion.2), channel_id=1, source_target_pairs={{0,8},{8,0},{16,24},{24,16},{32,40},{40,32},{48,56},{56,48},{64,72... | collective-permute-start | bytes 5505032 | tf_op jit(solution)/shard_map/ppermute | solution.py:36
  16.2 12.4 %collective-permute-start.2 = (bf16[512,1792]{1,0:T(8,128)(2,1)}, bf16[512,1792]{1,0:T(8,128)(2,1)}, u32[]{:S(2)}, u32[]{:S(2)}) collective-permute-start(bf16[512,1792]{1,0:T(8,128)(2,1)} %constant_dynamic-slice_fusion.1), channel_id=1, source_target_pairs={{0,8},{8,0},{16,24},{24,16},{32,40},{40,32},{48,56},{56,48},{64,72... | collective-permute-start | bytes 5505032 | tf_op jit(solution)/shard_map/ppermute | solution.py:36
  17.6 11.1 %collective-permute-start.3 = (bf16[1792,512]{1,0:T(8,128)(2,1)}, bf16[1792,512]{1,0:T(8,128)(2,1)}, u32[]{:S(2)}, u32[]{:S(2)}) collective-permute-start(bf16[1792,512]{1,0:T(8,128)(2,1)} %constant_dynamic-slice_fusion), channel_id=1, source_target_pairs={{0,8},{8,0},{16,24},{24,16},{32,40},{40,32},{48,56},{56,48},{64,72... | collective-permute-start | bytes 5505032 | tf_op jit(solution)/shard_map/ppermute | solution.py:36
  27.2 103.9 %copy-start.3 = (bf16[512,1024]{1,0:T(8,128)(2,1)}, bf16[512,1024]{1,0:T(8,128)(2,1)S(1)}, u32[]{:S(2)}) copy-start(bf16[512,1024]{1,0:T(8,128)(2,1)S(1)} %get-tuple-element.37.tg.refs_6_.refs_7_.refs_4_) | copy-start | bytes 3145732
  27.2 103.9 %copy-start.7 = (bf16[512,512]{1,0:T(8,128)(2,1)}, bf16[512,512]{1,0:T(8,128)(2,1)S(1)}, u32[]{:S(2)}) copy-start(bf16[512,512]{1,0:T(8,128)(2,1)S(1)} %get-tuple-element.55.refs_5_.refs_6_.refs_3_) | copy-start | bytes 1572868
  27.2 3.7 %collective-permute-start = (bf16[512,1024]{1,0:T(8,128)(2,1)S(1)}, bf16[512,1024]{1,0:T(8,128)(2,1)S(1)}, u32[]{:S(2)}, u32[]{:S(2)}) collective-permute-start(bf16[512,1024]{1,0:T(8,128)(2,1)S(1)} %get-tuple-element.37.tg.refs_6_.refs_7_.refs_4_), channel_id=1, source_target_pairs={{0,8},{8,0},{16,24},{24,16},{32,40},{40,32},{48,56},{56,48},{64,72... | collective-permute-start | bytes 3145736 | tf_op jit(solution)/shard_map/ppermute | solution.py:36
  38.6 8.4 %collective-permute-start.5 = (bf16[3,64,640]{2,1,0:T(8,128)(2,1)S(1)}, bf16[3,64,640]{2,1,0:T(8,128)(2,1)S(1)}, u32[]{:S(2)}, u32[]{:S(2)}) collective-permute-start(bf16[3,64,640]{2,1,0:T(8,128)(2,1)S(1)} %get-tuple-element.44), channel_id=1, source_target_pairs={{0,32},{8,40},{16,48},{24,56},{32,64},{40,72},{48,80},{56,88},{64,... | collective-permute-start | bytes 737288 | tf_op jit(solution)/shard_map/ppermute | solution.py:36
  39.8 7.2 %collective-permute-start.6 = (bf16[3,64,640]{2,1,0:T(8,128)(2,1)S(1)}, bf16[3,64,640]{2,1,0:T(8,128)(2,1)S(1)}, u32[]{:S(2)}, u32[]{:S(2)}) collective-permute-start(bf16[3,64,640]{2,1,0:T(8,128)(2,1)S(1)} %get-tuple-element.45), channel_id=1, source_target_pairs={{0,96},{8,104},{16,112},{24,120},{32,0},{40,8},{48,16},{56,24},{64... | collective-permute-start | bytes 737288 | tf_op jit(solution)/shard_map/ppermute | solution.py:36
  41.3 5.5 %collective-permute-start.4 = (bf16[3,64,512]{2,1,0:T(8,128)(2,1)S(1)}, bf16[3,64,512]{2,1,0:T(8,128)(2,1)S(1)}, u32[]{:S(2)}, u32[]{:S(2)}) collective-permute-start(bf16[3,64,512]{2,1,0:T(8,128)(2,1)S(1)} %get-tuple-element.43), channel_id=1, source_target_pairs={{0,16},{8,24},{16,0},{24,8},{32,48},{40,56},{48,32},{56,40},{64,80... | collective-permute-start | bytes 589832 | tf_op jit(solution)/shard_map/ppermute | solution.py:36
  47.3 16.6 %collective-permute-start.7 = (bf16[3,64,1792]{2,1,0:T(8,128)(2,1)S(1)}, bf16[3,64,1792]{2,1,0:T(8,128)(2,1)S(1)}, u32[]{:S(2)}, u32[]{:S(2)}) collective-permute-start(bf16[3,64,1792]{2,1,0:T(8,128)(2,1)S(1)} %get-tuple-element.46), channel_id=1, source_target_pairs={{0,32},{8,40},{16,48},{24,56},{32,64},{40,72},{48,80},{56,88},{64,... | collective-permute-start | bytes 2064392 | tf_op jit(solution)/shard_map/ppermute | solution.py:36
  48.2 15.7 %collective-permute-start.8 = (bf16[3,64,1792]{2,1,0:T(8,128)(2,1)S(1)}, bf16[3,64,1792]{2,1,0:T(8,128)(2,1)S(1)}, u32[]{:S(2)}, u32[]{:S(2)}) collective-permute-start(bf16[3,64,1792]{2,1,0:T(8,128)(2,1)S(1)} %get-tuple-element.47), channel_id=1, source_target_pairs={{0,16},{8,24},{16,0},{24,8},{32,48},{40,56},{48,32},{56,40},{64,80... | collective-permute-start | bytes 2064392 | tf_op jit(solution)/shard_map/ppermute | solution.py:36
  49.0 15.1 %collective-permute-start.10 = (bf16[3,64,1792]{2,1,0:T(8,128)(2,1)S(1)}, bf16[3,64,1792]{2,1,0:T(8,128)(2,1)S(1)}, u32[]{:S(2)}, u32[]{:S(2)}) collective-permute-start(bf16[3,64,1792]{2,1,0:T(8,128)(2,1)S(1)} %get-tuple-element.49), channel_id=1, source_target_pairs={{0,96},{8,104},{16,112},{24,120},{32,0},{40,8},{48,16},{56,24},{64... | collective-permute-start | bytes 2064392 | tf_op jit(solution)/shard_map/ppermute | solution.py:36
  64.7 15.4 %collective-permute-start.9 = (bf16[3,64,1792]{2,1,0:T(8,128)(2,1)S(1)}, bf16[3,64,1792]{2,1,0:T(8,128)(2,1)S(1)}, u32[]{:S(2)}, u32[]{:S(2)}) collective-permute-start(bf16[3,64,1792]{2,1,0:T(8,128)(2,1)S(1)} %pad_maximum_fusion.4), channel_id=1, source_target_pairs={{0,32},{8,40},{16,48},{24,56},{32,64},{40,72},{48,80},{56,88},{64,... | collective-permute-start | bytes 2064392 | tf_op jit(solution)/shard_map/ppermute | solution.py:36
  65.5 14.6 %collective-permute-start.11 = (bf16[3,64,1792]{2,1,0:T(8,128)(2,1)S(1)}, bf16[3,64,1792]{2,1,0:T(8,128)(2,1)S(1)}, u32[]{:S(2)}, u32[]{:S(2)}) collective-permute-start(bf16[3,64,1792]{2,1,0:T(8,128)(2,1)S(1)} %pad_maximum_fusion.5), channel_id=1, source_target_pairs={{0,96},{8,104},{16,112},{24,120},{32,0},{40,8},{48,16},{56,24},{64... | collective-permute-start | bytes 2064392 | tf_op jit(solution)/shard_map/ppermute | solution.py:36
  67.6 13.6 %collective-permute-start.12 = (bf16[3,64,1792]{2,1,0:T(8,128)(2,1)S(1)}, bf16[3,64,1792]{2,1,0:T(8,128)(2,1)S(1)}, u32[]{:S(2)}, u32[]{:S(2)}) collective-permute-start(bf16[3,64,1792]{2,1,0:T(8,128)(2,1)S(1)} %pad_maximum_fusion.6), channel_id=1, source_target_pairs={{0,16},{8,24},{16,0},{24,8},{32,48},{40,56},{48,32},{56,40},{64,80... | collective-permute-start | bytes 2064392 | tf_op jit(solution)/shard_map/ppermute | solution.py:36
  81.8 12.7 %collective-permute-start.14 = (bf16[3,64,1792]{2,1,0:T(8,128)(2,1)S(1)}, bf16[3,64,1792]{2,1,0:T(8,128)(2,1)S(1)}, u32[]{:S(2)}, u32[]{:S(2)}) collective-permute-start(bf16[3,64,1792]{2,1,0:T(8,128)(2,1)S(1)} %pad_maximum_fusion.7), channel_id=1, source_target_pairs={{0,96},{8,104},{16,112},{24,120},{32,0},{40,8},{48,16},{56,24},{64... | collective-permute-start | bytes 2064392 | tf_op jit(solution)/shard_map/ppermute | solution.py:36
  83.3 11.9 %collective-permute-start.13 = (bf16[3,64,1792]{2,1,0:T(8,128)(2,1)S(1)}, bf16[3,64,1792]{2,1,0:T(8,128)(2,1)S(1)}, u32[]{:S(2)}, u32[]{:S(2)}) collective-permute-start(bf16[3,64,1792]{2,1,0:T(8,128)(2,1)S(1)} %pad_maximum_fusion.7), channel_id=1, source_target_pairs={{0,16},{8,24},{16,0},{24,8},{32,48},{40,56},{48,32},{56,40},{64,80... | collective-permute-start | bytes 2064392 | tf_op jit(solution)/shard_map/ppermute | solution.py:36
  84.1 13.0 %collective-permute-start.16 = (bf16[3,64,1792]{2,1,0:T(8,128)(2,1)S(1)}, bf16[3,64,1792]{2,1,0:T(8,128)(2,1)S(1)}, u32[]{:S(2)}, u32[]{:S(2)}) collective-permute-start(bf16[3,64,1792]{2,1,0:T(8,128)(2,1)S(1)} %pad_maximum_fusion.7), channel_id=1, source_target_pairs={{0,32},{8,40},{16,48},{24,56},{32,64},{40,72},{48,80},{56,88},{64,... | collective-permute-start | bytes 2064392 | tf_op jit(solution)/shard_map/ppermute | solution.py:36
  97.2 10.2 %collective-permute-start.15 = (bf16[3,64,1792]{2,1,0:T(8,128)(2,1)S(1)}, bf16[3,64,1792]{2,1,0:T(8,128)(2,1)S(1)}, u32[]{:S(2)}, u32[]{:S(2)}) collective-permute-start(bf16[3,64,1792]{2,1,0:T(8,128)(2,1)S(1)} %get-tuple-element.81), channel_id=1, source_target_pairs={{0,96},{8,104},{16,112},{24,120},{32,0},{40,8},{48,16},{56,24},{64... | collective-permute-start | bytes 2064392 | tf_op jit(solution)/shard_map/ppermute | solution.py:36
  97.3 17.8 %collective-permute-start.20 = (bf16[3,64,1792]{2,1,0:T(8,128)(2,1)S(1)}, bf16[3,64,1792]{2,1,0:T(8,128)(2,1)S(1)}, u32[]{:S(2)}, u32[]{:S(2)}) collective-permute-start(bf16[3,64,1792]{2,1,0:T(8,128)(2,1)S(1)} %get-tuple-element.80), channel_id=1, source_target_pairs={{0,16},{8,24},{16,0},{24,8},{32,48},{40,56},{48,32},{56,40},{64,80... | collective-permute-start | bytes 2064392 | tf_op jit(solution)/shard_map/ppermute | solution.py:36
  98.0 17.2 %collective-permute-start.18 = (bf16[3,64,1792]{2,1,0:T(8,128)(2,1)S(1)}, bf16[3,64,1792]{2,1,0:T(8,128)(2,1)S(1)}, u32[]{:S(2)}, u32[]{:S(2)}) collective-permute-start(bf16[3,64,1792]{2,1,0:T(8,128)(2,1)S(1)} %get-tuple-element.79), channel_id=1, source_target_pairs={{0,32},{8,40},{16,48},{24,56},{32,64},{40,72},{48,80},{56,88},{64,... | collective-permute-start | bytes 2064392 | tf_op jit(solution)/shard_map/ppermute | solution.py:36
  107.4 27.6 %collective-permute-start.17 = (bf16[3,256,1792]{2,1,0:T(8,128)(2,1)S(1)}, bf16[3,256,1792]{2,1,0:T(8,128)(2,1)S(1)}, u32[]{:S(2)}, u32[]{:S(2)}) collective-permute-start(bf16[3,256,1792]{2,1,0:T(8,128)(2,1)S(1)} %maximum_maximum_fusion.refs_0_), channel_id=1, source_target_pairs={{0,8},{8,0},{16,24},{24,16},{32,40},{40,32},{48,56},{56,48},{64,72... | collective-permute-start | bytes 8257544 | tf_op jit(solution)/shard_map/ppermute | solution.py:36
  115.2 12.2 %copy-start.2 = (bf16[512,3584]{1,0:T(8,128)(2,1)S(1)}, bf16[512,3584]{1,0:T(8,128)(2,1)}, u32[]{:S(2)}) copy-start(bf16[512,3584]{1,0:T(8,128)(2,1)} %refs_4_.7) | copy-start | bytes 11010052
  115.2 7.8 %collective-permute-start.21 = (bf16[3,64,640]{2,1,0:T(8,128)(2,1)S(1)}, bf16[3,64,640]{2,1,0:T(8,128)(2,1)S(1)}, u32[]{:S(2)}, u32[]{:S(2)}) collective-permute-start(bf16[3,64,640]{2,1,0:T(8,128)(2,1)S(1)} %pad_maximum_fusion.9), channel_id=1, source_target_pairs={{0,32},{8,40},{16,48},{24,56},{32,64},{40,72},{48,80},{56,88},{64,... | collective-permute-start | bytes 737288 | tf_op jit(solution)/shard_map/ppermute | solution.py:36
  115.4 7.7 %collective-permute-start.22 = (bf16[3,64,640]{2,1,0:T(8,128)(2,1)S(1)}, bf16[3,64,640]{2,1,0:T(8,128)(2,1)S(1)}, u32[]{:S(2)}, u32[]{:S(2)}) collective-permute-start(bf16[3,64,640]{2,1,0:T(8,128)(2,1)S(1)} %slice.114), channel_id=1, source_target_pairs={{0,96},{8,104},{16,112},{24,120},{32,0},{40,8},{48,16},{56,24},{64... | collective-permute-start | bytes 737288 | tf_op jit(solution)/shard_map/ppermute | solution.py:36
  118.1 9.2 %copy-start = (bf16[512,3584]{1,0:T(8,128)(2,1)S(1)}, bf16[512,3584]{1,0:T(8,128)(2,1)}, u32[]{:S(2)}) copy-start(bf16[512,3584]{1,0:T(8,128)(2,1)} %refs_3_.7) | copy-start | bytes 11010052
  118.1 4.9 %collective-permute-start.19 = (bf16[3,64,512]{2,1,0:T(8,128)(2,1)S(1)}, bf16[3,64,512]{2,1,0:T(8,128)(2,1)S(1)}, u32[]{:S(2)}, u32[]{:S(2)}) collective-permute-start(bf16[3,64,512]{2,1,0:T(8,128)(2,1)S(1)} %slice.111), channel_id=1, source_target_pairs={{0,16},{8,24},{16,0},{24,8},{32,48},{40,56},{48,32},{56,40},{64,80... | collective-permute-start | bytes 589832 | tf_op jit(solution)/shard_map/ppermute | solution.py:36
  123.1 11.9 %collective-permute-start.23 = (bf16[3,192,1792]{2,1,0:T(8,128)(2,1)S(1)}, bf16[3,192,1792]{2,1,0:T(8,128)(2,1)S(1)}, u32[]{:S(2)}, u32[]{:S(2)}) collective-permute-start(bf16[3,192,1792]{2,1,0:T(8,128)(2,1)S(1)} %pad_maximum_fusion.refs_1_), channel_id=1, source_target_pairs={{0,8},{8,0},{16,24},{24,16},{32,40},{40,32},{48,56},{56,48},{64,72... | collective-permute-start | bytes 6193160 | tf_op jit(solution)/shard_map/ppermute | solution.py:36
  127.3 7.7 %collective-permute-start.24 = (bf16[3,64,1792]{2,1,0:T(8,128)(2,1)S(1)}, bf16[3,64,1792]{2,1,0:T(8,128)(2,1)S(1)}, u32[]{:S(2)}, u32[]{:S(2)}) collective-permute-start(bf16[3,64,1792]{2,1,0:T(8,128)(2,1)S(1)} %pad_maximum_fusion.8.refs_2_), channel_id=1, source_target_pairs={{0,8},{8,0},{16,24},{24,16},{32,40},{40,32},{48,56},{56,48},{64,72... | collective-permute-start | bytes 2064392 | tf_op jit(solution)/shard_map/ppermute | solution.py:36
  140.5 20.5 %all-to-all-start.1 = ((f32[8,64,512]{2,1,0:T(8,128)}), f32[8,64,512]{2,1,0:T(8,128)}, u32[]{:S(2)}, u32[]{:S(2)}) async-start(f32[8,64,512]{2,1,0:T(8,128)} %copy-done.9), calls=%async_computation.1 | async-start | bytes 2097152 | tf_op jit(solution)/shard_map/all_to_all | solution.py:391
  (6 other events, 9.4 us)

commit v6 on v4

--- a/solution.py
+++ b/solution.py
@@ -191,7 +191,7 @@
         ggw, guw, gdw = refs[-3:]
         ggw[...] = dot(tok_t[...], grads[0], 1, 0).astype(BF)
         guw[...] = dot(tok_t[...], grads[1], 1, 0).astype(BF)
-        gdw[...] = dot(grads[2], tg[:, 512:], 0, 0).astype(BF)
+        gdw[...] = dot(grads[2], tg[...], 0, 0).astype(BF)
     if has_terms:
         out = refs[-4] if has_weights else refs[-1]
         term = dot(grads[0], gw[...], 1, 1) + dot(grads[1], uw[...], 1, 1)
@@ -231,7 +231,7 @@
         scratch.append(pltpu.VMEM((512, 512), F32))
     if weights:
         tok_t, tg, beside = weights
-        in_specs += [square, whole((512, 1024))]
+        in_specs += [square, pl.BlockSpec((512, 512), lambda i, pos: (0, 1))]
         args += [tok_t, tg]
         if beside is not None:
             for k in range(3):

time: 158 us -> 158 us (level)
  no operation moved by 1% of the time
where the time goes in v6:
time: 158 us
  waiting for transfers between devices  58.4 us (37%)
  starting transfers between devices  47.1 us (30%)
  Pallas kernels  38.4 us (24%)
  local copies, waits for them, and re-layouts  10.6 us (7%)
  other arithmetic  2.14 us (1%)
    ppermute x25, waiting for transfers between devices, send(): return lax.ppermute(a, 'gx', pairs)  51 us
    ppermute x25, starting transfers between devices, send(): return lax.ppermute(a, 'gx', pairs)  34.1 us
    pallas_call x6, Pallas kernels, part(): pl.pallas_call(functools.partial(part_kernel, half, bool(terms), bool(wei...  19.1 us
    pallas_call x2, Pallas kernels, sums(): pl.pallas_call(functools.partial(sums_kernel, part), grid_spec=pltpu.Pref...  14.5 us
    all_to_all x1, starting transfers between devices, shards(): blocks = lax.all_to_all(spread(tokens, out_grad), 'gy', 0, 0, tiled=True)  8.33 us
    all_to_all x1, waiting for transfers between devices, shards(): blocks = lax.all_to_all(spread(tokens, out_grad), 'gy', 0, 0, tiled=True)  7.4 us
    dynamic_slice x3, local copies, waits for them, and re-layouts, shards(): lax.dynamic_slice_in_dim(w, far_half, HALF, axis)  5.69 us
    all_to_all x1, starting transfers between devices, shards(): grad_tokens = total_of(lax.all_to_all(terms, 'gy', 0, 0, tiled=True))  4.73 us
  transfers between devices with their start and end apart: 27, of which 12 were waited for; matrix products, arithmetic and copies ran while one was open for 4% of the time, Pallas kernels for 14%

profile of v6, /device:TPU:1, one launch (start us, length us, event | category | flops | bytes accessed | tf_op | source)
XLA Modules:
  0.0 157.7 jit_solution(13621231248126786456)
XLA Ops:
  0.6 1.9 %shard_map.84 = bf16[8,64,1024]{2,1,0:T(8,128)(2,1)} custom-call(bf16[64,512]{1,0:T(8,128)(2,1)} %tokens.1, bf16[64,512]{1,0:T(8,128)(2,1)} %out_grad.1), custom_call_target="tpu_custom_call" | custom-call | bytes 1048576 | tf_op jit(solution)/shard_map/pallas_call | solution.py:64
  2.6 8.3 %all-to-all-start = ((bf16[8,64,1024]{2,1,0:T(8,128)(2,1)}), bf16[8,64,1024]{2,1,0:T(8,128)(2,1)S(1)}, u32[]{:S(2)}, u32[]{:S(2)}) async-start(bf16[8,64,1024]{2,1,0:T(8,128)(2,1)} %shard_map.84), calls=%async_computation | async-start | bytes 2097152 | tf_op jit(solution)/shard_map/all_to_all | solution.py:370
  10.9 3.0 %constant_dynamic-slice_fusion.2 = bf16[512,1792]{1,0:T(8,128)(2,1)} fusion(bf16[512,3584]{1,0:T(8,128)(2,1)} %refs_3_.7, s32[]{:T(128)S(6)} %select_n.27), kind=kLoop, calls=%fused_computation.31 | loop fusion | bytes 3670020 | tf_op jit(solution)/shard_map/dynamic_slice | solution.py:373
  14.9 1.3 constant_dynamic-slice_fusion.1
  19.0 7.4 %all-to-all-done.blocks = bf16[8,64,1024]{2,1,0:T(8,128)(2,1)S(1)} async-done(((bf16[8,64,1024]{2,1,0:T(8,128)(2,1)}), bf16[8,64,1024]{2,1,0:T(8,128)(2,1)S(1)}, u32[]{:S(2)}, u32[]{:S(2)}) %all-to-all-start) | async-done | bytes 1048608 | tf_op jit(solution)/shard_map/all_to_all | solution.py:370
  27.2 1.4 collective-permute-start
  28.6 2.3 %collective-permute-done.tg_sib = bf16[512,1024]{1,0:T(8,128)(2,1)S(1)} collective-permute-done((bf16[512,1024]{1,0:T(8,128)(2,1)S(1)}, bf16[512,1024]{1,0:T(8,128)(2,1)S(1)}, u32[]{:S(2)}, u32[]{:S(2)}) %collective-permute-start) | collective-permute-done | bytes 1048608 | tf_op jit(solution)/shard_map/ppermute | solution.py:36
  30.9 7.6 %shard_map.87 = (f32[3,64,1792]{2,1,0:T(8,128)S(1)}, f32[3,64,1792]{2,1,0:T(8,128)S(1)}, f32[3,64,1792]{2,1,0:T(8,128)S(1)}, bf16[3,64,512]{2,1,0:T(8,128)(2,1)S...) custom-call(s32[3]{0:T(128)S(1)} %pad_add_fusion.pos, ...), custom_call_target="tpu_custom_call" | custom-call | flops 2818572288 | bytes 20971520 | tf_op jit(solution)/shard_map/pallas_call | solution.py:127
  39.8 1.5 collective-permute-start.6
  42.1 4.7 %collective-permute-done.4.rz = bf16[3,64,512]{2,1,0:T(8,128)(2,1)S(1)} collective-permute-done((bf16[3,64,512]{2,1,0:T(8,128)(2,1)S(1)}, bf16[3,64,512]{2,1,0:T(8,128)(2,1)S(1)}, u32[]{:S(2)}, u32[]{:S(2)}) %collective-permute-start.4) | collective-permute-done | bytes 196640 | tf_op jit(solution)/shard_map/ppermute | solution.py:36
  49.0 1.8 %collective-permute-start.10 = (bf16[3,64,1792]{2,1,0:T(8,128)(2,1)S(1)}, bf16[3,64,1792]{2,1,0:T(8,128)(2,1)S(1)}, u32[]{:S(2)}, u32[]{:S(2)}) collective-permute-start(bf16[3,64,1792]{2,1,0:T(8,128)(2,1)S(1)} %get-tuple-element.49), channel_id=1, source_target_pairs={{0,96},{8,104},{16,112},{24,120},{32,0},{40,8},{48,16},{56,24},{64... | collective-permute-start | bytes 2064392 | tf_op jit(solution)/shard_map/ppermute | solution.py:36
  50.8 6.9 %shard_map.86 = (f32[3,64,1792]{2,1,0:T(8,128)S(1)}, f32[3,64,1792]{2,1,0:T(8,128)S(1)}, f32[3,64,1792]{2,1,0:T(8,128)S(1)}, f32[3,64,1792]{2,1,0:T(8,128)S(1)}) custom-call(s32[3]{0:T(128)S(1)} %pad_add_fusion.pos, bf16[512,1024]{1,0:T(8,128)(2,1)S(1)} %get-tuple-element.37.tg.refs_6_.refs_7_.refs_4_, bf16[512,1024]{1,0:T(8,128)(2,1)S(1)} %collective-permute-done.tg_sib, ...), custom_call_target="tpu_custom_call" | custom-call | flops 2818572288 | bytes 20971520 | tf_op jit(solution)/shard_map/pallas_call | solution.py:127
  57.8 6.1 %collective-permute-done.7 = bf16[3,64,1792]{2,1,0:T(8,128)(2,1)S(1)} collective-permute-done((bf16[3,64,1792]{2,1,0:T(8,128)(2,1)S(1)}, bf16[3,64,1792]{2,1,0:T(8,128)(2,1)S(1)}, u32[]{:S(2)}, u32[]{:S(2)}) %collective-permute-start.7) | collective-permute-done | bytes 688160 | tf_op jit(solution)/shard_map/ppermute | solution.py:36
  65.5 2.1 %collective-permute-start.11 = (bf16[3,64,1792]{2,1,0:T(8,128)(2,1)S(1)}, bf16[3,64,1792]{2,1,0:T(8,128)(2,1)S(1)}, u32[]{:S(2)}, u32[]{:S(2)}) collective-permute-start(bf16[3,64,1792]{2,1,0:T(8,128)(2,1)S(1)} %pad_maximum_fusion.5), channel_id=1, source_target_pairs={{0,96},{8,104},{16,112},{24,120},{32,0},{40,8},{48,16},{56,24},{64... | collective-permute-start | bytes 2064392 | tf_op jit(solution)/shard_map/ppermute | solution.py:36
  68.4 11.7 %collective-permute-done.9 = bf16[3,64,1792]{2,1,0:T(8,128)(2,1)S(1)} collective-permute-done((bf16[3,64,1792]{2,1,0:T(8,128)(2,1)S(1)}, bf16[3,64,1792]{2,1,0:T(8,128)(2,1)S(1)}, u32[]{:S(2)}, u32[]{:S(2)}) %collective-permute-start.9) | collective-permute-done | bytes 688160 | tf_op jit(solution)/shard_map/ppermute | solution.py:36
  81.8 1.4 collective-permute-start.14
  84.2 10.4 %collective-permute-done.14 = bf16[3,64,1792]{2,1,0:T(8,128)(2,1)S(1)} collective-permute-done((bf16[3,64,1792]{2,1,0:T(8,128)(2,1)S(1)}, bf16[3,64,1792]{2,1,0:T(8,128)(2,1)S(1)}, u32[]{:S(2)}, u32[]{:S(2)}) %collective-permute-start.14) | collective-permute-done | bytes 688160 | tf_op jit(solution)/shard_map/ppermute | solution.py:36
  95.3 1.8 %collective-permute-done.16 = bf16[3,64,1792]{2,1,0:T(8,128)(2,1)S(1)} collective-permute-done((bf16[3,64,1792]{2,1,0:T(8,128)(2,1)S(1)}, bf16[3,64,1792]{2,1,0:T(8,128)(2,1)S(1)}, u32[]{:S(2)}, u32[]{:S(2)}) %collective-permute-start.16) | collective-permute-done | bytes 688160 | tf_op jit(solution)/shard_map/ppermute | solution.py:36
  99.5 7.9 %collective-permute-done.15 = bf16[3,64,1792]{2,1,0:T(8,128)(2,1)S(1)} collective-permute-done((bf16[3,64,1792]{2,1,0:T(8,128)(2,1)S(1)}, bf16[3,64,1792]{2,1,0:T(8,128)(2,1)S(1)}, u32[]{:S(2)}, u32[]{:S(2)}) %collective-permute-start.15) | collective-permute-done | bytes 688160 | tf_op jit(solution)/shard_map/ppermute | solution.py:36
  107.4 7.7 %collective-permute-start.17 = (bf16[3,256,1792]{2,1,0:T(8,128)(2,1)S(1)}, bf16[3,256,1792]{2,1,0:T(8,128)(2,1)S(1)}, u32[]{:S(2)}, u32[]{:S(2)}) collective-permute-start(bf16[3,256,1792]{2,1,0:T(8,128)(2,1)S(1)} %maximum_maximum_fusion.refs_0_), channel_id=1, source_target_pairs={{0,8},{8,0},{16,24},{24,16},{32,40},{40,32},{48,56},{56,48},{64,72... | collective-permute-start | bytes 8257544 | tf_op jit(solution)/shard_map/ppermute | solution.py:36
  115.4 2.7 %collective-permute-start.22 = (bf16[3,64,640]{2,1,0:T(8,128)(2,1)S(1)}, bf16[3,64,640]{2,1,0:T(8,128)(2,1)S(1)}, u32[]{:S(2)}, u32[]{:S(2)}) collective-permute-start(bf16[3,64,640]{2,1,0:T(8,128)(2,1)S(1)} %slice.114), channel_id=1, source_target_pairs={{0,96},{8,104},{16,112},{24,120},{32,0},{40,8},{48,16},{56,24},{64... | collective-permute-start | bytes 737288 | tf_op jit(solution)/shard_map/ppermute | solution.py:36
  118.8 4.2 %collective-permute-done.19 = bf16[3,64,512]{2,1,0:T(8,128)(2,1)S(1)} collective-permute-done((bf16[3,64,512]{2,1,0:T(8,128)(2,1)S(1)}, bf16[3,64,512]{2,1,0:T(8,128)(2,1)S(1)}, u32[]{:S(2)}, u32[]{:S(2)}) %collective-permute-start.19) | collective-permute-done | bytes 196640 | tf_op jit(solution)/shard_map/ppermute | solution.py:36
  123.1 4.2 %collective-permute-start.23 = (bf16[3,192,1792]{2,1,0:T(8,128)(2,1)S(1)}, bf16[3,192,1792]{2,1,0:T(8,128)(2,1)S(1)}, u32[]{:S(2)}, u32[]{:S(2)}) collective-permute-start(bf16[3,192,1792]{2,1,0:T(8,128)(2,1)S(1)} %pad_maximum_fusion.refs_1_), channel_id=1, source_target_pairs={{0,8},{8,0},{16,24},{24,16},{32,40},{40,32},{48,56},{56,48},{64,72... | collective-permute-start | bytes 6193160 | tf_op jit(solution)/shard_map/ppermute | solution.py:36
  127.3 3.8 %shard_map.89 = (f32[512,512]{1,0:T(8,128)S(1)}, bf16[512,3584]{1,0:T(8,128)(2,1)}, bf16[512,3584]{1,0:T(8,128)(2,1)}, bf16[3584,512]{1,0:T(8,128)(2,1)}) custom-call(s32[3]{0:T(128)S(1)} %pad_add_fusion.pos, bf16[3,256,1792]{2,1,0:T(8,128)(2,1)S(1)} %maximum_maximum_fusion.refs_0_, bf16[3,192,1792]{2,1,0:T(8,128)(2,1)S(1)} %pad_maximum_fusion.refs_1_, ...), custom_call_target="tpu_custom_call" | custom-call | flops 2348810240 | bytes 8388608 | tf_op jit(solution)/shard_map/pallas_call | solution.py:246
  131.2 3.8 %shard_map.90 = (f32[512,512]{1,0:T(8,128)S(1)}, bf16[512,3584]{1,0:T(8,128)(2,1)}, bf16[512,3584]{1,0:T(8,128)(2,1)}, bf16[3584,512]{1,0:T(8,128)(2,1)}) custom-call(s32[3]{0:T(128)S(1)} %pad_add_fusion.pos, bf16[3,256,1792]{2,1,0:T(8,128)(2,1)S(1)} %maximum_maximum_fusion.refs_0_, ...), custom_call_target="tpu_custom_call", output_to_operand_aliasing={{1}: (9, {}), {2}: (10, {}), {3}: (11, {})} | custom-call | flops 2348810240 | bytes 8388608 | tf_op jit(solution)/shard_map/pallas_call | solution.py:246
  135.1 2.2 %shard_map.91.refs_5_ = f32[512,512]{1,0:T(8,128)S(1)} custom-call(s32[3]{0:T(128)S(1)} %pad_add_fusion.pos, bf16[3,256,1792]{2,1,0:T(8,128)(2,1)S(1)} %collective-permute-done.17.refs_0_, bf16[3,192,1792]{2,1,0:T(8,128)(2,1)S(1)} %collective-permute-done.23.refs_1_, bf16[3,64,1792]{2,1,0:T(8,128)(2,1)S(1)} %collective-permute-done.24.refs_2_, ...), custom_call_target="tpu_custom_call" | custom-call | flops 939524096 | bytes 8388608 | tf_op jit(solution)/shard_map/pallas_call | solution.py:246
  137.3 2.3 %shard_map.92 = bf16[8,64,512]{2,1,0:T(8,128)(2,1)S(1)} custom-call(s32[3]{0:T(128)S(1)} %pad_add_fusion.pos, bf16[3,256,1792]{2,1,0:T(8,128)(2,1)S(1)} %collective-permute-done.17.refs_0_, bf16[3,192,1792]{2,1,0:T(8,128)(2,1)S(1)} %collective-permute-done.23.refs_1_, bf16[3,64,1792]{2,1,0:T(8,128)(2,1)S(1)} %collective-permute-done.24.refs_2_, ...), custom_call_target="tpu_custom_call" | custom-call | flops 939524096 | bytes 8388608 | tf_op jit(solution)/shard_map/pallas_call | solution.py:246
  140.4 4.7 %all-to-all-start.1 = ((bf16[8,64,512]{2,1,0:T(8,128)(2,1)}), bf16[8,64,512]{2,1,0:T(8,128)(2,1)}, u32[]{:S(2)}, u32[]{:S(2)}) async-start(bf16[8,64,512]{2,1,0:T(8,128)(2,1)} %copy-done.9), calls=%async_computation.1 | async-start | bytes 1048576 | tf_op jit(solution)/shard_map/all_to_all | solution.py:391
  146.3 1.6 %copy-done.6 = bf16[3,192,1792]{2,1,0:T(8,128)(2,1)S(1)} copy-done((bf16[3,192,1792]{2,1,0:T(8,128)(2,1)S(1)}, bf16[3,192,1792]{2,1,0:T(8,128)(2,1)}, u32[]{:S(2)}) %copy-start.6) | copy-done | bytes 2064408
  148.9 3.5 %shard_map.94 = (bf16[512,3584]{1,0:T(8,128)(2,1)}, bf16[512,3584]{1,0:T(8,128)(2,1)}, bf16[3584,512]{1,0:T(8,128)(2,1)}) custom-call(s32[3]{0:T(128)S(1)} %pad_add_fusion.pos, bf16[3,256,1792]{2,1,0:T(8,128)(2,1)S(1)} %collective-permute-done.17.refs_0_, ...), custom_call_target="tpu_custom_call", output_to_operand_aliasing={{0}: (6, {}), {1}: (7, {}), {2}: (8, {})} | custom-call | flops 1409286144 | bytes 8388608 | tf_op jit(solution)/shard_map/pallas_call | solution.py:246
  152.4 3.5 %shard_map.95 = (bf16[512,3584]{1,0:T(8,128)(2,1)}, bf16[512,3584]{1,0:T(8,128)(2,1)}, bf16[3584,512]{1,0:T(8,128)(2,1)}) custom-call(s32[3]{0:T(128)S(1)} %pad_add_fusion.pos, bf16[3,256,1792]{2,1,0:T(8,128)(2,1)S(1)} %collective-permute-done.17.refs_0_, ...), custom_call_target="tpu_custom_call", output_to_operand_aliasing={{0}: (6, {}), {1}: (7, {}), {2}: (8, {})} | custom-call | flops 1409286144 | bytes 8388608 | tf_op jit(solution)/shard_map/pallas_call | solution.py:246
  156.0 1.7 %shard_map.93 = bf16[64,512]{1,0:T(8,128)(2,1)} custom-call(bf16[8,64,512]{2,1,0:T(8,128)(2,1)} %all-to-all-done.1.terms), custom_call_target="tpu_custom_call" | custom-call | flops 262144 | bytes 524288 | tf_op jit(solution)/shard_map/pallas_call | solution.py:270
  (84 shorter events, 21.1 us)
Async XLA Ops:
  2.6 23.8 %all-to-all-start = ((bf16[8,64,1024]{2,1,0:T(8,128)(2,1)}), bf16[8,64,1024]{2,1,0:T(8,128)(2,1)S(1)}, u32[]{:S(2)}, u32[]{:S(2)}) async-start(bf16[8,64,1024]{2,1,0:T(8,128)(2,1)} %shard_map.84), calls=%async_computation | async-start | bytes 2097152 | tf_op jit(solution)/shard_map/all_to_all | solution.py:370
  10.9 4.0 %copy-start.1 = (bf16[512,3584]{1,0:T(8,128)(2,1)S(1)}, bf16[512,3584]{1,0:T(8,128)(2,1)}, u32[]{:S(2)}) copy-start(bf16[512,3584]{1,0:T(8,128)(2,1)} %refs_4_.7) | copy-start | bytes 11010052
  13.9 14.7 %collective-permute-start.1 = (bf16[512,1792]{1,0:T(8,128)(2,1)}, bf16[512,1792]{1,0:T(8,128)(2,1)S(1)}, u32[]{:S(2)}, u32[]{:S(2)}) collective-permute-start(bf16[512,1792]{1,0:T(8,128)(2,1)} %constant_dynamic-slice_fusion.2), channel_id=1, source_target_pairs={{0,8},{8,0},{16,24},{24,16},{32,40},{40,32},{48,56},{56,48},{64,72... | collective-permute-start | bytes 5505032 | tf_op jit(solution)/shard_map/ppermute | solution.py:36
  16.2 12.4 %collective-permute-start.2 = (bf16[512,1792]{1,0:T(8,128)(2,1)}, bf16[512,1792]{1,0:T(8,128)(2,1)}, u32[]{:S(2)}, u32[]{:S(2)}) collective-permute-start(bf16[512,1792]{1,0:T(8,128)(2,1)} %constant_dynamic-slice_fusion.1), channel_id=1, source_target_pairs={{0,8},{8,0},{16,24},{24,16},{32,40},{40,32},{48,56},{56,48},{64,72... | collective-permute-start | bytes 5505032 | tf_op jit(solution)/shard_map/ppermute | solution.py:36
  17.6 11.1 %collective-permute-start.3 = (bf16[1792,512]{1,0:T(8,128)(2,1)}, bf16[1792,512]{1,0:T(8,128)(2,1)}, u32[]{:S(2)}, u32[]{:S(2)}) collective-permute-start(bf16[1792,512]{1,0:T(8,128)(2,1)} %constant_dynamic-slice_fusion), channel_id=1, source_target_pairs={{0,8},{8,0},{16,24},{24,16},{32,40},{40,32},{48,56},{56,48},{64,72... | collective-permute-start | bytes 5505032 | tf_op jit(solution)/shard_map/ppermute | solution.py:36
  27.2 104.0 %copy-start.3 = (bf16[512,1024]{1,0:T(8,128)(2,1)}, bf16[512,1024]{1,0:T(8,128)(2,1)S(1)}, u32[]{:S(2)}) copy-start(bf16[512,1024]{1,0:T(8,128)(2,1)S(1)} %get-tuple-element.37.tg.refs_6_.refs_7_.refs_4_) | copy-start | bytes 3145732
  27.2 104.0 %copy-start.7 = (bf16[512,512]{1,0:T(8,128)(2,1)}, bf16[512,512]{1,0:T(8,128)(2,1)S(1)}, u32[]{:S(2)}) copy-start(bf16[512,512]{1,0:T(8,128)(2,1)S(1)} %get-tuple-element.55.refs_5_.refs_6_.refs_3_) | copy-start | bytes 1572868
  27.2 3.7 %collective-permute-start = (bf16[512,1024]{1,0:T(8,128)(2,1)S(1)}, bf16[512,1024]{1,0:T(8,128)(2,1)S(1)}, u32[]{:S(2)}, u32[]{:S(2)}) collective-permute-start(bf16[512,1024]{1,0:T(8,128)(2,1)S(1)} %get-tuple-element.37.tg.refs_6_.refs_7_.refs_4_), channel_id=1, source_target_pairs={{0,8},{8,0},{16,24},{24,16},{32,40},{40,32},{48,56},{56,48},{64,72... | collective-permute-start | bytes 3145736 | tf_op jit(solution)/shard_map/ppermute | solution.py:36
  38.6 8.4 %collective-permute-start.5 = (bf16[3,64,640]{2,1,0:T(8,128)(2,1)S(1)}, bf16[3,64,640]{2,1,0:T(8,128)(2,1)S(1)}, u32[]{:S(2)}, u32[]{:S(2)}) collective-permute-start(bf16[3,64,640]{2,1,0:T(8,128)(2,1)S(1)} %get-tuple-element.44), channel_id=1, source_target_pairs={{0,32},{8,40},{16,48},{24,56},{32,64},{40,72},{48,80},{56,88},{64,... | collective-permute-start | bytes 737288 | tf_op jit(solution)/shard_map/ppermute | solution.py:36
  39.8 7.2 %collective-permute-start.6 = (bf16[3,64,640]{2,1,0:T(8,128)(2,1)S(1)}, bf16[3,64,640]{2,1,0:T(8,128)(2,1)S(1)}, u32[]{:S(2)}, u32[]{:S(2)}) collective-permute-start(bf16[3,64,640]{2,1,0:T(8,128)(2,1)S(1)} %get-tuple-element.45), channel_id=1, source_target_pairs={{0,96},{8,104},{16,112},{24,120},{32,0},{40,8},{48,16},{56,24},{64... | collective-permute-start | bytes 737288 | tf_op jit(solution)/shard_map/ppermute | solution.py:36
  41.3 5.5 %collective-permute-start.4 = (bf16[3,64,512]{2,1,0:T(8,128)(2,1)S(1)}, bf16[3,64,512]{2,1,0:T(8,128)(2,1)S(1)}, u32[]{:S(2)}, u32[]{:S(2)}) collective-permute-start(bf16[3,64,512]{2,1,0:T(8,128)(2,1)S(1)} %get-tuple-element.43), channel_id=1, source_target_pairs={{0,16},{8,24},{16,0},{24,8},{32,48},{40,56},{48,32},{56,40},{64,80... | collective-permute-start | bytes 589832 | tf_op jit(solution)/shard_map/ppermute | solution.py:36
  47.3 16.6 %collective-permute-start.7 = (bf16[3,64,1792]{2,1,0:T(8,128)(2,1)S(1)}, bf16[3,64,1792]{2,1,0:T(8,128)(2,1)S(1)}, u32[]{:S(2)}, u32[]{:S(2)}) collective-permute-start(bf16[3,64,1792]{2,1,0:T(8,128)(2,1)S(1)} %get-tuple-element.46), channel_id=1, source_target_pairs={{0,32},{8,40},{16,48},{24,56},{32,64},{40,72},{48,80},{56,88},{64,... | collective-permute-start | bytes 2064392 | tf_op jit(solution)/shard_map/ppermute | solution.py:36
  48.2 15.7 %collective-permute-start.8 = (bf16[3,64,1792]{2,1,0:T(8,128)(2,1)S(1)}, bf16[3,64,1792]{2,1,0:T(8,128)(2,1)S(1)}, u32[]{:S(2)}, u32[]{:S(2)}) collective-permute-start(bf16[3,64,1792]{2,1,0:T(8,128)(2,1)S(1)} %get-tuple-element.47), channel_id=1, source_target_pairs={{0,16},{8,24},{16,0},{24,8},{32,48},{40,56},{48,32},{56,40},{64,80... | collective-permute-start | bytes 2064392 | tf_op jit(solution)/shard_map/ppermute | solution.py:36
  49.0 15.1 %collective-permute-start.10 = (bf16[3,64,1792]{2,1,0:T(8,128)(2,1)S(1)}, bf16[3,64,1792]{2,1,0:T(8,128)(2,1)S(1)}, u32[]{:S(2)}, u32[]{:S(2)}) collective-permute-start(bf16[3,64,1792]{2,1,0:T(8,128)(2,1)S(1)} %get-tuple-element.49), channel_id=1, source_target_pairs={{0,96},{8,104},{16,112},{24,120},{32,0},{40,8},{48,16},{56,24},{64... | collective-permute-start | bytes 2064392 | tf_op jit(solution)/shard_map/ppermute | solution.py:36
  64.7 15.4 %collective-permute-start.9 = (bf16[3,64,1792]{2,1,0:T(8,128)(2,1)S(1)}, bf16[3,64,1792]{2,1,0:T(8,128)(2,1)S(1)}, u32[]{:S(2)}, u32[]{:S(2)}) collective-permute-start(bf16[3,64,1792]{2,1,0:T(8,128)(2,1)S(1)} %pad_maximum_fusion.4), channel_id=1, source_target_pairs={{0,32},{8,40},{16,48},{24,56},{32,64},{40,72},{48,80},{56,88},{64,... | collective-permute-start | bytes 2064392 | tf_op jit(solution)/shard_map/ppermute | solution.py:36
  65.5 14.6 %collective-permute-start.11 = (bf16[3,64,1792]{2,1,0:T(8,128)(2,1)S(1)}, bf16[3,64,1792]{2,1,0:T(8,128)(2,1)S(1)}, u32[]{:S(2)}, u32[]{:S(2)}) collective-permute-start(bf16[3,64,1792]{2,1,0:T(8,128)(2,1)S(1)} %pad_maximum_fusion.5), channel_id=1, source_target_pairs={{0,96},{8,104},{16,112},{24,120},{32,0},{40,8},{48,16},{56,24},{64... | collective-permute-start | bytes 2064392 | tf_op jit(solution)/shard_map/ppermute | solution.py:36
  67.6 13.6 %collective-permute-start.12 = (bf16[3,64,1792]{2,1,0:T(8,128)(2,1)S(1)}, bf16[3,64,1792]{2,1,0:T(8,128)(2,1)S(1)}, u32[]{:S(2)}, u32[]{:S(2)}) collective-permute-start(bf16[3,64,1792]{2,1,0:T(8,128)(2,1)S(1)} %pad_maximum_fusion.6), channel_id=1, source_target_pairs={{0,16},{8,24},{16,0},{24,8},{32,48},{40,56},{48,32},{56,40},{64,80... | collective-permute-start | bytes 2064392 | tf_op jit(solution)/shard_map/ppermute | solution.py:36
  81.8 12.7 %collective-permute-start.14 = (bf16[3,64,1792]{2,1,0:T(8,128)(2,1)S(1)}, bf16[3,64,1792]{2,1,0:T(8,128)(2,1)S(1)}, u32[]{:S(2)}, u32[]{:S(2)}) collective-permute-start(bf16[3,64,1792]{2,1,0:T(8,128)(2,1)S(1)} %pad_maximum_fusion.7), channel_id=1, source_target_pairs={{0,96},{8,104},{16,112},{24,120},{32,0},{40,8},{48,16},{56,24},{64... | collective-permute-start | bytes 2064392 | tf_op jit(solution)/shard_map/ppermute | solution.py:36
  83.3 11.9 %collective-permute-start.13 = (bf16[3,64,1792]{2,1,0:T(8,128)(2,1)S(1)}, bf16[3,64,1792]{2,1,0:T(8,128)(2,1)S(1)}, u32[]{:S(2)}, u32[]{:S(2)}) collective-permute-start(bf16[3,64,1792]{2,1,0:T(8,128)(2,1)S(1)} %pad_maximum_fusion.7), channel_id=1, source_target_pairs={{0,16},{8,24},{16,0},{24,8},{32,48},{40,56},{48,32},{56,40},{64,80... | collective-permute-start | bytes 2064392 | tf_op jit(solution)/shard_map/ppermute | solution.py:36
  84.1 13.0 %collective-permute-start.16 = (bf16[3,64,1792]{2,1,0:T(8,128)(2,1)S(1)}, bf16[3,64,1792]{2,1,0:T(8,128)(2,1)S(1)}, u32[]{:S(2)}, u32[]{:S(2)}) collective-permute-start(bf16[3,64,1792]{2,1,0:T(8,128)(2,1)S(1)} %pad_maximum_fusion.7), channel_id=1, source_target_pairs={{0,32},{8,40},{16,48},{24,56},{32,64},{40,72},{48,80},{56,88},{64,... | collective-permute-start | bytes 2064392 | tf_op jit(solution)/shard_map/ppermute | solution.py:36
  97.2 10.2 %collective-permute-start.15 = (bf16[3,64,1792]{2,1,0:T(8,128)(2,1)S(1)}, bf16[3,64,1792]{2,1,0:T(8,128)(2,1)S(1)}, u32[]{:S(2)}, u32[]{:S(2)}) collective-permute-start(bf16[3,64,1792]{2,1,0:T(8,128)(2,1)S(1)} %get-tuple-element.81), channel_id=1, source_target_pairs={{0,96},{8,104},{16,112},{24,120},{32,0},{40,8},{48,16},{56,24},{64... | collective-permute-start | bytes 2064392 | tf_op jit(solution)/shard_map/ppermute | solution.py:36
  97.3 17.8 %collective-permute-start.20 = (bf16[3,64,1792]{2,1,0:T(8,128)(2,1)S(1)}, bf16[3,64,1792]{2,1,0:T(8,128)(2,1)S(1)}, u32[]{:S(2)}, u32[]{:S(2)}) collective-permute-start(bf16[3,64,1792]{2,1,0:T(8,128)(2,1)S(1)} %get-tuple-element.80), channel_id=1, source_target_pairs={{0,16},{8,24},{16,0},{24,8},{32,48},{40,56},{48,32},{56,40},{64,80... | collective-permute-start | bytes 2064392 | tf_op jit(solution)/shard_map/ppermute | solution.py:36
  98.0 17.2 %collective-permute-start.18 = (bf16[3,64,1792]{2,1,0:T(8,128)(2,1)S(1)}, bf16[3,64,1792]{2,1,0:T(8,128)(2,1)S(1)}, u32[]{:S(2)}, u32[]{:S(2)}) collective-permute-start(bf16[3,64,1792]{2,1,0:T(8,128)(2,1)S(1)} %get-tuple-element.79), channel_id=1, source_target_pairs={{0,32},{8,40},{16,48},{24,56},{32,64},{40,72},{48,80},{56,88},{64,... | collective-permute-start | bytes 2064392 | tf_op jit(solution)/shard_map/ppermute | solution.py:36
  107.4 27.7 %collective-permute-start.17 = (bf16[3,256,1792]{2,1,0:T(8,128)(2,1)S(1)}, bf16[3,256,1792]{2,1,0:T(8,128)(2,1)S(1)}, u32[]{:S(2)}, u32[]{:S(2)}) collective-permute-start(bf16[3,256,1792]{2,1,0:T(8,128)(2,1)S(1)} %maximum_maximum_fusion.refs_0_), channel_id=1, source_target_pairs={{0,8},{8,0},{16,24},{24,16},{32,40},{40,32},{48,56},{56,48},{64,72... | collective-permute-start | bytes 8257544 | tf_op jit(solution)/shard_map/ppermute | solution.py:36
  115.2 12.2 %copy-start.2 = (bf16[512,3584]{1,0:T(8,128)(2,1)S(1)}, bf16[512,3584]{1,0:T(8,128)(2,1)}, u32[]{:S(2)}) copy-start(bf16[512,3584]{1,0:T(8,128)(2,1)} %refs_4_.7) | copy-start | bytes 11010052
  115.2 7.8 %collective-permute-start.21 = (bf16[3,64,640]{2,1,0:T(8,128)(2,1)S(1)}, bf16[3,64,640]{2,1,0:T(8,128)(2,1)S(1)}, u32[]{:S(2)}, u32[]{:S(2)}) collective-permute-start(bf16[3,64,640]{2,1,0:T(8,128)(2,1)S(1)} %pad_maximum_fusion.9), channel_id=1, source_target_pairs={{0,32},{8,40},{16,48},{24,56},{32,64},{40,72},{48,80},{56,88},{64,... | collective-permute-start | bytes 737288 | tf_op jit(solution)/shard_map/ppermute | solution.py:36
  115.4 7.7 %collective-permute-start.22 = (bf16[3,64,640]{2,1,0:T(8,128)(2,1)S(1)}, bf16[3,64,640]{2,1,0:T(8,128)(2,1)S(1)}, u32[]{:S(2)}, u32[]{:S(2)}) collective-permute-start(bf16[3,64,640]{2,1,0:T(8,128)(2,1)S(1)} %slice.114), channel_id=1, source_target_pairs={{0,96},{8,104},{16,112},{24,120},{32,0},{40,8},{48,16},{56,24},{64... | collective-permute-start | bytes 737288 | tf_op jit(solution)/shard_map/ppermute | solution.py:36
  118.1 9.2 %copy-start = (bf16[512,3584]{1,0:T(8,128)(2,1)S(1)}, bf16[512,3584]{1,0:T(8,128)(2,1)}, u32[]{:S(2)}) copy-start(bf16[512,3584]{1,0:T(8,128)(2,1)} %refs_3_.7) | copy-start | bytes 11010052
  118.1 4.9 %collective-permute-start.19 = (bf16[3,64,512]{2,1,0:T(8,128)(2,1)S(1)}, bf16[3,64,512]{2,1,0:T(8,128)(2,1)S(1)}, u32[]{:S(2)}, u32[]{:S(2)}) collective-permute-start(bf16[3,64,512]{2,1,0:T(8,128)(2,1)S(1)} %slice.111), channel_id=1, source_target_pairs={{0,16},{8,24},{16,0},{24,8},{32,48},{40,56},{48,32},{56,40},{64,80... | collective-permute-start | bytes 589832 | tf_op jit(solution)/shard_map/ppermute | solution.py:36
  123.1 12.0 %collective-permute-start.23 = (bf16[3,192,1792]{2,1,0:T(8,128)(2,1)S(1)}, bf16[3,192,1792]{2,1,0:T(8,128)(2,1)S(1)}, u32[]{:S(2)}, u32[]{:S(2)}) collective-permute-start(bf16[3,192,1792]{2,1,0:T(8,128)(2,1)S(1)} %pad_maximum_fusion.refs_1_), channel_id=1, source_target_pairs={{0,8},{8,0},{16,24},{24,16},{32,40},{40,32},{48,56},{56,48},{64,72... | collective-permute-start | bytes 6193160 | tf_op jit(solution)/shard_map/ppermute | solution.py:36
  127.3 7.8 %collective-permute-start.24 = (bf16[3,64,1792]{2,1,0:T(8,128)(2,1)S(1)}, bf16[3,64,1792]{2,1,0:T(8,128)(2,1)S(1)}, u32[]{:S(2)}, u32[]{:S(2)}) collective-permute-start(bf16[3,64,1792]{2,1,0:T(8,128)(2,1)S(1)} %pad_maximum_fusion.8.refs_2_), channel_id=1, source_target_pairs={{0,8},{8,0},{16,24},{24,16},{32,40},{40,32},{48,56},{56,48},{64,72... | collective-permute-start | bytes 2064392 | tf_op jit(solution)/shard_map/ppermute | solution.py:36
  140.4 15.6 %all-to-all-start.1 = ((bf16[8,64,512]{2,1,0:T(8,128)(2,1)}), bf16[8,64,512]{2,1,0:T(8,128)(2,1)}, u32[]{:S(2)}, u32[]{:S(2)}) async-start(bf16[8,64,512]{2,1,0:T(8,128)(2,1)} %copy-done.9), calls=%async_computation.1 | async-start | bytes 1048576 | tf_op jit(solution)/shard_map/all_to_all | solution.py:391
  (6 other events, 9.2 us)
